TPU v7x, 256 devices: a whole 4x4x8 slice. The times are simulated.
256 devices in a mesh: tp: 8 (over x, core), cp: 32 (over z, y).
Axes of the slice: x: 4, y: 4, z: 8, core: 2. Of those that a mesh axis runs over, the one named last changes fastest.
Arguments:
- query: bfloat16 [4096, 128, 576], P('cp', 'tp'), may hold values from -36 to 36
- latent: bfloat16 [4096, 576], P('cp'), may hold values from -6 to 6
- grad_out: bfloat16 [4096, 128, 512], P('cp', 'tp'), may hold values from -24 to 24
- ancestors: int32 [32, 3], P('cp'), may hold values from -1 to 30, as said below
- parents: int32 [4096], P('cp'), may hold values from -1 to 126, as said below
Outputs:
- d_query: bfloat16 [4096, 128, 576], P('cp', 'tp')
- d_latent: bfloat16 [4096, 576], P('cp')
Inputs may be any that keep to these rules, and one draw needn't show every extreme that they name: `ancestors`: an entry that is not -1 names a block b - t with 1 <= t <= 3; the entries of one block differ from each other. Every block from 3 on whose id is a multiple of 3 lists 3 blocks. The last block lists the block before it. `parents`: the first row of each block is its root (-1); every other row names an earlier row of its own block; the last row of each block names the row before it.
All inputs are finite; a program needn't handle non-finite values.
Results may differ from a plain program's by a relative error of at most 0.01.
Values may be sent and summed in bfloat16 or wider, within the bound.
No kernel may reach another device: no remote copies, remote signals or barrier semaphores. Data moves between devices by JAX's collectives and lax.ppermute only.
A program may use at most 64 MiB of HBM per device.

v0:
```python
import jax
import jax.numpy as jnp
from jax import lax
from jax.sharding import PartitionSpec as P

LAT = 512
ROPE = 64
BS = 128
REACH = 3


score_scale = 192.0 ** (-0.5)
rope_base = 10000.0


def shifted(block, axis, distance):
    devices = range(lax.axis_size(axis))
    route = [(i - distance, i) for i in devices if i - distance in devices]
    return lax.ppermute(block, axis, route)


def tree_positions(ancestors, parents):
    blocks = ancestors.shape[0]
    parent_rows = parents.reshape(blocks, BS)
    row_index = jnp.arange(BS, dtype=jnp.int32)
    linked = (row_index[None, None, :] == parent_rows[:, :, None]) | (
        row_index[None, None, :] == row_index[None, :, None]
    )
    closure = linked.astype(jnp.float32)
    for sweep in range(max(1, (BS - 1).bit_length())):
        closure = jnp.minimum(
            jnp.einsum("bij,bjk->bik", closure, closure, precision=lax.Precision.HIGHEST), 1.0
        )
    tree_depth = jnp.sum(closure, axis=2) - 1.0
    list_count = jnp.sum((ancestors >= 0).astype(jnp.float32), axis=1)
    positions = BS * list_count[:, None] + tree_depth
    return (closure, positions.reshape(-1))


def rope_tables(positions):
    half_width = ROPE // 2
    frequency = rope_base ** (-2.0 * jnp.arange(half_width, dtype=jnp.float32) / ROPE)
    angles = positions[:, None] * frequency[None, :]
    return (jnp.cos(angles), jnp.sin(angles))


def rotate(values, cosine_table, sine_table):
    half_width = values.shape[-1] // 2
    first_half = values[..., :half_width]
    second_half = values[..., half_width:]
    return jnp.concatenate(
        [
            first_half * cosine_table - second_half * sine_table,
            first_half * sine_table + second_half * cosine_table,
        ],
        axis=-1,
    )


def unrotate(values, cosine_table, sine_table):
    half_width = values.shape[-1] // 2
    first_half = values[..., :half_width]
    second_half = values[..., half_width:]
    return jnp.concatenate(
        [
            first_half * cosine_table + second_half * sine_table,
            second_half * cosine_table - first_half * sine_table,
        ],
        axis=-1,
    )


def with_rope(values, cosine_table, sine_table):
    plain = values[..., :LAT].astype(jnp.float32)
    turned = rotate(values[..., LAT:].astype(jnp.float32), cosine_table, sine_table)
    return jnp.concatenate([plain, turned], axis=-1)


def return_pieces(pieces):
    summed = pieces[0]
    for offset in range(1, pieces.shape[0]):
        summed = summed + shifted(pieces[offset].astype(jnp.bfloat16), "cp", -offset).astype(
            jnp.float32
        )
    return summed


def on_device(query, latent, grad_out, ancestors, parents):
    rows_dev = query.shape[0]
    width = query.shape[2]
    blk_dev = ancestors.shape[0]
    slots = REACH + 1
    here = lax.axis_index("cp")
    closure, positions = tree_positions(ancestors, parents)
    cosine_table, sine_table = rope_tables(positions)
    query_rot = with_rope(query, cosine_table[:, None, :], sine_table[:, None, :]).astype(
        jnp.bfloat16
    )
    keys_rot = with_rope(latent, cosine_table, sine_table).astype(jnp.bfloat16)
    fetched = [keys_rot]
    for offset in range(1, slots):
        fetched.append(shifted(keys_rot, "cp", offset))
    window = jnp.stack(fetched)
    window_keys = window.reshape(slots * rows_dev, width)
    value_keys = window_keys[:, :LAT]
    slot_index = jnp.arange(slots, dtype=jnp.int32)
    local_index = jnp.arange(blk_dev, dtype=jnp.int32)
    window_ids = ((here - slot_index)[:, None] * blk_dev + local_index[None, :]).reshape(-1)
    block = here * blk_dev + 0
    listed = jnp.any(
        (window_ids[:, None] == ancestors[0][None, :]) & (window_ids[:, None] >= 0), axis=1
    )
    is_self = window_ids == block
    allowed = jnp.where(is_self[:, None, None], closure[0][None] > 0.5, listed[:, None, None])
    allowed = allowed.transpose(1, 0, 2).reshape(BS, slots * rows_dev)
    scores = (
        jnp.einsum("qhd,kd->hqk", query_rot, window_keys, preferred_element_type=jnp.float32)
        * score_scale
    )
    scores = jnp.where(allowed[None], scores, -jnp.inf)
    largest = jnp.max(scores, axis=2, keepdims=True)
    expo = jnp.exp(scores - largest)
    weights = expo / jnp.sum(expo, axis=2, keepdims=True)
    weights_b = weights.astype(jnp.bfloat16)
    output = jnp.einsum("hqk,kd->qhd", weights_b, value_keys, preferred_element_type=jnp.float32)
    row_delta = jnp.sum(grad_out.astype(jnp.float32) * output, axis=2)
    slope = jnp.einsum("qhd,kd->hqk", grad_out, value_keys, preferred_element_type=jnp.float32)
    dscore = (score_scale * weights * (slope - row_delta.T[:, :, None])).astype(jnp.bfloat16)
    grad_rows = jnp.einsum("hqk,kd->qhd", dscore, window_keys, preferred_element_type=jnp.float32)
    grad_keys = jnp.einsum("hqk,qhd->kd", dscore, query_rot, preferred_element_type=jnp.float32)
    grad_keys = grad_keys.at[:, :LAT].add(
        jnp.einsum("hqk,qhd->kd", weights_b, grad_out, preferred_element_type=jnp.float32)
    )
    d_query = jnp.concatenate(
        [
            grad_rows[..., :LAT],
            unrotate(grad_rows[..., LAT:], cosine_table[:, None, :], sine_table[:, None, :]),
        ],
        axis=-1,
    ).astype(jnp.bfloat16)
    pieces = grad_keys.reshape(slots, rows_dev, width)
    summed = lax.psum(return_pieces(pieces), "tp")
    d_latent = jnp.concatenate(
        [summed[:, :LAT], unrotate(summed[:, LAT:], cosine_table, sine_table)], axis=-1
    ).astype(jnp.bfloat16)
    return (d_query, d_latent)


def solution(mesh):
    placed = (P("cp", "tp", None), P("cp", None), P("cp", "tp", None), P("cp", None), P("cp"))
    return jax.shard_map(
        on_device,
        mesh=mesh,
        in_specs=placed,
        out_specs=(P("cp", "tp", None), P("cp", None)),
        check_vma=False,
    )
```

profile of v0, /device:TPU:1, one launch (start us, length us, event | category | flops | bytes accessed | tf_op | source)
XLA Modules:
  0.0 143.8 jit_solution(12763988456501908211)
XLA Ops:
  7.2 0.9 slice_convert_fusion.3
  8.1 0.9 slice_bitcast_fusion.3
  9.1 1.0 convolution_minimum_fusion.6
  10.1 0.2 convolution_minimum_fusion.5
  10.3 0.2 convolution_minimum_fusion.4
  10.5 0.2 convolution_minimum_fusion.3
  10.7 0.2 convolution_minimum_fusion.2
  10.9 0.2 convolution_minimum_fusion.1
  11.1 0.2 fusion.38
  11.4 1.3 fusion.32
  13.3 0.1 multiply_cosine_fusion
  13.5 0.6 copy-done.8
  14.1 0.7 pad_maximum_fusion.5
  14.7 4.0 %collective-permute-start = (bf16[128,576]{0,1:T(8,128)(2,1)}, bf16[128,576]{0,1:T(8,128)(2,1)S(1)}, u32[]{:S(2)}, u32[]{:S(2)}) collective-permute-start(bf16[128,576]{0,1:T(8,128)(2,1)} %pad_maximum_fusion.5), channel_id=1, source_target_pairs={{0,1},{1,2},{2,3},{3,4},{4,5},{5,6},{6,7},{7,8},{8,9},{9,10},{10,1... | collective-permute-start | bytes 442376 | tf_op jit(solution)/shard_map/ppermute | solution.py:19
  18.8 4.5 %collective-permute-start.1 = (bf16[128,576]{0,1:T(8,128)(2,1)}, bf16[128,576]{0,1:T(8,128)(2,1)S(1)}, u32[]{:S(2)}, u32[]{:S(2)}) collective-permute-start(bf16[128,576]{0,1:T(8,128)(2,1)} %pad_maximum_fusion.5), channel_id=1, source_target_pairs={{0,2},{1,3},{2,4},{3,5},{4,6},{5,7},{6,8},{7,9},{8,10},{9,11},{10,... | collective-permute-start | bytes 442376 | tf_op jit(solution)/shard_map/ppermute | solution.py:19
  23.3 4.3 %collective-permute-start.2 = (bf16[128,576]{0,1:T(8,128)(2,1)}, bf16[128,576]{0,1:T(8,128)(2,1)S(1)}, u32[]{:S(2)}, u32[]{:S(2)}) collective-permute-start(bf16[128,576]{0,1:T(8,128)(2,1)} %pad_maximum_fusion.5), channel_id=1, source_target_pairs={{0,3},{1,4},{2,5},{3,6},{4,7},{5,8},{6,9},{7,10},{8,11},{9,12},{10... | collective-permute-start | bytes 442376 | tf_op jit(solution)/shard_map/ppermute | solution.py:19
  27.7 1.0 slice_convert_fusion.2
  28.7 1.5 %slice.95 = bf16[128,16,512]{0,2,1:T(8,128)(2,1)} slice(bf16[128,16,576]{0,2,1:T(8,128)(2,1)S(1)} %copy-done), slice={[0:128], [0:16], [0:512]} | slice | bytes 4194304 | tf_op jit(solution)/shard_map/slice | solution.py:74
  30.2 0.7 compare_reduce_fusion
  30.8 0.8 and_reduce_fusion
  31.9 4.5 %copy.19 = bf16[128,16,512]{0,2,1:T(8,128)(2,1)} copy(bf16[128,16,512]{2,1,0:T(8,128)(2,1)} %param.9) | data formatting | bytes 4194304 | tf_op args[2]
  36.4 0.8 bitcast_select_fusion.4
  37.2 0.8 subtract_convert_fusion.1
  38.1 0.9 copy_bitcast_fusion
  39.0 0.5 copy.16
  39.5 0.2 reshape.298
  39.9 1.8 %fusion.10 = f32[512,128,16]{1,0,2:T(8,128)S(1)} fusion(bf16[512,576,1]{0,1,2:T(8,128)(2,1)S(1)} %reshape.298, bf16[128,16,32]{0,2,1:T(8,128)(2,1)S(1)} %copy-done.13, bf16[128,16,32]{0,2,1:T(8,128)(2,1)S(1)} %copy-done.12, bf16[128,16,512]{0,2,1:T(8,128)(2,1)S(1)} %copy-done.1), kind=kOutput, calls=%fused_computation.29 | convolution fusion | flops 1215037440 | bytes 7143424 | tf_op jit(solution)/shard_map/qhd,kd->hqk/dot_general | solution.py:117
  41.7 1.8 %fusion.39 = (f32[16,128]{1,0:T(8,128)S(1)}, f32[16,128,512]{1,2,0:T(8,128)S(1)}) fusion(f32[512,128,16]{1,0,2:T(8,128)S(1)} %fusion.10, pred[128,512]{0,1:T(8,128)(4,1)S(1)} %copy-done.14), kind=kOutput, calls=%fused_computation.87 | output fusion | flops 6291967 | bytes 8462336 | tf_op jit(solution)/shard_map/sub | solution.py:122
  43.5 0.5 fusion.8
  44.0 1.1 copy-done.2
  45.2 1.3 fusion.1
  46.4 1.6 %fusion.3 = bf16[16,128,512]{1,2,0:T(8,128)(2,1)S(1)} fusion(bf16[128,16,512]{0,2,1:T(8,128)(2,1)S(1)} %copy-done.2, f32[16,128]{1,0:T(8,128)S(1)} %bitcast.89, f32[16,128,512]{1,2,0:T(8,128)S(1)} %get-tuple-element.34, f32[16,128]{1,0:T(8,128)S(1)} %get-tuple-element.33, bf16[512,576]{0,1:T(8,128)(2,1)S(1)} %copy-done.3), kind=kOutput, calls=%fused_computation.6 | convolution fusion | flops 1078984704 | bytes 8929280 | tf_op jit(solution)/shard_map/qhd,kd->hqk/dot_general | solution.py:127
  48.0 1.4 convolution_bitcast_fusion.1
  49.4 1.4 convolution_bitcast_fusion
  50.8 2.0 %fusion.9 = f32[512,576]{0,1:T(8,128)S(1)} fusion(f32[512,576]{0,1:T(8,128)S(1)} %convolution_bitcast_fusion.1, bf16[16,128,512]{1,2,0:T(8,128)(2,1)S(1)} %fusion.8, bf16[128,16,512]{0,2,1:T(8,128)(2,1)S(1)} %copy-done.2, pred[]{:T(512)} %compare_reduce_fusion), kind=kOutput, calls=%fused_computation.21 | convolution fusion | flops 1074266112 | bytes 6291457 | tf_op jit(solution)/shard_map/hqk,qhd->kd/dot_general | solution.py:132
  53.0 1.3 collective-permute-start.3
  54.3 1.3 collective-permute-start.4
  55.6 1.3 collective-permute-start.5
  56.9 0.4 slice.157
  57.4 1.5 %collective-permute-done.3 = bf16[128,576]{0,1:T(8,128)(2,1)S(1)} collective-permute-done((bf16[128,576]{0,1:T(8,128)(2,1)S(1)}, bf16[128,576]{0,1:T(8,128)(2,1)S(1)}, u32[]{:S(2)}, u32[]{:S(2)}) %collective-permute-start.3) | collective-permute-done | bytes 147488 | tf_op jit(solution)/shard_map/ppermute | solution.py:19
  58.9 2.8 %collective-permute-done.4 = bf16[128,576]{0,1:T(8,128)(2,1)S(1)} collective-permute-done((bf16[128,576]{0,1:T(8,128)(2,1)S(1)}, bf16[128,576]{0,1:T(8,128)(2,1)S(1)}, u32[]{:S(2)}, u32[]{:S(2)}) %collective-permute-start.4) | collective-permute-done | bytes 147488 | tf_op jit(solution)/shard_map/ppermute | solution.py:19
  61.7 3.5 %collective-permute-done.5 = bf16[128,576]{0,1:T(8,128)(2,1)S(1)} collective-permute-done((bf16[128,576]{0,1:T(8,128)(2,1)S(1)}, bf16[128,576]{0,1:T(8,128)(2,1)S(1)}, u32[]{:S(2)}, u32[]{:S(2)}) %collective-permute-start.5) | collective-permute-done | bytes 147488 | tf_op jit(solution)/shard_map/ppermute | solution.py:19
  65.3 0.8 fusion.12
  66.1 1.6 %pad_maximum_fusion.1 = bf16[128,16,576]{0,2,1:T(8,128)(2,1)} fusion(bf16[128,16,32]{0,2,1:T(8,128)(2,1)S(1)} %get-tuple-element.15, bf16[128,16,32]{0,2,1:T(8,128)(2,1)S(1)} %get-tuple-element.14, bf16[128,16,512]{0,2,1:T(8,128)(2,1)S(1)} %slice.157), kind=kLoop, calls=%fused_computation.11 | loop fusion | flops 7077888 | bytes 4718592 | tf_op jit(solution)/shard_map/concatenate | solution.py:134
  67.7 66.8 %all-reduce.2.cloned.1.call-done = f32[128,576]{0,1:T(8,128)} async-done(((f32[128,576]{0,1:T(8,128)}), f32[128,576]{0,1:T(8,128)}) %all-reduce.2.cloned.1.call-update) | async-done | bytes 294928 | tf_op jit(solution)/shard_map/psum | solution.py:142
  134.5 1.0 slice.158
  135.4 0.9 fusion.29
  136.3 0.7 pad_maximum_fusion.6
  (52 shorter events, 0.8 us)
Async XLA Ops:
  7.2 21.5 %copy-start = (bf16[128,16,576]{0,2,1:T(8,128)(2,1)S(1)}, bf16[128,16,576]{0,2,1:T(8,128)(2,1)}, u32[]{:S(2)}) copy-start(bf16[128,16,576]{0,2,1:T(8,128)(2,1)} %param.7) | copy-start | bytes 7077892
  7.2 127.3 %all-reduce.2.cloned.1.call-start = ((), (), s32[]{:S(2)}) async-start(), calls=%async_computation | async-start | bytes 589824 | tf_op jit(solution)/shard_map/psum | solution.py:142
  7.2 11.5 %copy-start.15 = (f32[32]{0:T(128)}, f32[32]{0:T(128)S(1)}, u32[]{:S(2)}) copy-start(f32[32]{0:T(128)S(1)} %multiply_power_fusion) | copy-start | bytes 388
  13.3 1.4 %copy-start.17 = (f32[128]{0:T(128)}, f32[128]{0:T(128)S(1)}, u32[]{:S(2)}) copy-start(f32[128]{0:T(128)S(1)} %add_add_fusion) | copy-start | bytes 1540
  13.5 0.6 copy-start.8
  13.5 0.6 copy-start.10
  13.5 23.7 %copy-start.4 = (f32[128,32]{0,1:T(8,128)}, f32[128,32]{0,1:T(8,128)S(1)}, u32[]{:S(2)}) copy-start(f32[128,32]{0,1:T(8,128)S(1)} %get-tuple-element.27) | copy-start | bytes 49156
  13.5 23.7 %copy-start.6 = (f32[128,32]{0,1:T(8,128)}, f32[128,32]{0,1:T(8,128)S(1)}, u32[]{:S(2)}) copy-start(f32[128,32]{0,1:T(8,128)S(1)} %get-tuple-element.28) | copy-start | bytes 49156
  14.7 23.3 %collective-permute-start = (bf16[128,576]{0,1:T(8,128)(2,1)}, bf16[128,576]{0,1:T(8,128)(2,1)S(1)}, u32[]{:S(2)}, u32[]{:S(2)}) collective-permute-start(bf16[128,576]{0,1:T(8,128)(2,1)} %pad_maximum_fusion.5), channel_id=1, source_target_pairs={{0,1},{1,2},{2,3},{3,4},{4,5},{5,6},{6,7},{7,8},{8,9},{9,10},{10,1... | collective-permute-start | bytes 442376 | tf_op jit(solution)/shard_map/ppermute | solution.py:19
  18.8 19.3 %collective-permute-start.1 = (bf16[128,576]{0,1:T(8,128)(2,1)}, bf16[128,576]{0,1:T(8,128)(2,1)S(1)}, u32[]{:S(2)}, u32[]{:S(2)}) collective-permute-start(bf16[128,576]{0,1:T(8,128)(2,1)} %pad_maximum_fusion.5), channel_id=1, source_target_pairs={{0,2},{1,3},{2,4},{3,5},{4,6},{5,7},{6,8},{7,9},{8,10},{9,11},{10,... | collective-permute-start | bytes 442376 | tf_op jit(solution)/shard_map/ppermute | solution.py:19
  23.3 14.7 %collective-permute-start.2 = (bf16[128,576]{0,1:T(8,128)(2,1)}, bf16[128,576]{0,1:T(8,128)(2,1)S(1)}, u32[]{:S(2)}, u32[]{:S(2)}) collective-permute-start(bf16[128,576]{0,1:T(8,128)(2,1)} %pad_maximum_fusion.5), channel_id=1, source_target_pairs={{0,3},{1,4},{2,5},{3,6},{4,7},{5,8},{6,9},{7,10},{8,11},{9,12},{10... | collective-permute-start | bytes 442376 | tf_op jit(solution)/shard_map/ppermute | solution.py:19
  31.9 6.2 %copy-start.9 = (bf16[128,32]{0,1:T(8,128)(2,1)S(1)}, bf16[128,32]{0,1:T(8,128)(2,1)}, u32[]{:S(2)}) copy-start(bf16[128,32]{0,1:T(8,128)(2,1)} %copy-done.8) | copy-start | bytes 24580
  31.9 6.2 %copy-start.11 = (bf16[128,32]{0,1:T(8,128)(2,1)S(1)}, bf16[128,32]{0,1:T(8,128)(2,1)}, u32[]{:S(2)}) copy-start(bf16[128,32]{0,1:T(8,128)(2,1)} %copy-done.10) | copy-start | bytes 24580
  38.1 1.8 %copy-start.1 = (bf16[128,16,512]{0,2,1:T(8,128)(2,1)S(1)}, bf16[128,16,512]{0,2,1:T(8,128)(2,1)}, u32[]{:S(2)}) copy-start(bf16[128,16,512]{0,2,1:T(8,128)(2,1)} %slice.95) | copy-start | bytes 6291460
  38.1 1.8 %copy-start.12 = (bf16[128,16,32]{0,2,1:T(8,128)(2,1)S(1)}, bf16[128,16,32]{0,2,1:T(8,128)(2,1)}, u32[]{:S(2)}) copy-start(bf16[128,16,32]{0,2,1:T(8,128)(2,1)} %get-tuple-element.19) | copy-start | bytes 393220
  38.1 1.8 %copy-start.13 = (bf16[128,16,32]{0,2,1:T(8,128)(2,1)S(1)}, bf16[128,16,32]{0,2,1:T(8,128)(2,1)}, u32[]{:S(2)}) copy-start(bf16[128,16,32]{0,2,1:T(8,128)(2,1)} %get-tuple-element.20) | copy-start | bytes 393220
  39.9 1.8 %copy-start.14 = (pred[128,512]{0,1:T(8,128)(4,1)S(1)}, pred[128,512]{0,1:T(8,128)(4,1)}, u32[]{:S(2)}) copy-start(pred[128,512]{0,1:T(8,128)(4,1)} %bitcast_select_fusion.4) | copy-start | bytes 196612
  43.5 1.6 %copy-start.2 = (bf16[128,16,512]{0,2,1:T(8,128)(2,1)S(1)}, bf16[128,16,512]{0,2,1:T(8,128)(2,1)}, u32[]{:S(2)}) copy-start(bf16[128,16,512]{0,2,1:T(8,128)(2,1)} %copy.19) | copy-start | bytes 6291460
  43.5 1.7 %copy-start.3 = (bf16[512,576]{0,1:T(8,128)(2,1)S(1)}, bf16[512,576]{0,1:T(8,128)(2,1)}, u32[]{:S(2)}) copy-start(bf16[512,576]{0,1:T(8,128)(2,1)} %copy_bitcast_fusion) | copy-start | bytes 1769476
  52.9 4.4 %copy-start.5 = (f32[128,32]{0,1:T(8,128)S(1)}, f32[128,32]{0,1:T(8,128)}, u32[]{:S(2)}) copy-start(f32[128,32]{0,1:T(8,128)} %copy-done.4) | copy-start | bytes 49156
  52.9 4.4 %copy-start.7 = (f32[128,32]{0,1:T(8,128)S(1)}, f32[128,32]{0,1:T(8,128)}, u32[]{:S(2)}) copy-start(f32[128,32]{0,1:T(8,128)} %copy-done.6) | copy-start | bytes 49156
  53.0 5.9 %collective-permute-start.3 = (bf16[128,576]{0,1:T(8,128)(2,1)S(1)}, bf16[128,576]{0,1:T(8,128)(2,1)S(1)}, u32[]{:S(2)}, u32[]{:S(2)}) collective-permute-start(bf16[128,576]{0,1:T(8,128)(2,1)S(1)} %get-tuple-element.16), channel_id=1, source_target_pairs={{1,0},{2,1},{3,2},{4,3},{5,4},{6,5},{7,6},{8,7},{9,8},{10,9},{11,1... | collective-permute-start | bytes 442376 | tf_op jit(solution)/shard_map/ppermute | solution.py:19
  54.3 7.4 %collective-permute-start.4 = (bf16[128,576]{0,1:T(8,128)(2,1)S(1)}, bf16[128,576]{0,1:T(8,128)(2,1)S(1)}, u32[]{:S(2)}, u32[]{:S(2)}) collective-permute-start(bf16[128,576]{0,1:T(8,128)(2,1)S(1)} %get-tuple-element.18), channel_id=1, source_target_pairs={{2,0},{3,1},{4,2},{5,3},{6,4},{7,5},{8,6},{9,7},{10,8},{11,9},{12,... | collective-permute-start | bytes 442376 | tf_op jit(solution)/shard_map/ppermute | solution.py:19
  55.6 9.6 %collective-permute-start.5 = (bf16[128,576]{0,1:T(8,128)(2,1)S(1)}, bf16[128,576]{0,1:T(8,128)(2,1)S(1)}, u32[]{:S(2)}, u32[]{:S(2)}) collective-permute-start(bf16[128,576]{0,1:T(8,128)(2,1)S(1)} %get-tuple-element.17), channel_id=1, source_target_pairs={{3,0},{4,1},{5,2},{6,3},{7,4},{8,5},{9,6},{10,7},{11,8},{12,9},{13... | collective-permute-start | bytes 442376 | tf_op jit(solution)/shard_map/ppermute | solution.py:19
  66.1 69.4 %copy-start.16 = (f32[32]{0:T(128)S(1)}, f32[32]{0:T(128)}, u32[]{:S(2)}) copy-start(f32[32]{0:T(128)} %copy-done.15) | copy-start | bytes 388
  66.1 69.4 %copy-start.18 = (f32[128]{0:T(128)S(1)}, f32[128]{0:T(128)}, u32[]{:S(2)}) copy-start(f32[128]{0:T(128)} %copy-done.17) | copy-start | bytes 1540
Sparse Core Ops, SparseCore 0:
  66.2 68.2 all-reduce.1
where the time goes:
time: 146 us; the launch traced here: 144 us
  waiting for transfers between devices  74.6 us (51%)
  starting transfers between devices  16.8 us (12%)
  between operations  15.1 us (10%)
  other arithmetic  14.5 us (10%)
  matrix products  11.7 us (8%)
  local copies, waits for them, and re-layouts  11.1 us (8%)
    psum x1, waiting for transfers between devices, on_device(): summed = lax.psum(return_pieces(pieces), 'tp')  66.8 us
    ppermute x6, starting transfers between devices, shifted(): return lax.ppermute(block, axis, route)  16.8 us
    ppermute x6, waiting for transfers between devices, shifted(): return lax.ppermute(block, axis, route)  7.86 us
    unnamed x39, local copies, waits for them, and re-layouts  6.45 us
  transfers between devices with their start and end apart: 7, of which 4 were waited for; matrix products, arithmetic and copies ran while one was open for 9% of the time, Pallas kernels for 0%

commit v1 on v0

v1 whole, which is shorter than its diff:
```python
import functools

import jax
import jax.numpy as jnp
import numpy as np
from jax import lax
from jax.experimental import pallas as pl
from jax.experimental.pallas import tpu as pltpu
from jax.sharding import PartitionSpec as P

LAT = 512
ROPE = 64
BS = 128
WIDTH = LAT + ROPE
HALF = BS // 2
SIDE = BS + HALF
REMOTE = 2 * SIDE
KEYS = BS + REMOTE
TILE = 256

score_scale = 192.0 ** (-0.5)
rope_base = 10000.0
exponent_scale = score_scale * float(np.log2(np.e))
MASKED = -1e30

BF = jnp.bfloat16
F32 = jnp.float32
NT = (((1,), (1,)), ((), ()))
NN = (((1,), (0,)), ((), ()))
TN = (((0,), (0,)), ((), ()))


def dot(a, b, dims):
    return lax.dot_general(a, b, dims, preferred_element_type=F32)


def vmem(shape, dtype):
    return pltpu.VMEM(shape, dtype)


def in_vmem(x):
    return pltpu.with_memory_space_constraint(x, pltpu.VMEM)


def whole():
    return pl.BlockSpec(memory_space=pltpu.VMEM)


def scalars():
    return pl.BlockSpec(memory_space=pltpu.SMEM)


def turn(values, table):
    half = ROPE // 2
    first, second, cosine, sine = values[:half], values[half:], table[:half], table[half:]
    return jnp.concatenate([first * cosine - second * sine, first * sine + second * cosine], axis=0)


def turn_back(values, table):
    half = ROPE // 2
    first, second, cosine, sine = values[:half], values[half:], table[:half], table[half:]
    return jnp.concatenate([first * cosine + second * sine, second * cosine - first * sine], axis=0)


def keys_kernel(core_ref, anc_ref, parents_ref, freq_ref, latent_ref, keys_ref, half_ref, table_ref, closure_ref):
    row = lax.broadcasted_iota(jnp.int32, (BS, BS), 0)
    col = lax.broadcasted_iota(jnp.int32, (BS, BS), 1)
    linked = (row == parents_ref[...]) | (row == col)
    closure = jnp.where(linked, 1.0, 0.0).astype(BF)
    for _ in range((BS - 1).bit_length()):
        reach = jnp.minimum(dot(closure, closure, NN), 1.0)
        closure = reach.astype(BF)
    closure_ref[...] = reach
    depth = jnp.sum(reach, axis=0, keepdims=True) - 1.0
    count = 0
    for k in range(anc_ref.shape[1]):
        count = count + (anc_ref[0, k] >= 0).astype(jnp.int32)
    angles = (depth + (BS * count).astype(F32)) * freq_ref[...]
    table = jnp.concatenate([jnp.cos(angles), jnp.sin(angles)], axis=0)
    table_ref[...] = table
    turned = turn(latent_ref[LAT:, :].astype(F32), table)
    for lo in range(0, LAT, BS):
        keys_ref[:, lo : lo + BS] = latent_ref[lo : lo + BS, :].T
    keys_ref[:, LAT:] = turned.T.astype(BF)
    half_ref[...] = keys_ref[pl.ds(pl.multiple_of(core_ref[0] * HALF, HALF), HALF), :]


def own_kernel(heads, query_ref, grad_ref, keys_ref, table_ref, closure_ref, cat_ref, sorted_ref, score_ref, slope_ref):
    rows = TILE // heads
    row = lax.broadcasted_iota(jnp.int32, (TILE, TILE), 0)
    col = lax.broadcasted_iota(jnp.int32, (TILE, TILE), 1)
    order = jnp.where(col == (row % rows) * heads + row // rows, 1.0, 0.0).astype(BF)

    def sort(t, carry):
        chunk = grad_ref[pl.ds(pl.multiple_of(t * TILE, TILE), TILE), :]
        chunk = dot(order, chunk, NN).astype(BF)
        for h in range(heads):
            at = pl.multiple_of(h * BS + t * rows, rows)
            sorted_ref[pl.ds(at, rows), :] = chunk[h * rows : (h + 1) * rows]
        return carry

    lax.fori_loop(0, BS // rows, sort, 0)
    table = table_ref[...]
    seen = jnp.concatenate([closure_ref[...]] * (TILE // BS), axis=1) > 0.5

    def step(t, carry):
        here = pl.ds(pl.multiple_of(t * TILE, TILE), TILE)
        for k in range(TILE // BS):
            lanes = pl.ds(pl.multiple_of(t * TILE + k * BS, BS), BS)
            at = pl.multiple_of((t * (TILE // BS) + k) * WIDTH, ROPE)
            cat_ref[:LAT, lanes] = query_ref[pl.ds(at, LAT), :]
            cat_ref[LAT:, lanes] = turn(query_ref[pl.ds(at + LAT, ROPE), :].astype(F32), table).astype(BF)
        score = dot(keys_ref[...], cat_ref[:, here], NN)
        score_ref[:, here] = jnp.where(seen, score * exponent_scale, MASKED)
        slope_ref[:, here] = dot(keys_ref[:, :LAT], sorted_ref[here, :], NT)
        return carry

    lax.fori_loop(0, heads * BS // TILE, step, 0)


def key_grads(rows, weight_ref, dscore_ref, cat_ref, sorted_ref):
    turned = dot(dscore_ref[rows, :], cat_ref[...], NT) * score_scale
    plain = dot(weight_ref[rows, :], sorted_ref[...], NN)
    return turned[:, :LAT] + plain, turned[:, LAT:]


def main_kernel(bias_ref, cat_ref, sorted_ref, mine_ref, other_ref, score_ref, slope_ref,
                weight_ref, dscore_ref, gmine_ref, gother_ref):
    total = cat_ref.shape[1]
    bounds = ((0, BS), (BS, SIDE))

    def step(t, carry):
        here = pl.ds(pl.multiple_of(t * TILE, TILE), TILE)
        query = cat_ref[:, here]
        grad = sorted_ref[here, :]
        scores, slopes, biases = [score_ref[:, here]], [slope_ref[:, here]], [0.0]
        for side, ref in enumerate((mine_ref, other_ref)):
            score = dot(ref[...], query, NN) * exponent_scale
            slope = dot(ref[:, :LAT], grad, NT)
            for part, (lo, hi) in enumerate(bounds):
                scores.append(score[lo:hi])
                slopes.append(slope[lo:hi])
                biases.append(bias_ref[2 * side + part])
        largest = functools.reduce(
            jnp.maximum, [jnp.max(s, axis=0, keepdims=True) + b for s, b in zip(scores, biases)]
        )
        expos = [jnp.exp2(s - (largest - b)) for s, b in zip(scores, biases)]
        inverse = 1.0 / sum(jnp.sum(e, axis=0, keepdims=True) for e in expos)
        delta = sum(jnp.sum(e * s, axis=0, keepdims=True) for e, s in zip(expos, slopes)) * inverse
        at = 0
        for e, s in zip(expos, slopes):
            rows = pl.ds(at, e.shape[0])
            weight = e * inverse
            weight_ref[rows, here] = weight.astype(BF)
            dscore_ref[rows, here] = (weight * (s - delta)).astype(BF)
            at += e.shape[0]
        return carry

    lax.fori_loop(0, total // TILE, step, 0)
    for out, lo in ((gother_ref, BS + SIDE), (gmine_ref, BS)):
        lead, tail = key_grads(pl.ds(lo, SIDE), weight_ref, dscore_ref, cat_ref, sorted_ref)
        out[:, :LAT] = lead.astype(out.dtype)
        out[:, LAT:] = tail.astype(out.dtype)


def query_kernel(weight_ref, dscore_ref, cat_ref, sorted_ref, keys_ref, mine_ref, other_ref, table_ref,
                 dquery_ref, gown_ref, every_ref, turned_ref):
    t = pl.program_id(0)

    @pl.when(t == 0)
    def _():
        every_ref[:BS, :] = keys_ref[...]
        every_ref[BS : BS + SIDE, :] = mine_ref[...]
        every_ref[BS + SIDE :, :] = other_ref[...]
        for lo in range(0, KEYS, BS):
            turned_ref[:, lo : lo + BS] = every_ref[lo : lo + BS, :].T
        lead, tail = key_grads(pl.ds(0, BS), weight_ref, dscore_ref, cat_ref, sorted_ref)
        gown_ref[:, :LAT] = lead
        gown_ref[:, LAT:] = tail

    dscore = dscore_ref[:, pl.ds(pl.multiple_of(t * TILE, TILE), TILE)]
    grads = dot(turned_ref[...], dscore, NN) * score_scale
    for k in range(TILE // BS):
        part = grads[:, k * BS : (k + 1) * BS]
        dquery_ref[k, :LAT, :] = part[:LAT].astype(BF)
        dquery_ref[k, LAT:, :] = turn_back(part[LAT:], table_ref[...]).astype(BF)


def finish_kernel(core_ref, chip_ref, near_ref, far_ref, rest_ref, table_ref, out_ref, sum_ref):
    core = core_ref[0]
    sum_ref[...] = chip_ref[...].astype(F32)
    mine = pl.ds(pl.multiple_of(core * HALF, HALF), HALF)
    other = pl.ds(pl.multiple_of((1 - core) * HALF, HALF), HALF)
    sum_ref[mine, :] += far_ref[...].astype(F32)
    sum_ref[other, :] += rest_ref[BS:, :].astype(F32)
    sum_ref[...] += near_ref[...].astype(F32) + rest_ref[:BS, :].astype(F32)
    for lo in range(0, LAT, BS):
        out_ref[lo : lo + BS, :] = sum_ref[:, lo : lo + BS].T.astype(BF)
    out_ref[LAT:, :] = turn_back(sum_ref[:, LAT:].T, table_ref[...]).astype(BF)


def by_core(block, even, odd):
    tp, cp = lax.axis_size("tp"), lax.axis_size("cp")
    route = []
    for t in range(tp):
        step = odd if t % 2 else even
        for c in range(cp):
            if 0 <= c + step < cp or WRAP:
                route.append((t * cp + c, t * cp + (c + step) % cp))
    return lax.ppermute(block, ("tp", "cp"), route)


WRAP = True


def other_core(block):
    return lax.ppermute(block, "tp", [(t, t ^ 1) for t in range(lax.axis_size("tp"))])


def along_x(block, even, odd):
    tp = lax.axis_size("tp")
    route = [(t, (t + 2 * (odd if t % 2 else even)) % tp) for t in range(tp)]
    return lax.ppermute(block, "tp", route)


def halves(core, mine, other):
    return jnp.where(core == 0, jnp.concatenate([mine, other]), jnp.concatenate([other, mine]))


def on_device(query, latent, grad_out, ancestors, parents):
    rows, heads, _ = query.shape
    total = rows * heads
    core = lax.axis_index("tp") % 2
    here = lax.axis_index("cp")
    core_index = core.reshape(1).astype(jnp.int32)
    q = in_vmem(query.transpose(1, 2, 0).reshape(heads * WIDTH, rows))
    g = in_vmem(grad_out.reshape(total, LAT))
    half = ROPE // 2
    lane_freq = rope_base ** (-2.0 * np.arange(half, dtype=np.float64) / ROPE)
    freq = jnp.asarray(np.tile(lane_freq[:, None], (1, BS)), dtype=F32)
    params = pltpu.CompilerParams(vmem_limit_bytes=40 * 2**20)

    keys, keys_half, table, closure = pl.pallas_call(
        keys_kernel,
        in_specs=[scalars(), scalars(), whole(), whole(), whole()],
        out_specs=[whole()] * 4,
        out_shape=[vmem((BS, WIDTH), BF), vmem((HALF, WIDTH), BF), vmem((ROPE, BS), F32), vmem((BS, BS), F32)],
        name="keys",
    )(core_index, ancestors, parents.reshape(1, BS), freq, latent.T)

    fetched = by_core(keys, 1, 2)
    fetched_half = by_core(keys_half, 3, 3)

    cat, ordered, score_own, slope_own = pl.pallas_call(
        functools.partial(own_kernel, heads),
        in_specs=[whole()] * 5,
        out_specs=[whole()] * 4,
        out_shape=[vmem((WIDTH, total), BF), vmem((total, LAT), BF), vmem((BS, total), F32), vmem((BS, total), F32)],
        cost_estimate=pl.CostEstimate(flops=2 * total * BS * 1800, bytes_accessed=4 * total * WIDTH, transcendentals=0),
        compiler_params=params,
        name="own",
    )(q, g, keys, table, closure)

    mine = jnp.concatenate([fetched, fetched_half])
    other = other_core(mine)

    offsets = jnp.where(core == 0, jnp.array([1, 3, 2, 3]), jnp.array([2, 3, 1, 3]))
    ids = here - offsets
    listed = jnp.any((ids[:, None] == ancestors[0][None, :]) & (ids[:, None] >= 0), axis=1)
    bias = jnp.where(listed, 0.0, MASKED).astype(F32)

    weight, dscore, gmine, gother = pl.pallas_call(
        main_kernel,
        in_specs=[scalars()] + [whole()] * 6,
        out_specs=[whole()] * 4,
        out_shape=[vmem((KEYS, total), BF), vmem((KEYS, total), BF), vmem((SIDE, WIDTH), F32), vmem((SIDE, WIDTH), BF)],
        cost_estimate=pl.CostEstimate(flops=2 * total * REMOTE * 2560, bytes_accessed=8 * total * WIDTH, transcendentals=total * KEYS),
        compiler_params=params,
        name="main",
    )(bias, cat, ordered, mine, other, score_own, slope_own)

    gmine = (gmine + other_core(gother).astype(F32)).astype(BF)
    back = by_core(gmine[:BS], -1, -2)
    back_half = by_core(gmine[BS:], -3, -3)

    dquery, gown = pl.pallas_call(
        query_kernel,
        grid=(total // TILE,),
        in_specs=[whole()] * 8,
        out_specs=[pl.BlockSpec((TILE // BS, WIDTH, BS), lambda t: (t, 0, 0)), whole()],
        out_shape=[jax.ShapeDtypeStruct((heads, WIDTH, rows), BF), vmem((BS, WIDTH), F32)],
        scratch_shapes=[pltpu.VMEM((KEYS, WIDTH), BF), pltpu.VMEM((WIDTH, KEYS), BF)],
        cost_estimate=pl.CostEstimate(flops=2 * total * KEYS * 900, bytes_accessed=4 * total * WIDTH, transcendentals=0),
        compiler_params=params,
        name="dquery",
    )(weight, dscore, cat, ordered, keys, mine, other, table)

    back_half = back_half.astype(F32)
    nothing = jnp.zeros_like(back_half)
    device_sum = (gown + back.astype(F32) + halves(core, back_half, nothing)).astype(BF)
    chip_sum = (device_sum.astype(F32) + other_core(device_sum).astype(F32)).astype(BF)
    near = along_x(chip_sum, 1, -1)
    far = along_x(lax.dynamic_slice_in_dim(chip_sum, core * HALF, HALF), 2, 2)
    rest = other_core(jnp.concatenate([near, far]))
    d_latent = pl.pallas_call(
        finish_kernel,
        in_specs=[scalars()] + [whole()] * 5,
        out_specs=whole(),
        out_shape=jax.ShapeDtypeStruct((WIDTH, BS), BF),
        scratch_shapes=[pltpu.VMEM((BS, WIDTH), F32)],
        name="finish",
    )(core_index, chip_sum, near, far, rest, table)
    return (dquery.transpose(2, 0, 1), d_latent.T)


def solution(mesh):
    placed = (P("cp", "tp", None), P("cp", None), P("cp", "tp", None), P("cp", None), P("cp"))
    return jax.shard_map(
        on_device,
        mesh=mesh,
        in_specs=placed,
        out_specs=(P("cp", "tp", None), P("cp", None)),
        check_vma=False,
    )
```

time: 146 us -> 57.9 us (0.40); the launches traced: 144 us -> 57.7 us
  waiting for transfers between devices: 74.6 us -> 10.4 us
  Pallas kernels: 0 us -> 23.6 us
  between operations: 15.1 us -> 0.79 us
  other arithmetic: 14.5 us -> 1.03 us
  matrix products: 11.7 us -> 0 us
  local copies, waits for them, and re-layouts: 11.1 us -> 4.02 us
    psum x1 -> x0, waiting for transfers between devices: 66.8 us -> none  [on_device(): summed = lax.psum(return_pieces(pieces), 'tp')]
    pallas_call x0 -> x5, Pallas kernels: none -> 23.6 us  [the longest x1 8.94 us: on_device(): pl.pallas_call(main_kernel, in_specs=[scalars()] + [whole()] * 6, out_spe...]
    dot_general x13 -> x0, matrix products: 11.7 us -> none  [the longest x7 2.25 us: tree_positions(): jnp.einsum('bij,bjk->bik', closure, closure, precision=lax.Precision.HIGH...]
    concatenate x3 -> x1, other arithmetic: 2.95 us -> 0.02 us  [on_device(): rest = other_core(jnp.concatenate([near, far]))]
    slice x4 -> x2, local copies, waits for them, and re-layouts: 2.88 us -> 0.02 us  [the longest x1 0.02 us: on_device(): back = by_core(gmine[:BS], -1, -2)]
    ppermute x6 -> x10, waiting for transfers between devices: 7.86 us -> 10.4 us  [the longest x2 5.48 us: along_x(): return lax.ppermute(block, 'tp', route)]
    another operation x6 -> x0, other arithmetic: 2.57 us -> none
    unnamed x39 -> x17, local copies, waits for them, and re-layouts: 6.45 us -> 3.97 us
  transfers between devices with their start and end apart: 7 -> 10, of which waited for: 4 -> 5; matrix products, arithmetic and copies ran while one was open for 9% -> 2% of each run, Pallas kernels for 0% -> 18%
where the time goes in v1:
time: 57.9 us; the launch traced here: 57.7 us
  Pallas kernels  23.6 us (41%)
  starting transfers between devices  17.8 us (31%)
  waiting for transfers between devices  10.4 us (18%)
  local copies, waits for them, and re-layouts  4.02 us (7%)
  other arithmetic  1.03 us (2%)
  between operations  0.79 us (1%)
    ppermute x4, starting transfers between devices, by_core(): return lax.ppermute(block, ('tp', 'cp'), route)  12.9 us
    pallas_call x1, Pallas kernels, on_device(): pl.pallas_call(main_kernel, in_specs=[scalars()] + [whole()] * 6, out_spe...  8.94 us
    pallas_call x1, Pallas kernels, on_device(): pl.pallas_call(query_kernel, grid=(total // TILE,), in_specs=[whole()] *...  5.79 us
    ppermute x2, waiting for transfers between devices, along_x(): return lax.ppermute(block, 'tp', route)  5.48 us
    ppermute x4, waiting for transfers between devices, other_core(): lax.ppermute(block, 'tp', [(t, t ^ 1) for t in range(lax.axis_size('tp'))])  4.95 us
    pallas_call x1, Pallas kernels, on_device(): pl.pallas_call(functools.partial(own_kernel, heads), in_specs=[whole()] *...  4.78 us
    unnamed x17, local copies, waits for them, and re-layouts  3.97 us
    ppermute x2, starting transfers between devices, along_x(): return lax.ppermute(block, 'tp', route)  3.17 us
  transfers between devices with their start and end apart: 10, of which 5 were waited for; matrix products, arithmetic and copies ran while one was open for 2% of the time, Pallas kernels for 18%

profile of v1, /device:TPU:1, one launch (start us, length us, event | category | flops | bytes accessed | tf_op | source)
XLA Modules:
  0.0 57.7 jit_solution(13151569976329415143)
XLA Ops:
  0.6 2.1 %keys.1 = (bf16[128,576]{1,0:T(8,128)(2,1)S(1)}, bf16[64,576]{1,0:T(8,128)(2,1)S(1)}, f32[64,128]{1,0:T(8,128)S(1)}, f32[128,128]{1,0:T(8,128)S(1)}) custom-call(s32[1]{0:T(128)} %bitcast.4.core_ref, s32[1,3]{1,0:T(1,128)} %anc_ref.1, s32[1,128]{1,0:T(1,128)} %bitcast.15, f32[32,128]{1,0:T(8,128)} %constant.41.clone.freq_ref, bf16[576,128]{1,0:T(8,128)(2,1)} %bitcast.12), custom_call_target="tpu_custom_call" | custom-call | tf_op jit(solution)/shard_map/keys/pallas_call | solution.py:243
  2.8 0.0 copy-start.2
  2.8 3.8 %collective-permute-start = (bf16[128,576]{1,0:T(8,128)(2,1)S(1)}, bf16[128,576]{1,0:T(8,128)(2,1)S(1)}, u32[]{:S(2)}, u32[]{:S(2)}) collective-permute-start(bf16[128,576]{1,0:T(8,128)(2,1)S(1)} %get-tuple-element.16.keys_ref), channel_id=1, source_target_pairs={{0,1},{1,2},{2,3},{3,4},{4,5},{5,6},{6,7},{7,8},{8,9},{9,10},{10,1... | collective-permute-start | bytes 442376 | tf_op jit(solution)/shard_map/ppermute | solution.py:210
  6.6 2.1 %collective-permute-start.1 = (bf16[64,576]{1,0:T(8,128)(2,1)S(1)}, bf16[64,576]{1,0:T(8,128)(2,1)S(1)}, u32[]{:S(2)}, u32[]{:S(2)}) collective-permute-start(bf16[64,576]{1,0:T(8,128)(2,1)S(1)} %get-tuple-element.21), channel_id=1, source_target_pairs={{0,3},{1,4},{2,5},{3,6},{4,7},{5,8},{6,9},{7,10},{8,11},{9,12},{10... | collective-permute-start | bytes 221192 | tf_op jit(solution)/shard_map/ppermute | solution.py:210
  8.7 0.7 %broadcast_compare_fusion = (pred[4]{0:T(512)(128)(4,1)S(1)}, s32[4]{0:T(128)S(1)}) fusion(s32[4]{0:T(128)} %constant.42.clone, s32[4]{0:T(128)} %constant.43.clone, pred[]{:T(512)S(6)} %eq.21, s32[]{:T(128)S(6)} %axis_index.22), kind=kLoop, calls=%fused_computation.10 | loop fusion | flops 12 | bytes 57 | tf_op jit(solution)/shard_map/ge | solution.py:269
  9.4 0.0 copy-start
  9.4 1.7 %copy-done = bf16[128,16,576]{0,2,1:T(8,128)(2,1)S(1)} copy-done((bf16[128,16,576]{0,2,1:T(8,128)(2,1)S(1)}, bf16[128,16,576]{0,2,1:T(8,128)(2,1)}, u32[]{:S(2)}) %copy-start) | copy-done | bytes 2359320
  11.1 0.0 copy-start.1
  11.1 1.6 %copy-done.1 = bf16[128,16,512]{2,1,0:T(8,128)(2,1)S(1)} copy-done((bf16[128,16,512]{2,1,0:T(8,128)(2,1)S(1)}, bf16[128,16,512]{2,1,0:T(8,128)(2,1)}, u32[]{:S(2)}) %copy-start.1) | copy-done | bytes 2097176
  12.6 0.0 copy-start.7
  12.6 4.8 %own.1 = (bf16[576,2048]{1,0:T(8,128)(2,1)S(1)}, bf16[2048,512]{1,0:T(8,128)(2,1)S(1)}, f32[128,2048]{1,0:T(8,128)S(1)}, f32[128,2048]{1,0:T(8,128)S(1)}) custom-call(bf16[9216,128]{1,0:T(8,128)(2,1)S(1)} %bitcast.10, bf16[2048,512]{1,0:T(8,128)(2,1)S(1)} %bitcast.11, bf16[128,576]{1,0:T(8,128)(2,1)S(1)} %get-tuple-element.16.keys_ref, ...), custom_call_target="tpu_custom_call" | custom-call | flops 943718400 | bytes 4718592 | tf_op jit(solution)/shard_map/own/pallas_call | solution.py:254
  17.4 0.0 copy-done.7
  17.4 0.2 and_reduce_fusion
  17.6 0.0 collective-permute-done
  17.7 0.0 collective-permute-done.1
  17.7 0.4 collective-permute-start.2
  18.1 1.2 %collective-permute-done.2.other_ref = bf16[192,576]{1,0:T(8,128)(2,1)S(1)} collective-permute-done((bf16[192,576]{1,0:T(8,128)(2,1)S(1)}, bf16[192,576]{1,0:T(8,128)(2,1)S(1)}, u32[]{:S(2)}, u32[]{:S(2)}) %collective-permute-start.2) | collective-permute-done | bytes 221216 | tf_op jit(solution)/shard_map/ppermute | solution.py:217
  19.3 8.9 %main.1 = (bf16[512,2048]{1,0:T(8,128)(2,1)S(1)}, bf16[512,2048]{1,0:T(8,128)(2,1)S(1)}, f32[192,576]{1,0:T(8,128)S(1)}, bf16[192,576]{1,0:T(8,128)(2,1)S(1)}) custom-call(f32[4]{0:T(128)S(1)} %broadcast_select_fusion.1.bias_ref, bf16[576,2048]{1,0:T(8,128)(2,1)S(1)} %get-tuple-element.19.cat_ref, bf16[2048,512]{1,0:T(8,128)(2,1)S(1)} %get-tuple-element.20.sorted_ref, ...), custom_call_target="tpu_custom_call" | custom-call | flops 4026531840 | bytes 9437184 | tf_op jit(solution)/shard_map/main/pallas_call | solution.py:272
  28.2 0.4 collective-permute-start.3
  28.6 1.2 %collective-permute-done.3 = bf16[192,576]{1,0:T(8,128)(2,1)S(1)} collective-permute-done((bf16[192,576]{1,0:T(8,128)(2,1)S(1)}, bf16[192,576]{1,0:T(8,128)(2,1)S(1)}, u32[]{:S(2)}, u32[]{:S(2)}) %collective-permute-start.3) | collective-permute-done | bytes 221216 | tf_op jit(solution)/shard_map/ppermute | solution.py:217
  29.9 4.8 %collective-permute-start.4 = (bf16[128,576]{1,0:T(8,128)(2,1)S(1)}, bf16[128,576]{1,0:T(8,128)(2,1)S(1)}, u32[]{:S(2)}, u32[]{:S(2)}) collective-permute-start(bf16[128,576]{1,0:T(8,128)(2,1)S(1)} %slice.8), channel_id=1, source_target_pairs={{0,31},{1,0},{2,1},{3,2},{4,3},{5,4},{6,5},{7,6},{8,7},{9,8},{10,9... | collective-permute-start | bytes 442376 | tf_op jit(solution)/shard_map/ppermute | solution.py:210
  34.8 2.1 %collective-permute-start.5 = (bf16[64,576]{1,0:T(8,128)(2,1)S(1)}, bf16[64,576]{1,0:T(8,128)(2,1)S(1)}, u32[]{:S(2)}, u32[]{:S(2)}) collective-permute-start(bf16[64,576]{1,0:T(8,128)(2,1)S(1)} %slice.9), channel_id=1, source_target_pairs={{0,29},{1,30},{2,31},{3,0},{4,1},{5,2},{6,3},{7,4},{8,5},{9,6},{10... | collective-permute-start | bytes 221192 | tf_op jit(solution)/shard_map/ppermute | solution.py:210
  36.9 0.0 copy-done.2
  36.9 5.8 %dquery.1 = (bf16[16,576,128]{2,1,0:T(8,128)(2,1)}, f32[128,576]{1,0:T(8,128)S(1)}) custom-call(bf16[512,2048]{1,0:T(8,128)(2,1)S(1)} %get-tuple-element.24.weight_ref, bf16[512,2048]{1,0:T(8,128)(2,1)S(1)} %get-tuple-element.25.dscore_ref, bf16[576,2048]{1,0:T(8,128)(2,1)S(1)} %get-tuple-element.19.cat_ref, ...), custom_call_target="tpu_custom_call" | custom-call | flops 1887436800 | bytes 4718592 | tf_op jit(solution)/shard_map/dquery/pallas_call | solution.py:286
  42.6 0.0 collective-permute-done.5
  42.7 0.0 collective-permute-done.4
  42.7 0.1 add_convert_fusion.2
  42.7 0.1 collective-permute-start.6
  42.9 1.4 %collective-permute-done.6 = bf16[128,576]{1,0:T(8,128)(2,1)S(1)} collective-permute-done((bf16[128,576]{1,0:T(8,128)(2,1)S(1)}, bf16[128,576]{1,0:T(8,128)(2,1)S(1)}, u32[]{:S(2)}, u32[]{:S(2)}) %collective-permute-start.6) | collective-permute-done | bytes 147488 | tf_op jit(solution)/shard_map/ppermute | solution.py:217
  44.3 0.0 copy-start.3
  44.3 2.6 %collective-permute-start.7 = (bf16[128,576]{1,0:T(8,128)(2,1)S(1)}, bf16[128,576]{1,0:T(8,128)(2,1)S(1)}, u32[]{:S(2)}, u32[]{:S(2)}) collective-permute-start(bf16[128,576]{1,0:T(8,128)(2,1)S(1)} %add_convert_fusion.1.chip_ref), channel_id=1, source_target_pairs={{0,64},{32,224},{64,128},{96,32},{128,192},{160,96},{192,0},{224,1... | collective-permute-start | bytes 442376 | tf_op jit(solution)/shard_map/ppermute | solution.py:223
  46.9 0.6 %collective-permute-start.8 = (bf16[64,576]{1,0:T(8,128)(2,1)S(1)}, bf16[64,576]{1,0:T(8,128)(2,1)S(1)}, u32[]{:S(2)}, u32[]{:S(2)}) collective-permute-start(bf16[64,576]{1,0:T(8,128)(2,1)S(1)} %constant_dynamic-slice_fusion), channel_id=1, source_target_pairs={{0,128},{32,160},{64,192},{96,224},{128,0},{160,32},{192,64},{224,... | collective-permute-start | bytes 221192 | tf_op jit(solution)/shard_map/ppermute | solution.py:223
  47.5 5.5 %collective-permute-done.8.far_ref = bf16[64,576]{1,0:T(8,128)(2,1)S(1)} collective-permute-done((bf16[64,576]{1,0:T(8,128)(2,1)S(1)}, bf16[64,576]{1,0:T(8,128)(2,1)S(1)}, u32[]{:S(2)}, u32[]{:S(2)}) %collective-permute-start.8) | collective-permute-done | bytes 73760 | tf_op jit(solution)/shard_map/ppermute | solution.py:223
  52.9 0.0 copy-start.5
  52.9 0.0 collective-permute-done.7.near_ref
  52.9 0.0 copy-start.4
  53.0 0.9 %collective-permute-start.9 = (bf16[192,576]{1,0:T(8,128)(2,1)S(1)}, bf16[192,576]{1,0:T(8,128)(2,1)S(1)}, u32[]{:S(2)}, u32[]{:S(2)}) collective-permute-start(bf16[192,576]{1,0:T(8,128)(2,1)S(1)} %pad_maximum_fusion), channel_id=1, source_target_pairs={{0,32},{32,0},{64,96},{96,64},{128,160},{160,128},{192,224},{224,1... | collective-permute-start | bytes 663560 | tf_op jit(solution)/shard_map/ppermute | solution.py:217
  53.9 1.1 %collective-permute-done.9.rest_ref = bf16[192,576]{1,0:T(8,128)(2,1)S(1)} collective-permute-done((bf16[192,576]{1,0:T(8,128)(2,1)S(1)}, bf16[192,576]{1,0:T(8,128)(2,1)S(1)}, u32[]{:S(2)}, u32[]{:S(2)}) %collective-permute-start.9) | collective-permute-done | bytes 221216 | tf_op jit(solution)/shard_map/ppermute | solution.py:217
  55.0 0.0 copy-done.3
  55.0 0.0 copy-done.5
  55.0 0.0 copy-done.4
  55.0 0.0 copy-start.6
  55.1 0.7 %copy-done.6 = bf16[192,576]{1,0:T(8,128)(2,1)} copy-done((bf16[192,576]{1,0:T(8,128)(2,1)}, bf16[192,576]{1,0:T(8,128)(2,1)S(1)}, u32[]{:S(2)}) %copy-start.6) | copy-done | bytes 221208
  55.7 2.0 %finish.1 = bf16[576,128]{1,0:T(8,128)(2,1)} custom-call(s32[1]{0:T(128)} %bitcast.4.core_ref, bf16[128,576]{1,0:T(8,128)(2,1)} %copy-done.3, bf16[128,576]{1,0:T(8,128)(2,1)} %copy-done.4, bf16[64,576]{1,0:T(8,128)(2,1)} %copy-done.5, bf16[192,576]{1,0:T(8,128)(2,1)} %copy-done.6, f32[64,128]{1,0:T(8,128)} %copy-done.2), custom_call_target="tpu_custom_call" | custom-call | tf_op jit(solution)/shard_map/finish/pallas_call | solution.py:305
  (10 shorter events, 0.2 us)
Async XLA Ops:
  2.8 34.1 %copy-start.2 = (f32[64,128]{1,0:T(8,128)}, f32[64,128]{1,0:T(8,128)S(1)}, u32[]{:S(2)}) copy-start(f32[64,128]{1,0:T(8,128)S(1)} %get-tuple-element.17.table_ref) | copy-start | bytes 98308
  2.8 14.9 %collective-permute-start = (bf16[128,576]{1,0:T(8,128)(2,1)S(1)}, bf16[128,576]{1,0:T(8,128)(2,1)S(1)}, u32[]{:S(2)}, u32[]{:S(2)}) collective-permute-start(bf16[128,576]{1,0:T(8,128)(2,1)S(1)} %get-tuple-element.16.keys_ref), channel_id=1, source_target_pairs={{0,1},{1,2},{2,3},{3,4},{4,5},{5,6},{6,7},{7,8},{8,9},{9,10},{10,1... | collective-permute-start | bytes 442376 | tf_op jit(solution)/shard_map/ppermute | solution.py:210
  6.6 11.1 %collective-permute-start.1 = (bf16[64,576]{1,0:T(8,128)(2,1)S(1)}, bf16[64,576]{1,0:T(8,128)(2,1)S(1)}, u32[]{:S(2)}, u32[]{:S(2)}) collective-permute-start(bf16[64,576]{1,0:T(8,128)(2,1)S(1)} %get-tuple-element.21), channel_id=1, source_target_pairs={{0,3},{1,4},{2,5},{3,6},{4,7},{5,8},{6,9},{7,10},{8,11},{9,12},{10... | collective-permute-start | bytes 221192 | tf_op jit(solution)/shard_map/ppermute | solution.py:210
  9.4 1.7 %copy-start = (bf16[128,16,576]{0,2,1:T(8,128)(2,1)S(1)}, bf16[128,16,576]{0,2,1:T(8,128)(2,1)}, u32[]{:S(2)}) copy-start(bf16[128,16,576]{0,2,1:T(8,128)(2,1)} %param.8) | copy-start | bytes 7077892
  11.1 1.6 %copy-start.1 = (bf16[128,16,512]{2,1,0:T(8,128)(2,1)S(1)}, bf16[128,16,512]{2,1,0:T(8,128)(2,1)}, u32[]{:S(2)}) copy-start(bf16[128,16,512]{2,1,0:T(8,128)(2,1)} %param.10) | copy-start | bytes 6291460
  12.6 4.8 %copy-start.7 = (s32[1,3]{1,0:T(1,128)S(1)}, s32[1,3]{1,0:T(1,128)}, u32[]{:S(2)}) copy-start(s32[1,3]{1,0:T(1,128)} %anc_ref.1) | copy-start | bytes 40
  17.7 1.6 %collective-permute-start.2 = (bf16[192,576]{1,0:T(8,128)(2,1)S(1)}, bf16[192,576]{1,0:T(8,128)(2,1)S(1)}, u32[]{:S(2)}, u32[]{:S(2)}) collective-permute-start(bf16[192,576]{1,0:T(8,128)(2,1)S(1)} %constant_dynamic-update-slice_fusion.mine_ref), channel_id=1, source_target_pairs={{0,32},{32,0},{64,96},{96,64},{128,160},{160,128},{192,224},{224,1... | collective-permute-start | bytes 663560 | tf_op jit(solution)/shard_map/ppermute | solution.py:217
  28.2 1.6 %collective-permute-start.3 = (bf16[192,576]{1,0:T(8,128)(2,1)S(1)}, bf16[192,576]{1,0:T(8,128)(2,1)S(1)}, u32[]{:S(2)}, u32[]{:S(2)}) collective-permute-start(bf16[192,576]{1,0:T(8,128)(2,1)S(1)} %get-tuple-element.29), channel_id=1, source_target_pairs={{0,32},{32,0},{64,96},{96,64},{128,160},{160,128},{192,224},{224,1... | collective-permute-start | bytes 663560 | tf_op jit(solution)/shard_map/ppermute | solution.py:217
  29.9 12.7 %collective-permute-start.4 = (bf16[128,576]{1,0:T(8,128)(2,1)S(1)}, bf16[128,576]{1,0:T(8,128)(2,1)S(1)}, u32[]{:S(2)}, u32[]{:S(2)}) collective-permute-start(bf16[128,576]{1,0:T(8,128)(2,1)S(1)} %slice.8), channel_id=1, source_target_pairs={{0,31},{1,0},{2,1},{3,2},{4,3},{5,4},{6,5},{7,6},{8,7},{9,8},{10,9... | collective-permute-start | bytes 442376 | tf_op jit(solution)/shard_map/ppermute | solution.py:210
  34.8 7.9 %collective-permute-start.5 = (bf16[64,576]{1,0:T(8,128)(2,1)S(1)}, bf16[64,576]{1,0:T(8,128)(2,1)S(1)}, u32[]{:S(2)}, u32[]{:S(2)}) collective-permute-start(bf16[64,576]{1,0:T(8,128)(2,1)S(1)} %slice.9), channel_id=1, source_target_pairs={{0,29},{1,30},{2,31},{3,0},{4,1},{5,2},{6,3},{7,4},{8,5},{9,6},{10... | collective-permute-start | bytes 221192 | tf_op jit(solution)/shard_map/ppermute | solution.py:210
  42.7 1.5 %collective-permute-start.6 = (bf16[128,576]{1,0:T(8,128)(2,1)S(1)}, bf16[128,576]{1,0:T(8,128)(2,1)S(1)}, u32[]{:S(2)}, u32[]{:S(2)}) collective-permute-start(bf16[128,576]{1,0:T(8,128)(2,1)S(1)} %add_convert_fusion.2), channel_id=1, source_target_pairs={{0,32},{32,0},{64,96},{96,64},{128,160},{160,128},{192,224},{224,1... | collective-permute-start | bytes 442376 | tf_op jit(solution)/shard_map/ppermute | solution.py:217
  44.3 10.8 %copy-start.3 = (bf16[128,576]{1,0:T(8,128)(2,1)}, bf16[128,576]{1,0:T(8,128)(2,1)S(1)}, u32[]{:S(2)}) copy-start(bf16[128,576]{1,0:T(8,128)(2,1)S(1)} %add_convert_fusion.1.chip_ref) | copy-start | bytes 442372
  44.3 8.7 %collective-permute-start.7 = (bf16[128,576]{1,0:T(8,128)(2,1)S(1)}, bf16[128,576]{1,0:T(8,128)(2,1)S(1)}, u32[]{:S(2)}, u32[]{:S(2)}) collective-permute-start(bf16[128,576]{1,0:T(8,128)(2,1)S(1)} %add_convert_fusion.1.chip_ref), channel_id=1, source_target_pairs={{0,64},{32,224},{64,128},{96,32},{128,192},{160,96},{192,0},{224,1... | collective-permute-start | bytes 442376 | tf_op jit(solution)/shard_map/ppermute | solution.py:223
  46.9 6.1 %collective-permute-start.8 = (bf16[64,576]{1,0:T(8,128)(2,1)S(1)}, bf16[64,576]{1,0:T(8,128)(2,1)S(1)}, u32[]{:S(2)}, u32[]{:S(2)}) collective-permute-start(bf16[64,576]{1,0:T(8,128)(2,1)S(1)} %constant_dynamic-slice_fusion), channel_id=1, source_target_pairs={{0,128},{32,160},{64,192},{96,224},{128,0},{160,32},{192,64},{224,... | collective-permute-start | bytes 221192 | tf_op jit(solution)/shard_map/ppermute | solution.py:223
  52.9 2.1 %copy-start.5 = (bf16[64,576]{1,0:T(8,128)(2,1)}, bf16[64,576]{1,0:T(8,128)(2,1)S(1)}, u32[]{:S(2)}) copy-start(bf16[64,576]{1,0:T(8,128)(2,1)S(1)} %collective-permute-done.8.far_ref) | copy-start | bytes 221188
  52.9 2.1 %copy-start.4 = (bf16[128,576]{1,0:T(8,128)(2,1)}, bf16[128,576]{1,0:T(8,128)(2,1)S(1)}, u32[]{:S(2)}) copy-start(bf16[128,576]{1,0:T(8,128)(2,1)S(1)} %collective-permute-done.7.near_ref) | copy-start | bytes 442372
  53.0 2.1 %collective-permute-start.9 = (bf16[192,576]{1,0:T(8,128)(2,1)S(1)}, bf16[192,576]{1,0:T(8,128)(2,1)S(1)}, u32[]{:S(2)}, u32[]{:S(2)}) collective-permute-start(bf16[192,576]{1,0:T(8,128)(2,1)S(1)} %pad_maximum_fusion), channel_id=1, source_target_pairs={{0,32},{32,0},{64,96},{96,64},{128,160},{160,128},{192,224},{224,1... | collective-permute-start | bytes 663560 | tf_op jit(solution)/shard_map/ppermute | solution.py:217
  55.0 0.7 %copy-start.6 = (bf16[192,576]{1,0:T(8,128)(2,1)}, bf16[192,576]{1,0:T(8,128)(2,1)S(1)}, u32[]{:S(2)}) copy-start(bf16[192,576]{1,0:T(8,128)(2,1)S(1)} %collective-permute-done.9.rest_ref) | copy-start | bytes 663556

commit v2 on v1

v2 whole, which is shorter than its diff:
```python
import functools

import jax
import jax.numpy as jnp
import numpy as np
from jax import lax
from jax.experimental import pallas as pl
from jax.experimental.pallas import tpu as pltpu
from jax.sharding import PartitionSpec as P

LAT = 512
ROPE = 64
BS = 128
WIDTH = LAT + ROPE
HALF = BS // 2
SIDE = BS + HALF
REMOTE = 2 * SIDE
KEYS = BS + REMOTE
TILE = 256
STEP = 1024

score_scale = 192.0 ** (-0.5)
rope_base = 10000.0
exponent_scale = score_scale * float(np.log2(np.e))
MASKED = -1e30

BF = jnp.bfloat16
F32 = jnp.float32
NT = (((1,), (1,)), ((), ()))
NN = (((1,), (0,)), ((), ()))
TN = (((0,), (0,)), ((), ()))


def dot(a, b, dims):
    return lax.dot_general(a, b, dims, preferred_element_type=F32)


def vmem(shape, dtype):
    return pltpu.VMEM(shape, dtype)


def in_vmem(x):
    return pltpu.with_memory_space_constraint(x, pltpu.VMEM)


def in_hbm(x):
    return pltpu.with_memory_space_constraint(x, pltpu.HBM)


def whole():
    return pl.BlockSpec(memory_space=pltpu.VMEM)


def scalars():
    return pl.BlockSpec(memory_space=pltpu.SMEM)


def turn(values, table):
    half = ROPE // 2
    first, second, cosine, sine = values[:half], values[half:], table[:half], table[half:]
    return jnp.concatenate([first * cosine - second * sine, first * sine + second * cosine], axis=0)


def turn_back(values, table):
    half = ROPE // 2
    first, second, cosine, sine = values[:half], values[half:], table[:half], table[half:]
    return jnp.concatenate([first * cosine + second * sine, second * cosine - first * sine], axis=0)


def this_core():
    return lax.rem(lax.axis_index("tp"), 2)


def keys_kernel(anc_ref, parents_ref, freq_ref, latent_ref, keys_ref, half_ref, table_ref, closure_ref):
    row = lax.broadcasted_iota(jnp.int32, (BS, BS), 0)
    col = lax.broadcasted_iota(jnp.int32, (BS, BS), 1)
    linked = (row == parents_ref[...]) | (row == col)
    closure = jnp.where(linked, 1.0, 0.0).astype(BF)
    for _ in range((BS - 1).bit_length()):
        reach = jnp.minimum(dot(closure, closure, NN), 1.0)
        closure = reach.astype(BF)
    closure_ref[...] = reach
    depth = jnp.sum(reach, axis=0, keepdims=True) - 1.0
    count = 0
    for k in range(anc_ref.shape[1]):
        count = count + (anc_ref[0, k] >= 0).astype(jnp.int32)
    angles = (depth + (BS * count).astype(F32)) * freq_ref[...]
    table = jnp.concatenate([jnp.cos(angles), jnp.sin(angles)], axis=0)
    table_ref[...] = table
    for lo in range(0, LAT, BS):
        keys_ref[:, lo : lo + BS] = latent_ref[lo : lo + BS, :].T
    turned = turn(latent_ref[LAT:, :].astype(F32), table)
    keys_ref[:, LAT:] = turned.T.astype(BF)
    half_ref[...] = keys_ref[own_half(), :]


def own_kernel(heads, query_hbm, grad_hbm, keys_ref, table_ref, closure_ref, cat_ref, sorted_ref, score_ref, slope_ref,
               query_ref, grad_ref, sems):
    pieces = heads * BS // TILE
    pair = TILE // BS * WIDTH
    grad_copies, query_copies = [], []
    for t in range(pieces):
        at = pl.ds(t * TILE, TILE)
        grad_copies.append(pltpu.make_async_copy(grad_hbm.at[at], grad_ref.at[at], sems.at[t]))
    for t in range(pieces):
        at = pl.ds(t * pair, pair)
        query_copies.append(pltpu.make_async_copy(query_hbm.at[at], query_ref.at[at], sems.at[pieces + t]))
    for copy in grad_copies + query_copies:
        copy.start()
    rows = TILE // heads
    row = lax.broadcasted_iota(jnp.int32, (TILE, TILE), 0)
    col = lax.broadcasted_iota(jnp.int32, (TILE, TILE), 1)
    order = jnp.where(col == (row % rows) * heads + row // rows, 1.0, 0.0).astype(BF)
    for t in range(pieces):
        grad_copies[t].wait()
        chunk = dot(order, grad_ref[t * TILE : (t + 1) * TILE, :], NN).astype(BF)
        for h in range(heads):
            sorted_ref[pl.ds(h * BS + t * rows, rows), :] = chunk[h * rows : (h + 1) * rows]
    table = table_ref[...]
    seen = jnp.concatenate([closure_ref[...]] * (TILE // BS), axis=1) > 0.5
    for t in range(pieces):
        query_copies[t].wait()
        here = pl.ds(t * TILE, TILE)
        for k in range(TILE // BS):
            lanes = pl.ds(t * TILE + k * BS, BS)
            at = t * pair + k * WIDTH
            cat_ref[:LAT, lanes] = query_ref[pl.ds(at, LAT), :]
            cat_ref[LAT:, lanes] = turn(query_ref[pl.ds(at + LAT, ROPE), :].astype(F32), table).astype(BF)
        score = dot(keys_ref[...], cat_ref[:, here], NN)
        score_ref[:, here] = jnp.where(seen, score * exponent_scale, MASKED)
        slope_ref[:, here] = dot(keys_ref[:, :LAT], sorted_ref[here, :], NT)


def key_grads(rows, weight_ref, dscore_ref, cat_ref, sorted_ref):
    turned = dot(dscore_ref[rows, :], cat_ref[...], NT) * score_scale
    plain = dot(weight_ref[rows, :], sorted_ref[...], NN)
    return turned[:, :LAT] + plain, turned[:, LAT:]


def mine_kernel(cat_ref, sorted_ref, mine_ref, score_ref, slope_ref):
    for lo in range(0, cat_ref.shape[1], TILE):
        here = pl.ds(lo, TILE)
        score_ref[:, here] = dot(mine_ref[...], cat_ref[:, here], NN) * exponent_scale
        slope_ref[:, here] = dot(mine_ref[:, :LAT], sorted_ref[here, :], NT)


def main_kernel(anc_ref, cat_ref, sorted_ref, other_ref, own_score, own_slope, mine_score, mine_slope,
                weight_ref, dscore_ref, gother_ref, score_ref, slope_ref):
    tiles = cat_ref.shape[1] // TILE
    core, block = this_core(), lax.axis_index("cp")

    def bias(offset):
        wanted = block - offset
        listed = jnp.int32(0)
        for k in range(anc_ref.shape[1]):
            listed = jnp.where(anc_ref[0, k] == wanted, 1, listed)
        return jnp.where((wanted >= 0) & (listed > 0), 0.0, MASKED).astype(F32)

    whole_mine, whole_other, part = bias(1 + core), bias(2 - core), bias(3)

    def products(t):
        here = pl.ds(t * TILE, TILE)
        score_ref[t % 2] = dot(other_ref[...], cat_ref[:, here], NN) * exponent_scale
        slope_ref[t % 2] = dot(other_ref[:, :LAT], sorted_ref[here, :], NT)

    def softmax(t):
        here = pl.ds(t * TILE, TILE)
        places = (
            (own_score[:, here], own_slope[:, here], 0.0),
            (mine_score[:BS, here], mine_slope[:BS, here], whole_mine),
            (mine_score[BS:, here], mine_slope[BS:, here], part),
            (score_ref[t % 2, :BS], slope_ref[t % 2, :BS], whole_other),
            (score_ref[t % 2, BS:], slope_ref[t % 2, BS:], part),
        )
        largest = functools.reduce(jnp.maximum, [jnp.max(s, axis=0, keepdims=True) + b for s, _, b in places])
        expos = [jnp.exp2(s - (largest - b)) for s, _, b in places]
        inverse = 1.0 / sum(jnp.sum(e, axis=0, keepdims=True) for e in expos)
        delta = sum(jnp.sum(e * l, axis=0, keepdims=True) for e, (_, l, _) in zip(expos, places)) * inverse
        at = 0
        for e, (_, l, _) in zip(expos, places):
            rows = pl.ds(at, e.shape[0])
            weight = e * inverse
            weight_ref[rows, here] = weight.astype(BF)
            dscore_ref[rows, here] = (weight * (l - delta)).astype(BF)
            at += e.shape[0]

    products(0)
    for t in range(tiles):
        if t + 1 < tiles:
            products(t + 1)
        softmax(t)
    lead, tail = key_grads(pl.ds(BS + SIDE, SIDE), weight_ref, dscore_ref, cat_ref, sorted_ref)
    gother_ref[:, :LAT] = lead.astype(BF)
    gother_ref[:, LAT:] = tail.astype(BF)


def grads_kernel(weight_ref, dscore_ref, cat_ref, sorted_ref, gmine_ref):
    lead, tail = key_grads(pl.ds(BS, SIDE), weight_ref, dscore_ref, cat_ref, sorted_ref)
    gmine_ref[:, :LAT] = lead
    gmine_ref[:, LAT:] = tail


def query_kernel(weight_ref, dscore_ref, cat_ref, sorted_ref, keys_ref, mine_ref, other_ref, table_ref,
                 dquery_ref, gown_ref, every_ref, turned_ref):
    t = pl.program_id(0)

    @pl.when(t == 0)
    def _():
        every_ref[:BS, :] = keys_ref[...]
        every_ref[BS : BS + SIDE, :] = mine_ref[...]
        every_ref[BS + SIDE :, :] = other_ref[...]
        for lo in range(0, KEYS, BS):
            turned_ref[:, lo : lo + BS] = every_ref[lo : lo + BS, :].T
        lead, tail = key_grads(pl.ds(0, BS), weight_ref, dscore_ref, cat_ref, sorted_ref)
        gown_ref[:, :LAT] = lead
        gown_ref[:, LAT:] = tail

    dscore = dscore_ref[:, pl.ds(pl.multiple_of(t * STEP, STEP), STEP)]
    grads = dot(turned_ref[...], dscore, NN) * score_scale
    for k in range(STEP // BS):
        part = grads[:, k * BS : (k + 1) * BS]
        dquery_ref[k, :LAT, :] = part[:LAT].astype(BF)
        dquery_ref[k, LAT:, :] = turn_back(part[LAT:], table_ref[...]).astype(BF)


def own_half():
    return pl.ds(pl.multiple_of(this_core() * HALF, HALF), HALF)


def other_half():
    return pl.ds(pl.multiple_of((1 - this_core()) * HALF, HALF), HALF)


def device_kernel(gown_ref, back_ref, half_ref, out_ref, sum_ref):
    sum_ref[...] = gown_ref[...] + back_ref[...].astype(F32)
    sum_ref[own_half(), :] += half_ref[...].astype(F32)
    out_ref[...] = sum_ref[...].astype(BF)


def chip_kernel(device_ref, other_ref, chip_ref, half_ref):
    chip_ref[...] = (device_ref[...].astype(F32) + other_ref[...].astype(F32)).astype(BF)
    half_ref[...] = chip_ref[own_half(), :]


def finish_kernel(chip_ref, near_ref, far_ref, rest_ref, table_ref, out_ref, sum_ref):
    sum_ref[...] = chip_ref[...].astype(F32)
    sum_ref[own_half(), :] += far_ref[...].astype(F32)
    sum_ref[other_half(), :] += rest_ref[BS:, :].astype(F32)
    sum_ref[...] += near_ref[...].astype(F32) + rest_ref[:BS, :].astype(F32)
    for lo in range(0, LAT, BS):
        out_ref[lo : lo + BS, :] = sum_ref[:, lo : lo + BS].T.astype(BF)
    out_ref[LAT:, :] = turn_back(sum_ref[:, LAT:].T, table_ref[...]).astype(BF)


def by_core(block, even, odd):
    tp, cp = lax.axis_size("tp"), lax.axis_size("cp")
    route = []
    for t in range(tp):
        step = odd if t % 2 else even
        for c in range(cp):
            if 0 <= c + step < cp or WRAP:
                route.append((t * cp + c, t * cp + (c + step) % cp))
    return lax.ppermute(block, ("tp", "cp"), route)


WRAP = True


def other_core(block):
    return lax.ppermute(block, "tp", [(t, t ^ 1) for t in range(lax.axis_size("tp"))])


def along_x(block, even, odd):
    tp = lax.axis_size("tp")
    route = [(t, (t + 2 * (odd if t % 2 else even)) % tp) for t in range(tp)]
    return lax.ppermute(block, "tp", route)


def on_device(query, latent, grad_out, ancestors, parents):
    rows, heads, _ = query.shape
    total = rows * heads
    half = ROPE // 2
    lane_freq = rope_base ** (-2.0 * np.arange(half, dtype=np.float64) / ROPE)
    freq = jnp.asarray(np.tile(lane_freq[:, None], (1, BS)), dtype=F32)
    params = pltpu.CompilerParams(vmem_limit_bytes=16 * 2**20)
    outside = pl.BlockSpec(memory_space=pltpu.HBM)

    def call(kernel, name, ins, outs, flops=0, **more):
        return pl.pallas_call(
            kernel,
            in_specs=ins,
            out_specs=[whole()] * len(outs),
            out_shape=[vmem(*o) for o in outs],
            cost_estimate=pl.CostEstimate(flops=flops, bytes_accessed=4 * total * WIDTH, transcendentals=0),
            compiler_params=params,
            name=name,
            **more,
        )

    keys, keys_half, table, closure = call(
        keys_kernel,
        "keys",
        [scalars(), whole(), whole(), whole()],
        [((BS, WIDTH), BF), ((HALF, WIDTH), BF), ((ROPE, BS), F32), ((BS, BS), F32)],
    )(*map(in_hbm, (ancestors, parents.reshape(1, BS), freq, latent.T)))

    fetched = by_core(keys, 1, 2)
    fetched_half = by_core(keys_half, 3, 3)

    cat, ordered, own_score, own_slope = call(
        functools.partial(own_kernel, heads),
        "own",
        [outside] * 2 + [whole()] * 3,
        [((WIDTH, total), BF), ((total, LAT), BF), ((BS, total), F32), ((BS, total), F32)],
        flops=2 * total * BS * 1800,
        scratch_shapes=[
            pltpu.VMEM((heads * WIDTH, rows), BF),
            pltpu.VMEM((total, LAT), BF),
            pltpu.SemaphoreType.DMA((2 * total // TILE,)),
        ],
    )(in_hbm(query.transpose(1, 2, 0).reshape(heads * WIDTH, rows)), in_hbm(grad_out.reshape(total, LAT)),
      keys, table, closure)

    mine, cat = lax.optimization_barrier((jnp.concatenate([fetched, fetched_half]), cat))
    other = other_core(mine)
    mine_score, mine_slope = call(
        mine_kernel, "mine", [whole()] * 3, [((SIDE, total), F32), ((SIDE, total), F32)], flops=2 * total * SIDE * 1280
    )(cat, ordered, mine)

    weight, dscore, gother = call(
        main_kernel,
        "main",
        [scalars()] + [whole()] * 7,
        [((KEYS, total), BF), ((KEYS, total), BF), ((SIDE, WIDTH), BF)],
        flops=2 * total * SIDE * 2560,
        scratch_shapes=[pltpu.VMEM((2, SIDE, TILE), F32), pltpu.VMEM((2, SIDE, TILE), F32)],
    )(in_hbm(ancestors), cat, ordered, other, own_score, own_slope, mine_score, mine_slope)

    gother = other_core(gother)
    (gmine,) = call(
        grads_kernel, "grads", [whole()] * 4, [((SIDE, WIDTH), F32)], flops=2 * total * SIDE * 1280
    )(weight, dscore, cat, ordered)
    gmine = (gmine + gother.astype(F32)).astype(BF)
    back = by_core(gmine[:BS], -1, -2)
    back_half = by_core(gmine[BS:], -3, -3)

    dquery, gown = pl.pallas_call(
        query_kernel,
        grid=(total // STEP,),
        in_specs=[whole()] * 8,
        out_specs=[pl.BlockSpec((STEP // BS, WIDTH, BS), lambda t: (t, 0, 0)), whole()],
        out_shape=[jax.ShapeDtypeStruct((heads, WIDTH, rows), BF), vmem((BS, WIDTH), F32)],
        scratch_shapes=[pltpu.VMEM((KEYS, WIDTH), BF), pltpu.VMEM((WIDTH, KEYS), BF)],
        cost_estimate=pl.CostEstimate(flops=2 * total * KEYS * 900, bytes_accessed=4 * total * WIDTH, transcendentals=0),
        compiler_params=params,
        name="dquery",
    )(weight, dscore, cat, ordered, keys, mine, other, table)

    (device_sum,) = call(
        device_kernel,
        "device",
        [whole()] * 3,
        [((BS, WIDTH), BF)],
        scratch_shapes=[pltpu.VMEM((BS, WIDTH), F32)],
    )(gown, back, back_half)
    chip_sum, chip_half = call(
        chip_kernel, "chip", [whole()] * 2, [((BS, WIDTH), BF), ((HALF, WIDTH), BF)]
    )(device_sum, other_core(device_sum))
    near = along_x(chip_sum, 1, -1)
    far = along_x(chip_half, 2, 2)
    rest = other_core(jnp.concatenate([near, far]))
    d_latent = pl.pallas_call(
        finish_kernel,
        in_specs=[whole()] * 5,
        out_specs=whole(),
        out_shape=jax.ShapeDtypeStruct((WIDTH, BS), BF),
        scratch_shapes=[pltpu.VMEM((BS, WIDTH), F32)],
        compiler_params=params,
        name="finish",
    )(*map(in_vmem, (chip_sum, near, far, rest, table)))
    return (dquery.transpose(2, 0, 1), d_latent.T)


def solution(mesh):
    placed = (P("cp", "tp", None), P("cp", None), P("cp", "tp", None), P("cp", None), P("cp"))
    return jax.shard_map(
        on_device,
        mesh=mesh,
        in_specs=placed,
        out_specs=(P("cp", "tp", None), P("cp", None)),
        check_vma=False,
    )
```

time: 57.9 us -> 48.7 us (0.84)
  local copies, waits for them, and re-layouts: 4.02 us -> 0.02 us
  Pallas kernels: 23.6 us -> 20.5 us
  waiting for transfers between devices: 10.4 us -> 8.17 us
  starting transfers between devices: 17.8 us -> 19.1 us
  other arithmetic: 1.03 us -> 0.1 us
    unnamed x17 -> x0, local copies, waits for them, and re-layouts: 3.97 us -> none
    ppermute x4, starting transfers between devices: 1.77 us -> 5.05 us  [other_core(): lax.ppermute(block, 'tp', [(t, t ^ 1) for t in range(lax.axis_size('tp'))])]
    pallas_call x5 -> x9, Pallas kernels: 23.6 us -> 20.5 us  [the longest x1 5.91 us: on_device(): call(functools.partial(own_kernel, heads), 'own', [outside] * 2 + [whole(...]
    ppermute x4, waiting for transfers between devices: 4.95 us -> 2.17 us  [other_core(): lax.ppermute(block, 'tp', [(t, t ^ 1) for t in range(lax.axis_size('tp'))])]
    ppermute x4, starting transfers between devices: 12.9 us -> 11 us  [by_core(): return lax.ppermute(block, ('tp', 'cp'), route)]
    ge x1 -> x0, other arithmetic: 0.66 us -> none  [on_device(): ids[:, None] >= 0]
  transfers between devices with their start and end apart: 10 -> 10, of which waited for: 5 -> 5; matrix products, arithmetic and copies ran while one was open for 2% -> 0% of each run, Pallas kernels for 18% -> 26%
where the time goes in v2:
time: 48.7 us; the launch traced here: 48.6 us
  Pallas kernels  20.5 us (42%)
  starting transfers between devices  19.1 us (39%)
  waiting for transfers between devices  8.17 us (17%)
  between operations  0.72 us (1%)
    ppermute x4, starting transfers between devices, by_core(): return lax.ppermute(block, ('tp', 'cp'), route)  11 us
    pallas_call x1, Pallas kernels, on_device(): call(functools.partial(own_kernel, heads), 'own', [outside] * 2 + [whole(...  5.91 us
    ppermute x2, waiting for transfers between devices, along_x(): return lax.ppermute(block, 'tp', route)  5.45 us
    ppermute x4, starting transfers between devices, other_core(): lax.ppermute(block, 'tp', [(t, t ^ 1) for t in range(lax.axis_size('tp'))])  5.05 us
    pallas_call x1, Pallas kernels, on_device(): call(main_kernel, 'main', [scalars()] + [whole()] * 7, [((KEYS, total), B...  4.79 us
    pallas_call x1, Pallas kernels, on_device(): pl.pallas_call(query_kernel, grid=(total // STEP,), in_specs=[whole()] *...  3.82 us
    ppermute x2, starting transfers between devices, along_x(): return lax.ppermute(block, 'tp', route)  3.08 us
    ppermute x4, waiting for transfers between devices, other_core(): lax.ppermute(block, 'tp', [(t, t ^ 1) for t in range(lax.axis_size('tp'))])  2.17 us
  transfers between devices with their start and end apart: 10, of which 5 were waited for; matrix products, arithmetic and copies ran while one was open for 0% of the time, Pallas kernels for 26%

profile of v2, /device:TPU:1, one launch (start us, length us, event | category | flops | bytes accessed | tf_op | source)
XLA Modules:
  0.0 48.6 jit_solution(1569131143114380103)
XLA Ops:
  0.6 2.1 %keys.1 = (bf16[128,576]{1,0:T(8,128)(2,1)S(1)}, bf16[64,576]{1,0:T(8,128)(2,1)S(1)}, f32[64,128]{1,0:T(8,128)S(1)}, f32[128,128]{1,0:T(8,128)S(1)}) custom-call(s32[1,3]{1,0:T(1,128)} %anc_ref.3, s32[1,128]{1,0:T(1,128)} %bitcast.12, f32[32,128]{1,0:T(8,128)} %constant.2.clone.freq_ref, bf16[576,128]{1,0:T(8,128)(2,1)} %bitcast.11), custom_call_target="tpu_custom_call" | custom-call | bytes 4718592 | tf_op jit(solution)/shard_map/keys/pallas_call | solution.py:300
  2.8 3.8 %collective-permute-start = (bf16[128,576]{1,0:T(8,128)(2,1)S(1)}, bf16[128,576]{1,0:T(8,128)(2,1)S(1)}, u32[]{:S(2)}, u32[]{:S(2)}) collective-permute-start(bf16[128,576]{1,0:T(8,128)(2,1)S(1)} %get-tuple-element.21.keys_ref), channel_id=1, source_target_pairs={{0,1},{1,2},{2,3},{3,4},{4,5},{5,6},{6,7},{7,8},{8,9},{9,10},{10,1... | collective-permute-start | bytes 442376 | tf_op jit(solution)/shard_map/ppermute | solution.py:263
  6.6 2.1 %collective-permute-start.1 = (bf16[64,576]{1,0:T(8,128)(2,1)S(1)}, bf16[64,576]{1,0:T(8,128)(2,1)S(1)}, u32[]{:S(2)}, u32[]{:S(2)}) collective-permute-start(bf16[64,576]{1,0:T(8,128)(2,1)S(1)} %get-tuple-element.22), channel_id=1, source_target_pairs={{0,3},{1,4},{2,5},{3,6},{4,7},{5,8},{6,9},{7,10},{8,11},{9,12},{10... | collective-permute-start | bytes 221192 | tf_op jit(solution)/shard_map/ppermute | solution.py:263
  8.7 5.9 %own.1 = (bf16[576,2048]{1,0:T(8,128)(2,1)S(1)}, bf16[2048,512]{1,0:T(8,128)(2,1)S(1)}, f32[128,2048]{1,0:T(8,128)S(1)}, f32[128,2048]{1,0:T(8,128)S(1)}) custom-call(bf16[9216,128]{1,0:T(8,128)(2,1)} %bitcast.8, bf16[2048,512]{1,0:T(8,128)(2,1)} %bitcast.9, bf16[128,576]{1,0:T(8,128)(2,1)S(1)} %get-tuple-element.21.keys_ref, ...), custom_call_target="tpu_custom_call" | custom-call | flops 943718400 | bytes 4718592 | tf_op jit(solution)/shard_map/own/pallas_call | solution.py:310
  14.6 0.3 collective-permute-done.1
  14.9 0.2 collective-permute-done
  15.2 2.6 %collective-permute-start.2 = (bf16[192,576]{1,0:T(8,128)(2,1)S(1)}, bf16[192,576]{1,0:T(8,128)(2,1)S(1)}, u32[]{:S(2)}, u32[]{:S(2)}) collective-permute-start(bf16[192,576]{1,0:T(8,128)(2,1)S(1)} %pad_maximum_fusion.mine_ref), channel_id=1, source_target_pairs={{0,32},{32,0},{64,96},{96,64},{128,160},{160,128},{192,224},{224,1... | collective-permute-start | bytes 663560 | tf_op jit(solution)/shard_map/ppermute | solution.py:270
  17.8 1.3 %mine.1 = (f32[192,2048]{1,0:T(8,128)S(1)}, f32[192,2048]{1,0:T(8,128)S(1)}) custom-call(bf16[576,2048]{1,0:T(8,128)(2,1)S(1)} %get-tuple-element.26.cat_ref, bf16[2048,512]{1,0:T(8,128)(2,1)S(1)} %get-tuple-element.27.sorted_ref, bf16[192,576]{1,0:T(8,128)(2,1)S(1)} %pad_maximum_fusion.mine_ref), custom_call_target="tpu_custom_call" | custom-call | flops 1006632960 | bytes 4718592 | tf_op jit(solution)/shard_map/mine/pallas_call | solution.py:326
  19.1 0.0 collective-permute-done.2.other_ref
  19.1 4.8 %main.1 = (bf16[512,2048]{1,0:T(8,128)(2,1)S(1)}, bf16[512,2048]{1,0:T(8,128)(2,1)S(1)}, bf16[192,576]{1,0:T(8,128)(2,1)S(1)}) custom-call(s32[1,3]{1,0:T(1,128)} %anc_ref.3, bf16[576,2048]{1,0:T(8,128)(2,1)S(1)} %get-tuple-element.26.cat_ref, bf16[2048,512]{1,0:T(8,128)(2,1)S(1)} %get-tuple-element.27.sorted_ref, ...), custom_call_target="tpu_custom_call" | custom-call | flops 2013265920 | bytes 4718592 | tf_op jit(solution)/shard_map/main/pallas_call | solution.py:330
  23.9 0.2 collective-permute-start.3
  24.2 1.4 %grads.1 = f32[192,576]{1,0:T(8,128)S(1)} custom-call(bf16[512,2048]{1,0:T(8,128)(2,1)S(1)} %get-tuple-element.33.weight_ref, bf16[512,2048]{1,0:T(8,128)(2,1)S(1)} %get-tuple-element.34.dscore_ref, bf16[576,2048]{1,0:T(8,128)(2,1)S(1)} %get-tuple-element.26.cat_ref, bf16[2048,512]{1,0:T(8,128)(2,1)S(1)} %get-tuple-element.27.sorted_ref), custom_call_target="tpu_custom_call" | custom-call | flops 1006632960 | bytes 4718592 | tf_op jit(solution)/shard_map/grads/pallas_call | solution.py:340
  25.6 0.0 collective-permute-done.3
  25.7 1.7 %collective-permute-start.5 = (bf16[64,576]{1,0:T(8,128)(2,1)S(1)}, bf16[64,576]{1,0:T(8,128)(2,1)S(1)}, u32[]{:S(2)}, u32[]{:S(2)}) collective-permute-start(bf16[64,576]{1,0:T(8,128)(2,1)S(1)} %slice.9), channel_id=1, source_target_pairs={{0,29},{1,30},{2,31},{3,0},{4,1},{5,2},{6,3},{7,4},{8,5},{9,6},{10... | collective-permute-start | bytes 221192 | tf_op jit(solution)/shard_map/ppermute | solution.py:263
  27.4 3.3 %collective-permute-start.4 = (bf16[128,576]{1,0:T(8,128)(2,1)S(1)}, bf16[128,576]{1,0:T(8,128)(2,1)S(1)}, u32[]{:S(2)}, u32[]{:S(2)}) collective-permute-start(bf16[128,576]{1,0:T(8,128)(2,1)S(1)} %slice.8), channel_id=1, source_target_pairs={{0,31},{1,0},{2,1},{3,2},{4,3},{5,4},{6,5},{7,6},{8,7},{9,8},{10,9... | collective-permute-start | bytes 442376 | tf_op jit(solution)/shard_map/ppermute | solution.py:263
  30.7 3.8 %dquery.1 = (bf16[16,576,128]{2,1,0:T(8,128)(2,1)}, f32[128,576]{1,0:T(8,128)S(1)}) custom-call(bf16[512,2048]{1,0:T(8,128)(2,1)S(1)} %get-tuple-element.33.weight_ref, bf16[512,2048]{1,0:T(8,128)(2,1)S(1)} %get-tuple-element.34.dscore_ref, bf16[576,2048]{1,0:T(8,128)(2,1)S(1)} %get-tuple-element.26.cat_ref, ...), custom_call_target="tpu_custom_call" | custom-call | flops 1887436800 | bytes 4718592 | tf_op jit(solution)/shard_map/dquery/pallas_call | solution.py:347
  34.5 0.0 collective-permute-done.5.half_ref
  34.5 0.0 collective-permute-done.4.back_ref
  34.6 0.1 device.1.device_ref
  34.7 0.9 %collective-permute-start.6 = (bf16[128,576]{1,0:T(8,128)(2,1)S(1)}, bf16[128,576]{1,0:T(8,128)(2,1)S(1)}, u32[]{:S(2)}, u32[]{:S(2)}) collective-permute-start(bf16[128,576]{1,0:T(8,128)(2,1)S(1)} %device.1.device_ref), channel_id=1, source_target_pairs={{0,32},{32,0},{64,96},{96,64},{128,160},{160,128},{192,224},{224,1... | collective-permute-start | bytes 442376 | tf_op jit(solution)/shard_map/ppermute | solution.py:270
  35.6 1.0 %collective-permute-done.6.other_ref = bf16[128,576]{1,0:T(8,128)(2,1)S(1)} collective-permute-done((bf16[128,576]{1,0:T(8,128)(2,1)S(1)}, bf16[128,576]{1,0:T(8,128)(2,1)S(1)}, u32[]{:S(2)}, u32[]{:S(2)}) %collective-permute-start.6) | collective-permute-done | bytes 147488 | tf_op jit(solution)/shard_map/ppermute | solution.py:270
  36.6 0.1 chip.1
  36.7 2.6 %collective-permute-start.7 = (bf16[128,576]{1,0:T(8,128)(2,1)S(1)}, bf16[128,576]{1,0:T(8,128)(2,1)S(1)}, u32[]{:S(2)}, u32[]{:S(2)}) collective-permute-start(bf16[128,576]{1,0:T(8,128)(2,1)S(1)} %get-tuple-element.38.chip_ref), channel_id=1, source_target_pairs={{0,64},{32,224},{64,128},{96,32},{128,192},{160,96},{192,0},{224,1... | collective-permute-start | bytes 442376 | tf_op jit(solution)/shard_map/ppermute | solution.py:276
  39.2 0.5 %collective-permute-start.8 = (bf16[64,576]{1,0:T(8,128)(2,1)S(1)}, bf16[64,576]{1,0:T(8,128)(2,1)S(1)}, u32[]{:S(2)}, u32[]{:S(2)}) collective-permute-start(bf16[64,576]{1,0:T(8,128)(2,1)S(1)} %get-tuple-element.39), channel_id=1, source_target_pairs={{0,128},{32,160},{64,192},{96,224},{128,0},{160,32},{192,64},{224,... | collective-permute-start | bytes 221192 | tf_op jit(solution)/shard_map/ppermute | solution.py:276
  39.7 5.5 %collective-permute-done.8.far_ref = bf16[64,576]{1,0:T(8,128)(2,1)S(1)} collective-permute-done((bf16[64,576]{1,0:T(8,128)(2,1)S(1)}, bf16[64,576]{1,0:T(8,128)(2,1)S(1)}, u32[]{:S(2)}, u32[]{:S(2)}) %collective-permute-start.8) | collective-permute-done | bytes 73760 | tf_op jit(solution)/shard_map/ppermute | solution.py:276
  45.2 0.0 collective-permute-done.7.near_ref
  45.2 1.3 %collective-permute-start.9 = (bf16[192,576]{1,0:T(8,128)(2,1)S(1)}, bf16[192,576]{1,0:T(8,128)(2,1)S(1)}, u32[]{:S(2)}, u32[]{:S(2)}) collective-permute-start(bf16[192,576]{1,0:T(8,128)(2,1)S(1)} %pad_maximum_fusion.1), channel_id=1, source_target_pairs={{0,32},{32,0},{64,96},{96,64},{128,160},{160,128},{192,224},{224,1... | collective-permute-start | bytes 663560 | tf_op jit(solution)/shard_map/ppermute | solution.py:270
  46.5 1.1 %collective-permute-done.9.rest_ref = bf16[192,576]{1,0:T(8,128)(2,1)S(1)} collective-permute-done((bf16[192,576]{1,0:T(8,128)(2,1)S(1)}, bf16[192,576]{1,0:T(8,128)(2,1)S(1)}, u32[]{:S(2)}, u32[]{:S(2)}) %collective-permute-start.9) | collective-permute-done | bytes 221216 | tf_op jit(solution)/shard_map/ppermute | solution.py:270
  47.6 0.9 %finish.1 = bf16[576,128]{1,0:T(8,128)(2,1)} custom-call(bf16[128,576]{1,0:T(8,128)(2,1)S(1)} %get-tuple-element.38.chip_ref, bf16[128,576]{1,0:T(8,128)(2,1)S(1)} %collective-permute-done.7.near_ref, bf16[64,576]{1,0:T(8,128)(2,1)S(1)} %collective-permute-done.8.far_ref, bf16[192,576]{1,0:T(8,128)(2,1)S(1)} %collective-permute-done.9.rest_ref, ...), custom_call_target="tpu_custom_call" | custom-call | tf_op jit(solution)/shard_map/finish/pallas_call | solution.py:372
  (5 shorter events, 0.1 us)
Async XLA Ops:
  2.8 12.4 %collective-permute-start = (bf16[128,576]{1,0:T(8,128)(2,1)S(1)}, bf16[128,576]{1,0:T(8,128)(2,1)S(1)}, u32[]{:S(2)}, u32[]{:S(2)}) collective-permute-start(bf16[128,576]{1,0:T(8,128)(2,1)S(1)} %get-tuple-element.21.keys_ref), channel_id=1, source_target_pairs={{0,1},{1,2},{2,3},{3,4},{4,5},{5,6},{6,7},{7,8},{8,9},{9,10},{10,1... | collective-permute-start | bytes 442376 | tf_op jit(solution)/shard_map/ppermute | solution.py:263
  6.6 8.4 %collective-permute-start.1 = (bf16[64,576]{1,0:T(8,128)(2,1)S(1)}, bf16[64,576]{1,0:T(8,128)(2,1)S(1)}, u32[]{:S(2)}, u32[]{:S(2)}) collective-permute-start(bf16[64,576]{1,0:T(8,128)(2,1)S(1)} %get-tuple-element.22), channel_id=1, source_target_pairs={{0,3},{1,4},{2,5},{3,6},{4,7},{5,8},{6,9},{7,10},{8,11},{9,12},{10... | collective-permute-start | bytes 221192 | tf_op jit(solution)/shard_map/ppermute | solution.py:263
  15.2 4.0 %collective-permute-start.2 = (bf16[192,576]{1,0:T(8,128)(2,1)S(1)}, bf16[192,576]{1,0:T(8,128)(2,1)S(1)}, u32[]{:S(2)}, u32[]{:S(2)}) collective-permute-start(bf16[192,576]{1,0:T(8,128)(2,1)S(1)} %pad_maximum_fusion.mine_ref), channel_id=1, source_target_pairs={{0,32},{32,0},{64,96},{96,64},{128,160},{160,128},{192,224},{224,1... | collective-permute-start | bytes 663560 | tf_op jit(solution)/shard_map/ppermute | solution.py:270
  23.9 1.7 %collective-permute-start.3 = (bf16[192,576]{1,0:T(8,128)(2,1)S(1)}, bf16[192,576]{1,0:T(8,128)(2,1)S(1)}, u32[]{:S(2)}, u32[]{:S(2)}) collective-permute-start(bf16[192,576]{1,0:T(8,128)(2,1)S(1)} %get-tuple-element.37), channel_id=1, source_target_pairs={{0,32},{32,0},{64,96},{96,64},{128,160},{160,128},{192,224},{224,1... | collective-permute-start | bytes 663560 | tf_op jit(solution)/shard_map/ppermute | solution.py:270
  25.7 8.8 %collective-permute-start.5 = (bf16[64,576]{1,0:T(8,128)(2,1)S(1)}, bf16[64,576]{1,0:T(8,128)(2,1)S(1)}, u32[]{:S(2)}, u32[]{:S(2)}) collective-permute-start(bf16[64,576]{1,0:T(8,128)(2,1)S(1)} %slice.9), channel_id=1, source_target_pairs={{0,29},{1,30},{2,31},{3,0},{4,1},{5,2},{6,3},{7,4},{8,5},{9,6},{10... | collective-permute-start | bytes 221192 | tf_op jit(solution)/shard_map/ppermute | solution.py:263
  27.4 7.2 %collective-permute-start.4 = (bf16[128,576]{1,0:T(8,128)(2,1)S(1)}, bf16[128,576]{1,0:T(8,128)(2,1)S(1)}, u32[]{:S(2)}, u32[]{:S(2)}) collective-permute-start(bf16[128,576]{1,0:T(8,128)(2,1)S(1)} %slice.8), channel_id=1, source_target_pairs={{0,31},{1,0},{2,1},{3,2},{4,3},{5,4},{6,5},{7,6},{8,7},{9,8},{10,9... | collective-permute-start | bytes 442376 | tf_op jit(solution)/shard_map/ppermute | solution.py:263
  34.7 1.9 %collective-permute-start.6 = (bf16[128,576]{1,0:T(8,128)(2,1)S(1)}, bf16[128,576]{1,0:T(8,128)(2,1)S(1)}, u32[]{:S(2)}, u32[]{:S(2)}) collective-permute-start(bf16[128,576]{1,0:T(8,128)(2,1)S(1)} %device.1.device_ref), channel_id=1, source_target_pairs={{0,32},{32,0},{64,96},{96,64},{128,160},{160,128},{192,224},{224,1... | collective-permute-start | bytes 442376 | tf_op jit(solution)/shard_map/ppermute | solution.py:270
  36.7 8.5 %collective-permute-start.7 = (bf16[128,576]{1,0:T(8,128)(2,1)S(1)}, bf16[128,576]{1,0:T(8,128)(2,1)S(1)}, u32[]{:S(2)}, u32[]{:S(2)}) collective-permute-start(bf16[128,576]{1,0:T(8,128)(2,1)S(1)} %get-tuple-element.38.chip_ref), channel_id=1, source_target_pairs={{0,64},{32,224},{64,128},{96,32},{128,192},{160,96},{192,0},{224,1... | collective-permute-start | bytes 442376 | tf_op jit(solution)/shard_map/ppermute | solution.py:276
  39.2 6.0 %collective-permute-start.8 = (bf16[64,576]{1,0:T(8,128)(2,1)S(1)}, bf16[64,576]{1,0:T(8,128)(2,1)S(1)}, u32[]{:S(2)}, u32[]{:S(2)}) collective-permute-start(bf16[64,576]{1,0:T(8,128)(2,1)S(1)} %get-tuple-element.39), channel_id=1, source_target_pairs={{0,128},{32,160},{64,192},{96,224},{128,0},{160,32},{192,64},{224,... | collective-permute-start | bytes 221192 | tf_op jit(solution)/shard_map/ppermute | solution.py:276
  45.2 2.4 %collective-permute-start.9 = (bf16[192,576]{1,0:T(8,128)(2,1)S(1)}, bf16[192,576]{1,0:T(8,128)(2,1)S(1)}, u32[]{:S(2)}, u32[]{:S(2)}) collective-permute-start(bf16[192,576]{1,0:T(8,128)(2,1)S(1)} %pad_maximum_fusion.1), channel_id=1, source_target_pairs={{0,32},{32,0},{64,96},{96,64},{128,160},{160,128},{192,224},{224,1... | collective-permute-start | bytes 663560 | tf_op jit(solution)/shard_map/ppermute | solution.py:270

commit v3 on v2

v3 whole, which is shorter than its diff:
```python
import functools

import jax
import jax.numpy as jnp
import numpy as np
from jax import lax
from jax.experimental import pallas as pl
from jax.experimental.pallas import tpu as pltpu
from jax.sharding import PartitionSpec as P

LAT = 512
ROPE = 64
BS = 128
WIDTH = LAT + ROPE
HALF = BS // 2
SIDE = BS + HALF
REMOTE = 2 * SIDE
KEYS = BS + REMOTE
TILE = 256
STEP = 1024

score_scale = 192.0 ** (-0.5)
rope_base = 10000.0
exponent_scale = score_scale * float(np.log2(np.e))
MASKED = -1e30

BF = jnp.bfloat16
F32 = jnp.float32
NT = (((1,), (1,)), ((), ()))
NN = (((1,), (0,)), ((), ()))
TN = (((0,), (0,)), ((), ()))


def dot(a, b, dims):
    return lax.dot_general(a, b, dims, preferred_element_type=F32)


def vmem(shape, dtype):
    return pltpu.VMEM(shape, dtype)


def in_vmem(x):
    return pltpu.with_memory_space_constraint(x, pltpu.VMEM)


def in_hbm(x):
    return pltpu.with_memory_space_constraint(x, pltpu.HBM)


def whole():
    return pl.BlockSpec(memory_space=pltpu.VMEM)


def scalars():
    return pl.BlockSpec(memory_space=pltpu.SMEM)


def turn(values, table):
    half = ROPE // 2
    first, second, cosine, sine = values[:half], values[half:], table[:half], table[half:]
    return jnp.concatenate([first * cosine - second * sine, first * sine + second * cosine], axis=0)


def turn_back(values, table):
    half = ROPE // 2
    first, second, cosine, sine = values[:half], values[half:], table[:half], table[half:]
    return jnp.concatenate([first * cosine + second * sine, second * cosine - first * sine], axis=0)


def heads_of(ref, first, count, rows=(0, WIDTH)):
    lo, hi = rows
    return jnp.concatenate([ref[h * WIDTH + lo : h * WIDTH + hi, :] for h in range(first, first + count)], axis=1)


def this_core():
    return lax.rem(lax.axis_index("tp"), 2)


def keys_kernel(anc_ref, parents_ref, freq_hbm, latent_hbm, grad_hbm,
                keys_ref, half_ref, table_ref, closure_ref, bias_ref, grad_ref, freq_ref, latent_ref, sems):
    first = grad_hbm.at[pl.ds(0, grad_ref.shape[0])]
    copies = [
        pltpu.make_async_copy(source, target, sems.at[k])
        for k, (source, target) in enumerate(((latent_hbm, latent_ref), (freq_hbm, freq_ref), (first, grad_ref)))
    ]
    for copy in copies:
        copy.start()
    row = lax.broadcasted_iota(jnp.int32, (BS, BS), 0)
    col = lax.broadcasted_iota(jnp.int32, (BS, BS), 1)
    linked = (row == parents_ref[...]) | (row == col)

    def sweep(closure):
        return jnp.minimum(dot(closure.astype(BF), closure.astype(BF), NN), 1.0)

    reach = jnp.where(linked, 1.0, 0.0)
    early = 4
    for _ in range(early):
        reach = sweep(reach)
    closure_ref[...] = reach

    @pl.when(jnp.max(jnp.sum(reach, axis=0, keepdims=True)) > 2.0**early)
    def _():
        deep = closure_ref[...]
        for _ in range((BS - 1).bit_length() - early):
            deep = sweep(deep)
        closure_ref[...] = deep

    depth = jnp.sum(closure_ref[...], axis=0, keepdims=True) - 1.0
    block, core = lax.axis_index("cp"), this_core()
    count = 0
    for k in range(anc_ref.shape[1]):
        count = count + (anc_ref[0, k] >= 0).astype(jnp.int32)

    def bias(offset):
        wanted = block - offset
        listed = jnp.int32(0)
        for k in range(anc_ref.shape[1]):
            listed = jnp.where(anc_ref[0, k] == wanted, 1, listed)
        return jnp.where((wanted >= 0) & (listed > 0), 0.0, MASKED).astype(F32)

    for k, offset in enumerate((1 + core, 3, 2 - core, 3)):
        bias_ref[k : k + 1, :] = jnp.full((1, TILE), bias(offset), F32)
    bias_ref[4:, :] = jnp.zeros((4, TILE), F32)
    copies[1].wait()
    angles = (depth + (BS * count).astype(F32)) * freq_ref[...]
    table = jnp.concatenate([jnp.cos(angles), jnp.sin(angles)], axis=0)
    table_ref[...] = table
    copies[0].wait()
    for lo in range(0, LAT, BS):
        keys_ref[:, lo : lo + BS] = latent_ref[lo : lo + BS, :].T
    turned = turn(latent_ref[LAT:, :].astype(F32), table)
    keys_ref[:, LAT:] = turned.T.astype(BF)
    half_ref[...] = keys_ref[own_half(), :]
    copies[2].wait()


def own_kernel(heads, query_hbm, grad_hbm, early_ref, keys_ref, table_ref, closure_ref,
               query_ref, sorted_ref, score_ref, slope_ref, late_ref, sems):
    per = TILE // BS
    pieces = heads // per
    pair = per * WIDTH
    late = late_ref.shape[0]
    grad_copy = pltpu.make_async_copy(grad_hbm.at[pl.ds(late, late)], late_ref, sems.at[pieces])
    grad_copy.start()
    copies = []
    for t in range(pieces):
        at = pl.ds(t * pair, pair)
        copies.append(pltpu.make_async_copy(query_hbm.at[at], query_ref.at[at], sems.at[t]))
    for copy in copies:
        copy.start()
    rows = TILE // heads
    row = lax.broadcasted_iota(jnp.int32, (TILE, TILE), 0)
    col = lax.broadcasted_iota(jnp.int32, (TILE, TILE), 1)
    order = jnp.where(col == (row % rows) * heads + row // rows, 1.0, 0.0).astype(BF)
    table = table_ref[...]
    seen = jnp.concatenate([closure_ref[...]] * per, axis=1) > 0.5
    for t in range(pieces):
        if t == pieces // 2:
            grad_copy.wait()
        source, at = (early_ref, t * TILE) if t < pieces // 2 else (late_ref, t * TILE - late)
        chunk = dot(order, source[at : at + TILE, :], NN).astype(BF)
        for h in range(heads):
            sorted_ref[pl.ds(h * BS + t * rows, rows), :] = chunk[h * rows : (h + 1) * rows]
    for copy in copies:
        copy.wait()
    for h in range(heads):
        tail = pl.ds(h * WIDTH + LAT, ROPE)
        query_ref[tail, :] = turn(query_ref[tail, :].astype(F32), table).astype(BF)
    for t in range(pieces):
        here = pl.ds(t * TILE, TILE)
        score = dot(keys_ref[...], heads_of(query_ref, per * t, per), NN)
        score_ref[:, here] = jnp.where(seen, score * exponent_scale, MASKED)
        slope_ref[:, here] = dot(keys_ref[:, :LAT], sorted_ref[here, :], NT)


def key_grads(rows, weight_ref, dscore_ref, query_ref, sorted_ref):
    heads = query_ref.shape[0] // WIDTH
    turned = dot(dscore_ref[rows, :], heads_of(query_ref, 0, heads), NT) * score_scale
    plain = dot(weight_ref[rows, :], sorted_ref[...], NN)
    return turned[:, :LAT] + plain, turned[:, LAT:]


def mine_kernel(query_ref, sorted_ref, mine_ref, score_ref, slope_ref):
    per = TILE // BS
    for t in range(sorted_ref.shape[0] // TILE):
        here = pl.ds(t * TILE, TILE)
        score_ref[:, here] = dot(mine_ref[...], heads_of(query_ref, per * t, per), NN) * exponent_scale
        slope_ref[:, here] = dot(mine_ref[:, :LAT], sorted_ref[here, :], NT)


def main_kernel(bias_ref, query_ref, sorted_ref, other_ref, own_score, own_slope, mine_score, mine_slope,
                weight_ref, dscore_ref, gother_ref, score_ref, slope_ref):
    tiles = sorted_ref.shape[0] // TILE
    per = TILE // BS
    whole_mine, part, whole_other, _ = (bias_ref[k : k + 1, :] for k in range(4))

    def products(t):
        here = pl.ds(t * TILE, TILE)
        score_ref[t % 2] = dot(other_ref[...], heads_of(query_ref, per * t, per), NN) * exponent_scale
        slope_ref[t % 2] = dot(other_ref[:, :LAT], sorted_ref[here, :], NT)

    def softmax(t):
        here = pl.ds(t * TILE, TILE)
        places = (
            (own_score[:, here], own_slope[:, here], 0.0),
            (mine_score[:BS, here], mine_slope[:BS, here], whole_mine),
            (mine_score[BS:, here], mine_slope[BS:, here], part),
            (score_ref[t % 2, :BS], slope_ref[t % 2, :BS], whole_other),
            (score_ref[t % 2, BS:], slope_ref[t % 2, BS:], part),
        )
        largest = functools.reduce(jnp.maximum, [jnp.max(s, axis=0, keepdims=True) + b for s, _, b in places])
        expos = [jnp.exp2(s - (largest - b)) for s, _, b in places]
        inverse = 1.0 / sum(jnp.sum(e, axis=0, keepdims=True) for e in expos)
        delta = sum(jnp.sum(e * l, axis=0, keepdims=True) for e, (_, l, _) in zip(expos, places)) * inverse
        at = 0
        for e, (_, l, _) in zip(expos, places):
            rows = pl.ds(at, e.shape[0])
            weight = e * inverse
            weight_ref[rows, here] = weight.astype(BF)
            dscore_ref[rows, here] = (weight * (l - delta)).astype(BF)
            at += e.shape[0]

    products(0)
    for t in range(tiles):
        if t + 1 < tiles:
            products(t + 1)
        softmax(t)
    lead, tail = key_grads(pl.ds(BS + SIDE, SIDE), weight_ref, dscore_ref, query_ref, sorted_ref)
    gother_ref[:, :LAT] = lead.astype(BF)
    gother_ref[:, LAT:] = tail.astype(BF)


def grads_kernel(rows, weight_ref, dscore_ref, query_ref, sorted_ref, out_ref):
    lead, tail = key_grads(rows, weight_ref, dscore_ref, query_ref, sorted_ref)
    out_ref[:, :LAT] = lead
    out_ref[:, LAT:] = tail


def query_kernel(dscore_ref, keys_ref, mine_ref, other_ref, table_ref, dquery_ref, every_ref, turned_ref):
    t = pl.program_id(0)

    @pl.when(t == 0)
    def _():
        every_ref[:BS, :] = keys_ref[...]
        every_ref[BS : BS + SIDE, :] = mine_ref[...]
        every_ref[BS + SIDE :, :] = other_ref[...]
        for lo in range(0, KEYS, BS):
            turned_ref[:, lo : lo + BS] = every_ref[lo : lo + BS, :].T

    dscore = dscore_ref[:, pl.ds(pl.multiple_of(t * STEP, STEP), STEP)]
    grads = dot(turned_ref[...], dscore, NN) * score_scale
    for k in range(STEP // BS):
        part = grads[:, k * BS : (k + 1) * BS]
        dquery_ref[k, :LAT, :] = part[:LAT].astype(BF)
        dquery_ref[k, LAT:, :] = turn_back(part[LAT:], table_ref[...]).astype(BF)


def own_half():
    return pl.ds(pl.multiple_of(this_core() * HALF, HALF), HALF)


def other_half():
    return pl.ds(pl.multiple_of((1 - this_core()) * HALF, HALF), HALF)


def device_kernel(gown_ref, back_ref, half_ref, out_ref, sum_ref):
    sum_ref[...] = gown_ref[...] + back_ref[...].astype(F32)
    sum_ref[own_half(), :] += half_ref[...].astype(F32)
    out_ref[...] = sum_ref[...].astype(BF)


def chip_kernel(device_ref, other_ref, chip_ref, half_ref):
    chip_ref[...] = (device_ref[...].astype(F32) + other_ref[...].astype(F32)).astype(BF)
    half_ref[...] = chip_ref[own_half(), :]


def finish_kernel(chip_ref, near_ref, far_ref, rest_ref, table_ref, out_ref, sum_ref):
    sum_ref[...] = chip_ref[...].astype(F32)
    sum_ref[own_half(), :] += far_ref[...].astype(F32)
    sum_ref[other_half(), :] += rest_ref[BS:, :].astype(F32)
    sum_ref[...] += near_ref[...].astype(F32) + rest_ref[:BS, :].astype(F32)
    for lo in range(0, LAT, BS):
        out_ref[lo : lo + BS, :] = sum_ref[:, lo : lo + BS].T.astype(BF)
    out_ref[LAT:, :] = turn_back(sum_ref[:, LAT:].T, table_ref[...]).astype(BF)


def by_core(block, even, odd):
    tp, cp = lax.axis_size("tp"), lax.axis_size("cp")
    route = []
    for t in range(tp):
        step = odd if t % 2 else even
        for c in range(cp):
            if 0 <= c + step < cp or WRAP:
                route.append((t * cp + c, t * cp + (c + step) % cp))
    return lax.ppermute(block, ("tp", "cp"), route)


WRAP = True


def other_core(block):
    return lax.ppermute(block, "tp", [(t, t ^ 1) for t in range(lax.axis_size("tp"))])


def along_x(block, even, odd):
    route = [(t, t ^ (2 * (odd if t % 2 else even))) for t in range(lax.axis_size("tp"))]
    return lax.ppermute(block, "tp", route)


def on_device(query, latent, grad_out, ancestors, parents):
    rows, heads, _ = query.shape
    total = rows * heads
    half = ROPE // 2
    lane_freq = rope_base ** (-2.0 * np.arange(half, dtype=np.float64) / ROPE)
    freq = jnp.asarray(np.tile(lane_freq[:, None], (1, BS)), dtype=F32)
    params = pltpu.CompilerParams(vmem_limit_bytes=16 * 2**20)
    outside = pl.BlockSpec(memory_space=pltpu.HBM)

    def call(kernel, name, ins, outs, flops=0, **more):
        return pl.pallas_call(
            kernel,
            in_specs=ins,
            out_specs=[whole()] * len(outs),
            out_shape=[vmem(*o) for o in outs],
            cost_estimate=pl.CostEstimate(flops=flops, bytes_accessed=4 * total * WIDTH, transcendentals=0),
            compiler_params=params,
            name=name,
            **more,
        )

    keys, keys_half, table, closure, bias, early = call(
        keys_kernel,
        "keys",
        [scalars(), whole(), outside, outside, outside],
        [((BS, WIDTH), BF), ((HALF, WIDTH), BF), ((ROPE, BS), F32), ((BS, BS), F32), ((8, TILE), F32), ((total // 2, LAT), BF)],
        scratch_shapes=[pltpu.VMEM((half, BS), F32), pltpu.VMEM((WIDTH, BS), BF), pltpu.SemaphoreType.DMA((3,))],
    )(*map(in_hbm, (ancestors, parents.reshape(1, BS), freq, latent.T, grad_out.reshape(total, LAT))))

    fetched = by_core(keys, 1, 2)
    fetched_half = by_core(keys_half, 3, 3)

    q, g, own_score, own_slope = call(
        functools.partial(own_kernel, heads),
        "own",
        [outside] * 2 + [whole()] * 4,
        [((heads * WIDTH, rows), BF), ((total, LAT), BF), ((BS, total), F32), ((BS, total), F32)],
        flops=2 * total * BS * 1800,
        scratch_shapes=[pltpu.VMEM((total // 2, LAT), BF), pltpu.SemaphoreType.DMA((total // TILE + 1,))],
    )(in_hbm(query.transpose(1, 2, 0).reshape(heads * WIDTH, rows)), in_hbm(grad_out.reshape(total, LAT)),
      early, keys, table, closure)

    mine, q = lax.optimization_barrier((jnp.concatenate([fetched, fetched_half]), q))
    other = other_core(mine)
    mine_score, mine_slope = call(
        mine_kernel, "mine", [whole()] * 3, [((SIDE, total), F32), ((SIDE, total), F32)], flops=2 * total * SIDE * 1280
    )(q, g, mine)

    weight, dscore, gother = call(
        main_kernel,
        "main",
        [whole()] * 8,
        [((KEYS, total), BF), ((KEYS, total), BF), ((SIDE, WIDTH), BF)],
        flops=2 * total * SIDE * 2560,
        scratch_shapes=[pltpu.VMEM((2, SIDE, TILE), F32), pltpu.VMEM((2, SIDE, TILE), F32)],
    )(bias, q, g, other, own_score, own_slope, mine_score, mine_slope)

    gother = other_core(gother)
    (gmine,) = call(
        functools.partial(grads_kernel, slice(BS, BS + SIDE)),
        "grads",
        [whole()] * 4,
        [((SIDE, WIDTH), F32)],
        flops=2 * total * SIDE * 1280,
    )(weight, dscore, q, g)
    gmine = (gmine + gother.astype(F32)).astype(BF)
    back = by_core(gmine[:BS], -1, -2)
    back_half = by_core(gmine[BS:], -3, -3)

    (gown,) = call(
        functools.partial(grads_kernel, slice(0, BS)),
        "gown",
        [whole()] * 4,
        [((BS, WIDTH), F32)],
        flops=2 * total * BS * 1280,
    )(weight, dscore, q, g)
    (device_sum,) = call(
        device_kernel,
        "device",
        [whole()] * 3,
        [((BS, WIDTH), BF)],
        scratch_shapes=[pltpu.VMEM((BS, WIDTH), F32)],
    )(gown, back, back_half)
    chip_sum, chip_half = call(
        chip_kernel, "chip", [whole()] * 2, [((BS, WIDTH), BF), ((HALF, WIDTH), BF)]
    )(device_sum, other_core(device_sum))
    chip_sum, dscore = lax.optimization_barrier((chip_sum, dscore))
    near = along_x(chip_sum, 1, 3)
    far = along_x(chip_half, 2, 2)
    dquery = pl.pallas_call(
        query_kernel,
        grid=(total // STEP,),
        in_specs=[whole()] * 5,
        out_specs=pl.BlockSpec((STEP // BS, WIDTH, BS), lambda t: (t, 0, 0)),
        out_shape=jax.ShapeDtypeStruct((heads, WIDTH, rows), BF),
        scratch_shapes=[pltpu.VMEM((KEYS, WIDTH), BF), pltpu.VMEM((WIDTH, KEYS), BF)],
        cost_estimate=pl.CostEstimate(flops=2 * total * KEYS * 768, bytes_accessed=4 * total * WIDTH, transcendentals=0),
        compiler_params=params,
        name="dquery",
    )(dscore, keys, mine, other, table)
    near, dquery = lax.optimization_barrier((near, dquery))
    rest = other_core(jnp.concatenate([near, far]))
    d_latent = pl.pallas_call(
        finish_kernel,
        in_specs=[whole()] * 5,
        out_specs=whole(),
        out_shape=jax.ShapeDtypeStruct((WIDTH, BS), BF),
        scratch_shapes=[pltpu.VMEM((BS, WIDTH), F32)],
        compiler_params=params,
        name="finish",
    )(*map(in_vmem, (chip_sum, near, far, rest, table)))
    return (dquery.transpose(2, 0, 1), d_latent.T)


def solution(mesh):
    placed = (P("cp", "tp", None), P("cp", None), P("cp", "tp", None), P("cp", None), P("cp"))
    return jax.shard_map(
        on_device,
        mesh=mesh,
        in_specs=placed,
        out_specs=(P("cp", "tp", None), P("cp", None)),
        check_vma=False,
    )
```

time: 48.7 us -> 46.4 us (0.953)
  Pallas kernels: 20.5 us -> 17.4 us
  waiting for transfers between devices: 8.17 us -> 10.6 us
  starting transfers between devices: 19.1 us -> 17.4 us
    ppermute x4, waiting for transfers between devices: 0.55 us -> 6.42 us  [by_core(): return lax.ppermute(block, ('tp', 'cp'), route)]
    ppermute x2, waiting for transfers between devices: 5.45 us -> 1.68 us  [along_x(): return lax.ppermute(block, 'tp', route)]
    pallas_call x1, Pallas kernels: 5.91 us -> 3.33 us  [on_device(): call(functools.partial(own_kernel, heads), 'own', [outside] * 2 + [whole(...]
    ppermute x4, starting transfers between devices: 5.05 us -> 3.42 us  [other_core(): lax.ppermute(block, 'tp', [(t, t ^ 1) for t in range(lax.axis_size('tp'))])]
    pallas_call x1, Pallas kernels: 3.82 us -> 2.84 us  [on_device(): pl.pallas_call(query_kernel, grid=(total // STEP,), in_specs=[whole()] *...]
    ppermute x4, starting transfers between devices: 11 us -> 10.3 us  [by_core(): return lax.ppermute(block, ('tp', 'cp'), route)]
    ppermute x2, starting transfers between devices: 3.08 us -> 3.69 us  [along_x(): return lax.ppermute(block, 'tp', route)]
    pallas_call x3 -> x4, Pallas kernels: 8.32 us -> 8.82 us  [the longest x1 4.19 us: on_device(): call(main_kernel, 'main', [whole()] * 8, [((KEYS, total), BF), ((KEYS, to...]
  transfers between devices with their start and end apart: 10 -> 10, of which waited for: 5 -> 6; matrix products, arithmetic and copies ran while one was open for 0% -> 0% of each run, Pallas kernels for 26% -> 22%
where the time goes in v3:
time: 46.4 us; the launch traced here: 46.3 us
  Pallas kernels  17.4 us (37%)
  starting transfers between devices  17.4 us (37%)
  waiting for transfers between devices  10.6 us (23%)
  between operations  0.75 us (2%)
    ppermute x4, starting transfers between devices, by_core(): return lax.ppermute(block, ('tp', 'cp'), route)  10.3 us
    ppermute x4, waiting for transfers between devices, by_core(): return lax.ppermute(block, ('tp', 'cp'), route)  6.42 us
    pallas_call x1, Pallas kernels, on_device(): call(main_kernel, 'main', [whole()] * 8, [((KEYS, total), BF), ((KEYS, to...  4.19 us
    ppermute x2, starting transfers between devices, along_x(): return lax.ppermute(block, 'tp', route)  3.69 us
    ppermute x4, starting transfers between devices, other_core(): lax.ppermute(block, 'tp', [(t, t ^ 1) for t in range(lax.axis_size('tp'))])  3.42 us
    pallas_call x1, Pallas kernels, on_device(): call(functools.partial(own_kernel, heads), 'own', [outside] * 2 + [whole(...  3.33 us
    pallas_call x1, Pallas kernels, on_device(): pl.pallas_call(query_kernel, grid=(total // STEP,), in_specs=[whole()] *...  2.84 us
    ppermute x4, waiting for transfers between devices, other_core(): lax.ppermute(block, 'tp', [(t, t ^ 1) for t in range(lax.axis_size('tp'))])  2.53 us
  transfers between devices with their start and end apart: 10, of which 6 were waited for; matrix products, arithmetic and copies ran while one was open for 0% of the time, Pallas kernels for 22%

profile of v3, /device:TPU:1, one launch (start us, length us, event | category | flops | bytes accessed | tf_op | source)
XLA Modules:
  0.0 46.3 jit_solution(1067452261657736140)
XLA Ops:
  0.6 2.0 %keys.1 = (bf16[128,576]{1,0:T(8,128)(2,1)S(1)}, bf16[64,576]{1,0:T(8,128)(2,1)S(1)}, f32[64,128]{1,0:T(8,128)S(1)}, f32[128,128]{1,0:T(8,128)S(1)}, f32[8,256]{...) custom-call(s32[1,3]{1,0:T(1,128)} %anc_ref.1, s32[1,128]{1,0:T(1,128)} %bitcast.13, f32[32,128]{1,0:T(8,128)} %constant.2.clone.freq_hbm, ...), custom_call_target="tpu_custom_call" | custom-call | bytes 4718592 | tf_op jit(solution)/shard_map/keys/pallas_call | solution.py:331
  2.7 3.8 %collective-permute-start = (bf16[128,576]{1,0:T(8,128)(2,1)S(1)}, bf16[128,576]{1,0:T(8,128)(2,1)S(1)}, u32[]{:S(2)}, u32[]{:S(2)}) collective-permute-start(bf16[128,576]{1,0:T(8,128)(2,1)S(1)} %get-tuple-element.26.keys_ref), channel_id=1, source_target_pairs={{0,1},{1,2},{2,3},{3,4},{4,5},{5,6},{6,7},{7,8},{8,9},{9,10},{10,1... | collective-permute-start | bytes 442376 | tf_op jit(solution)/shard_map/ppermute | solution.py:295
  6.5 2.1 %collective-permute-start.1 = (bf16[64,576]{1,0:T(8,128)(2,1)S(1)}, bf16[64,576]{1,0:T(8,128)(2,1)S(1)}, u32[]{:S(2)}, u32[]{:S(2)}) collective-permute-start(bf16[64,576]{1,0:T(8,128)(2,1)S(1)} %get-tuple-element.27), channel_id=1, source_target_pairs={{0,3},{1,4},{2,5},{3,6},{4,7},{5,8},{6,9},{7,10},{8,11},{9,12},{10... | collective-permute-start | bytes 221192 | tf_op jit(solution)/shard_map/ppermute | solution.py:295
  8.6 3.3 %own.1 = (bf16[9216,128]{1,0:T(8,128)(2,1)S(1)}, bf16[2048,512]{1,0:T(8,128)(2,1)S(1)}, f32[128,2048]{1,0:T(8,128)S(1)}, f32[128,2048]{1,0:T(8,128)S(1)}) custom-call(bf16[9216,128]{1,0:T(8,128)(2,1)} %bitcast.10, bf16[2048,512]{1,0:T(8,128)(2,1)} %bitcast.9, bf16[1024,512]{1,0:T(8,128)(2,1)S(1)} %get-tuple-element.28.early_ref, ...), custom_call_target="tpu_custom_call" | custom-call | flops 943718400 | bytes 4718592 | tf_op jit(solution)/shard_map/own/pallas_call | solution.py:342
  12.0 2.9 %collective-permute-done.1 = bf16[64,576]{1,0:T(8,128)(2,1)S(1)} collective-permute-done((bf16[64,576]{1,0:T(8,128)(2,1)S(1)}, bf16[64,576]{1,0:T(8,128)(2,1)S(1)}, u32[]{:S(2)}, u32[]{:S(2)}) %collective-permute-start.1) | collective-permute-done | bytes 73760 | tf_op jit(solution)/shard_map/ppermute | solution.py:295
  14.8 0.2 collective-permute-done
  15.1 2.6 %collective-permute-start.2 = (bf16[192,576]{1,0:T(8,128)(2,1)S(1)}, bf16[192,576]{1,0:T(8,128)(2,1)S(1)}, u32[]{:S(2)}, u32[]{:S(2)}) collective-permute-start(bf16[192,576]{1,0:T(8,128)(2,1)S(1)} %pad_maximum_fusion.mine_ref), channel_id=1, source_target_pairs={{0,32},{32,0},{64,96},{96,64},{128,160},{160,128},{192,224},{224,1... | collective-permute-start | bytes 663560 | tf_op jit(solution)/shard_map/ppermute | solution.py:302
  17.7 1.3 %mine.1 = (f32[192,2048]{1,0:T(8,128)S(1)}, f32[192,2048]{1,0:T(8,128)S(1)}) custom-call(bf16[9216,128]{1,0:T(8,128)(2,1)S(1)} %get-tuple-element.32.query_ref, bf16[2048,512]{1,0:T(8,128)(2,1)S(1)} %get-tuple-element.33.sorted_ref, bf16[192,576]{1,0:T(8,128)(2,1)S(1)} %pad_maximum_fusion.mine_ref), custom_call_target="tpu_custom_call" | custom-call | flops 1006632960 | bytes 4718592 | tf_op jit(solution)/shard_map/mine/pallas_call | solution.py:354
  19.0 0.0 collective-permute-done.2.other_ref
  19.1 4.2 %main.1 = (bf16[512,2048]{1,0:T(8,128)(2,1)S(1)}, bf16[512,2048]{1,0:T(8,128)(2,1)S(1)}, bf16[192,576]{1,0:T(8,128)(2,1)S(1)}) custom-call(f32[8,256]{1,0:T(8,128)S(1)} %get-tuple-element.25.bias_ref, bf16[9216,128]{1,0:T(8,128)(2,1)S(1)} %get-tuple-element.32.query_ref, bf16[2048,512]{1,0:T(8,128)(2,1)S(1)} %get-tuple-element.33.sorted_ref, ...), custom_call_target="tpu_custom_call" | custom-call | flops 2013265920 | bytes 4718592 | tf_op jit(solution)/shard_map/main/pallas_call | solution.py:358
  23.2 0.2 collective-permute-start.3
  23.5 1.4 %grads.1 = f32[192,576]{1,0:T(8,128)S(1)} custom-call(bf16[512,2048]{1,0:T(8,128)(2,1)S(1)} %get-tuple-element.39.weight_ref, bf16[512,2048]{1,0:T(8,128)(2,1)S(1)} %get-tuple-element.44.dscore_ref, bf16[9216,128]{1,0:T(8,128)(2,1)S(1)} %get-tuple-element.32.query_ref, bf16[2048,512]{1,0:T(8,128)(2,1)S(1)} %get-tuple-element.33.sorted_ref), custom_call_target="tpu_custom_call" | custom-call | flops 1006632960 | bytes 4718592 | tf_op jit(solution)/shard_map/grads/pallas_call | solution.py:368
  24.9 0.0 collective-permute-done.3
  24.9 0.1 add_convert_fusion
  25.0 4.0 %collective-permute-start.4 = (bf16[128,576]{1,0:T(8,128)(2,1)S(1)}, bf16[128,576]{1,0:T(8,128)(2,1)S(1)}, u32[]{:S(2)}, u32[]{:S(2)}) collective-permute-start(bf16[128,576]{1,0:T(8,128)(2,1)S(1)} %slice.8), channel_id=1, source_target_pairs={{0,31},{1,0},{2,1},{3,2},{4,3},{5,4},{6,5},{7,6},{8,7},{9,8},{10,9... | collective-permute-start | bytes 442376 | tf_op jit(solution)/shard_map/ppermute | solution.py:295
  29.1 0.3 collective-permute-start.5
  29.3 1.2 %gown.1.gown_ref = f32[128,576]{1,0:T(8,128)S(1)} custom-call(bf16[512,2048]{1,0:T(8,128)(2,1)S(1)} %get-tuple-element.39.weight_ref, bf16[512,2048]{1,0:T(8,128)(2,1)S(1)} %get-tuple-element.44.dscore_ref, bf16[9216,128]{1,0:T(8,128)(2,1)S(1)} %get-tuple-element.32.query_ref, bf16[2048,512]{1,0:T(8,128)(2,1)S(1)} %get-tuple-element.33.sorted_ref), custom_call_target="tpu_custom_call" | custom-call | flops 671088640 | bytes 4718592 | tf_op jit(solution)/shard_map/gown/pallas_call | solution.py:379
  30.5 3.3 %collective-permute-done.5.half_ref = bf16[64,576]{1,0:T(8,128)(2,1)S(1)} collective-permute-done((bf16[64,576]{1,0:T(8,128)(2,1)S(1)}, bf16[64,576]{1,0:T(8,128)(2,1)S(1)}, u32[]{:S(2)}, u32[]{:S(2)}) %collective-permute-start.5) | collective-permute-done | bytes 73760 | tf_op jit(solution)/shard_map/ppermute | solution.py:295
  33.9 0.0 collective-permute-done.4.back_ref
  33.9 0.1 device.1.device_ref
  33.9 0.1 collective-permute-start.6
  34.0 1.4 %collective-permute-done.6.other_ref = bf16[128,576]{1,0:T(8,128)(2,1)S(1)} collective-permute-done((bf16[128,576]{1,0:T(8,128)(2,1)S(1)}, bf16[128,576]{1,0:T(8,128)(2,1)S(1)}, u32[]{:S(2)}, u32[]{:S(2)}) %collective-permute-start.6) | collective-permute-done | bytes 147488 | tf_op jit(solution)/shard_map/ppermute | solution.py:302
  35.4 0.1 chip.1
  35.5 2.8 %collective-permute-start.8 = (bf16[64,576]{1,0:T(8,128)(2,1)S(1)}, bf16[64,576]{1,0:T(8,128)(2,1)S(1)}, u32[]{:S(2)}, u32[]{:S(2)}) collective-permute-start(bf16[64,576]{1,0:T(8,128)(2,1)S(1)} %get-tuple-element.47), channel_id=1, source_target_pairs={{0,128},{32,160},{64,192},{96,224},{128,0},{160,32},{192,64},{224,... | collective-permute-start | bytes 221192 | tf_op jit(solution)/shard_map/ppermute | solution.py:307
  38.3 0.9 %collective-permute-start.7 = (bf16[128,576]{1,0:T(8,128)(2,1)S(1)}, bf16[128,576]{1,0:T(8,128)(2,1)S(1)}, u32[]{:S(2)}, u32[]{:S(2)}) collective-permute-start(bf16[128,576]{1,0:T(8,128)(2,1)S(1)} %get-tuple-element.43.chip_ref), channel_id=1, source_target_pairs={{0,64},{32,224},{64,0},{96,160},{128,192},{160,96},{192,128},{224,... | collective-permute-start | bytes 442376 | tf_op jit(solution)/shard_map/ppermute | solution.py:307
  39.2 2.8 %dquery.1 = bf16[16,576,128]{2,1,0:T(8,128)(2,1)} custom-call(bf16[512,2048]{1,0:T(8,128)(2,1)S(1)} %get-tuple-element.44.dscore_ref, bf16[128,576]{1,0:T(8,128)(2,1)S(1)} %get-tuple-element.26.keys_ref, bf16[192,576]{1,0:T(8,128)(2,1)S(1)} %pad_maximum_fusion.mine_ref, bf16[192,576]{1,0:T(8,128)(2,1)S(1)} %collective-permute-done.2.other_ref, ...), custom_call_target="tpu_custom_call" | custom-call | flops 1610612736 | bytes 4718592 | tf_op jit(solution)/shard_map/dquery/pallas_call | solution.py:399
  42.0 1.7 %collective-permute-done.7.near_ref = bf16[128,576]{1,0:T(8,128)(2,1)S(1)} collective-permute-done((bf16[128,576]{1,0:T(8,128)(2,1)S(1)}, bf16[128,576]{1,0:T(8,128)(2,1)S(1)}, u32[]{:S(2)}, u32[]{:S(2)}) %collective-permute-start.7) | collective-permute-done | bytes 147488 | tf_op jit(solution)/shard_map/ppermute | solution.py:307
  43.7 0.0 collective-permute-done.8.far_ref
  43.7 0.5 %collective-permute-start.9 = (bf16[192,576]{1,0:T(8,128)(2,1)S(1)}, bf16[192,576]{1,0:T(8,128)(2,1)S(1)}, u32[]{:S(2)}, u32[]{:S(2)}) collective-permute-start(bf16[192,576]{1,0:T(8,128)(2,1)S(1)} %pad_maximum_fusion.1), channel_id=1, source_target_pairs={{0,32},{32,0},{64,96},{96,64},{128,160},{160,128},{192,224},{224,1... | collective-permute-start | bytes 663560 | tf_op jit(solution)/shard_map/ppermute | solution.py:302
  44.2 1.1 %collective-permute-done.9.rest_ref = bf16[192,576]{1,0:T(8,128)(2,1)S(1)} collective-permute-done((bf16[192,576]{1,0:T(8,128)(2,1)S(1)}, bf16[192,576]{1,0:T(8,128)(2,1)S(1)}, u32[]{:S(2)}, u32[]{:S(2)}) %collective-permute-start.9) | collective-permute-done | bytes 221216 | tf_op jit(solution)/shard_map/ppermute | solution.py:302
  45.3 0.9 %finish.1 = bf16[576,128]{1,0:T(8,128)(2,1)} custom-call(bf16[128,576]{1,0:T(8,128)(2,1)S(1)} %get-tuple-element.43.chip_ref, bf16[128,576]{1,0:T(8,128)(2,1)S(1)} %collective-permute-done.7.near_ref, bf16[64,576]{1,0:T(8,128)(2,1)S(1)} %collective-permute-done.8.far_ref, bf16[192,576]{1,0:T(8,128)(2,1)S(1)} %collective-permute-done.9.rest_ref, ...), custom_call_target="tpu_custom_call" | custom-call | tf_op jit(solution)/shard_map/finish/pallas_call | solution.py:412
  (4 shorter events, 0.1 us)
Async XLA Ops:
  2.7 12.4 %collective-permute-start = (bf16[128,576]{1,0:T(8,128)(2,1)S(1)}, bf16[128,576]{1,0:T(8,128)(2,1)S(1)}, u32[]{:S(2)}, u32[]{:S(2)}) collective-permute-start(bf16[128,576]{1,0:T(8,128)(2,1)S(1)} %get-tuple-element.26.keys_ref), channel_id=1, source_target_pairs={{0,1},{1,2},{2,3},{3,4},{4,5},{5,6},{6,7},{7,8},{8,9},{9,10},{10,1... | collective-permute-start | bytes 442376 | tf_op jit(solution)/shard_map/ppermute | solution.py:295
  6.5 8.4 %collective-permute-start.1 = (bf16[64,576]{1,0:T(8,128)(2,1)S(1)}, bf16[64,576]{1,0:T(8,128)(2,1)S(1)}, u32[]{:S(2)}, u32[]{:S(2)}) collective-permute-start(bf16[64,576]{1,0:T(8,128)(2,1)S(1)} %get-tuple-element.27), channel_id=1, source_target_pairs={{0,3},{1,4},{2,5},{3,6},{4,7},{5,8},{6,9},{7,10},{8,11},{9,12},{10... | collective-permute-start | bytes 221192 | tf_op jit(solution)/shard_map/ppermute | solution.py:295
  15.1 4.0 %collective-permute-start.2 = (bf16[192,576]{1,0:T(8,128)(2,1)S(1)}, bf16[192,576]{1,0:T(8,128)(2,1)S(1)}, u32[]{:S(2)}, u32[]{:S(2)}) collective-permute-start(bf16[192,576]{1,0:T(8,128)(2,1)S(1)} %pad_maximum_fusion.mine_ref), channel_id=1, source_target_pairs={{0,32},{32,0},{64,96},{96,64},{128,160},{160,128},{192,224},{224,1... | collective-permute-start | bytes 663560 | tf_op jit(solution)/shard_map/ppermute | solution.py:302
  23.2 1.7 %collective-permute-start.3 = (bf16[192,576]{1,0:T(8,128)(2,1)S(1)}, bf16[192,576]{1,0:T(8,128)(2,1)S(1)}, u32[]{:S(2)}, u32[]{:S(2)}) collective-permute-start(bf16[192,576]{1,0:T(8,128)(2,1)S(1)} %get-tuple-element.41), channel_id=1, source_target_pairs={{0,32},{32,0},{64,96},{96,64},{128,160},{160,128},{192,224},{224,1... | collective-permute-start | bytes 663560 | tf_op jit(solution)/shard_map/ppermute | solution.py:302
  25.0 8.9 %collective-permute-start.4 = (bf16[128,576]{1,0:T(8,128)(2,1)S(1)}, bf16[128,576]{1,0:T(8,128)(2,1)S(1)}, u32[]{:S(2)}, u32[]{:S(2)}) collective-permute-start(bf16[128,576]{1,0:T(8,128)(2,1)S(1)} %slice.8), channel_id=1, source_target_pairs={{0,31},{1,0},{2,1},{3,2},{4,3},{5,4},{6,5},{7,6},{8,7},{9,8},{10,9... | collective-permute-start | bytes 442376 | tf_op jit(solution)/shard_map/ppermute | solution.py:295
  29.1 4.8 %collective-permute-start.5 = (bf16[64,576]{1,0:T(8,128)(2,1)S(1)}, bf16[64,576]{1,0:T(8,128)(2,1)S(1)}, u32[]{:S(2)}, u32[]{:S(2)}) collective-permute-start(bf16[64,576]{1,0:T(8,128)(2,1)S(1)} %slice.9), channel_id=1, source_target_pairs={{0,29},{1,30},{2,31},{3,0},{4,1},{5,2},{6,3},{7,4},{8,5},{9,6},{10... | collective-permute-start | bytes 221192 | tf_op jit(solution)/shard_map/ppermute | solution.py:295
  33.9 1.5 %collective-permute-start.6 = (bf16[128,576]{1,0:T(8,128)(2,1)S(1)}, bf16[128,576]{1,0:T(8,128)(2,1)S(1)}, u32[]{:S(2)}, u32[]{:S(2)}) collective-permute-start(bf16[128,576]{1,0:T(8,128)(2,1)S(1)} %device.1.device_ref), channel_id=1, source_target_pairs={{0,32},{32,0},{64,96},{96,64},{128,160},{160,128},{192,224},{224,1... | collective-permute-start | bytes 442376 | tf_op jit(solution)/shard_map/ppermute | solution.py:302
  35.5 8.2 %collective-permute-start.8 = (bf16[64,576]{1,0:T(8,128)(2,1)S(1)}, bf16[64,576]{1,0:T(8,128)(2,1)S(1)}, u32[]{:S(2)}, u32[]{:S(2)}) collective-permute-start(bf16[64,576]{1,0:T(8,128)(2,1)S(1)} %get-tuple-element.47), channel_id=1, source_target_pairs={{0,128},{32,160},{64,192},{96,224},{128,0},{160,32},{192,64},{224,... | collective-permute-start | bytes 221192 | tf_op jit(solution)/shard_map/ppermute | solution.py:307
  38.3 5.4 %collective-permute-start.7 = (bf16[128,576]{1,0:T(8,128)(2,1)S(1)}, bf16[128,576]{1,0:T(8,128)(2,1)S(1)}, u32[]{:S(2)}, u32[]{:S(2)}) collective-permute-start(bf16[128,576]{1,0:T(8,128)(2,1)S(1)} %get-tuple-element.43.chip_ref), channel_id=1, source_target_pairs={{0,64},{32,224},{64,0},{96,160},{128,192},{160,96},{192,128},{224,... | collective-permute-start | bytes 442376 | tf_op jit(solution)/shard_map/ppermute | solution.py:307
  43.7 1.6 %collective-permute-start.9 = (bf16[192,576]{1,0:T(8,128)(2,1)S(1)}, bf16[192,576]{1,0:T(8,128)(2,1)S(1)}, u32[]{:S(2)}, u32[]{:S(2)}) collective-permute-start(bf16[192,576]{1,0:T(8,128)(2,1)S(1)} %pad_maximum_fusion.1), channel_id=1, source_target_pairs={{0,32},{32,0},{64,96},{96,64},{128,160},{160,128},{192,224},{224,1... | collective-permute-start | bytes 663560 | tf_op jit(solution)/shard_map/ppermute | solution.py:302

commit v4 on v3

--- a/solution.py
+++ b/solution.py
@@ -18,6 +18,7 @@
 KEYS = BS + REMOTE
 TILE = 256
 STEP = 1024
+EVEN, ODD, BOTH = 2, 3, 1
 
 score_scale = 192.0 ** (-0.5)
 rope_base = 10000.0
@@ -118,7 +119,7 @@
             listed = jnp.where(anc_ref[0, k] == wanted, 1, listed)
         return jnp.where((wanted >= 0) & (listed > 0), 0.0, MASKED).astype(F32)
 
-    for k, offset in enumerate((1 + core, 3, 2 - core, 3)):
+    for k, offset in enumerate((EVEN + (ODD - EVEN) * core, BOTH, ODD - (ODD - EVEN) * core, BOTH)):
         bias_ref[k : k + 1, :] = jnp.full((1, TILE), bias(offset), F32)
     bias_ref[4:, :] = jnp.zeros((4, TILE), F32)
     copies[1].wait()
@@ -134,8 +135,17 @@
     copies[2].wait()
 
 
+def partial_softmax(score, slope, stat_ref, first, here):
+    largest = jnp.max(score, axis=0, keepdims=True)
+    expo = jnp.exp2(score - largest)
+    stat_ref[first : first + 1, here] = largest
+    stat_ref[first + 1 : first + 2, here] = jnp.sum(expo, axis=0, keepdims=True)
+    stat_ref[first + 2 : first + 3, here] = jnp.sum(expo * slope, axis=0, keepdims=True)
+    return expo
+
+
 def own_kernel(heads, query_hbm, grad_hbm, early_ref, keys_ref, table_ref, closure_ref,
-               query_ref, sorted_ref, score_ref, slope_ref, late_ref, sems):
+               query_ref, sorted_ref, expo_ref, slope_ref, stat_ref, late_ref, sems):
     per = TILE // BS
     pieces = heads // per
     pair = per * WIDTH
@@ -169,8 +179,10 @@
     for t in range(pieces):
         here = pl.ds(t * TILE, TILE)
         score = dot(keys_ref[...], heads_of(query_ref, per * t, per), NN)
-        score_ref[:, here] = jnp.where(seen, score * exponent_scale, MASKED)
-        slope_ref[:, here] = dot(keys_ref[:, :LAT], sorted_ref[here, :], NT)
+        score = jnp.where(seen, score * exponent_scale, MASKED)
+        slope = dot(keys_ref[:, :LAT], sorted_ref[here, :], NT)
+        expo_ref[:, here] = partial_softmax(score, slope, stat_ref, 0, here)
+        slope_ref[:, here] = slope
 
 
 def key_grads(rows, weight_ref, dscore_ref, query_ref, sorted_ref):
@@ -180,15 +192,18 @@
     return turned[:, :LAT] + plain, turned[:, LAT:]
 
 
-def mine_kernel(query_ref, sorted_ref, mine_ref, score_ref, slope_ref):
+def mine_kernel(query_ref, sorted_ref, mine_ref, expo_ref, slope_ref, stat_ref):
     per = TILE // BS
     for t in range(sorted_ref.shape[0] // TILE):
         here = pl.ds(t * TILE, TILE)
-        score_ref[:, here] = dot(mine_ref[...], heads_of(query_ref, per * t, per), NN) * exponent_scale
-        slope_ref[:, here] = dot(mine_ref[:, :LAT], sorted_ref[here, :], NT)
-
-
-def main_kernel(bias_ref, query_ref, sorted_ref, other_ref, own_score, own_slope, mine_score, mine_slope,
+        score = dot(mine_ref[...], heads_of(query_ref, per * t, per), NN) * exponent_scale
+        slope = dot(mine_ref[:, :LAT], sorted_ref[here, :], NT)
+        slope_ref[:, here] = slope
+        expo_ref[:BS, here] = partial_softmax(score[:BS], slope[:BS], stat_ref, 0, here)
+        expo_ref[BS:, here] = partial_softmax(score[BS:], slope[BS:], stat_ref, 3, here)
+
+
+def main_kernel(bias_ref, query_ref, sorted_ref, other_ref, own_expo, own_slope, own_stat, mine_expo, mine_slope, mine_stat,
                 weight_ref, dscore_ref, gother_ref, score_ref, slope_ref):
     tiles = sorted_ref.shape[0] // TILE
     per = TILE // BS
@@ -201,21 +216,35 @@
 
     def softmax(t):
         here = pl.ds(t * TILE, TILE)
+        before = (
+            (own_expo[:, here], own_slope[:, here], own_stat, 0, 0.0),
+            (mine_expo[:BS, here], mine_slope[:BS, here], mine_stat, 0, whole_mine),
+            (mine_expo[BS:, here], mine_slope[BS:, here], mine_stat, 3, part),
+        )
         places = (
-            (own_score[:, here], own_slope[:, here], 0.0),
-            (mine_score[:BS, here], mine_slope[:BS, here], whole_mine),
-            (mine_score[BS:, here], mine_slope[BS:, here], part),
             (score_ref[t % 2, :BS], slope_ref[t % 2, :BS], whole_other),
             (score_ref[t % 2, BS:], slope_ref[t % 2, BS:], part),
         )
-        largest = functools.reduce(jnp.maximum, [jnp.max(s, axis=0, keepdims=True) + b for s, _, b in places])
+        tops = [stat[k : k + 1, here] + b for _, _, stat, k, b in before]
+        largest = functools.reduce(
+            jnp.maximum, tops + [jnp.max(s, axis=0, keepdims=True) + b for s, _, b in places]
+        )
+        factors = [jnp.exp2(top - largest) for top in tops]
         expos = [jnp.exp2(s - (largest - b)) for s, _, b in places]
-        inverse = 1.0 / sum(jnp.sum(e, axis=0, keepdims=True) for e in expos)
-        delta = sum(jnp.sum(e * l, axis=0, keepdims=True) for e, (_, l, _) in zip(expos, places)) * inverse
+        inverse = 1.0 / (
+            sum(stat[k + 1 : k + 2, here] * f for (_, _, stat, k, _), f in zip(before, factors))
+            + sum(jnp.sum(e, axis=0, keepdims=True) for e in expos)
+        )
+        delta = inverse * (
+            sum(stat[k + 2 : k + 3, here] * f for (_, _, stat, k, _), f in zip(before, factors))
+            + sum(jnp.sum(e * l, axis=0, keepdims=True) for e, (_, l, _) in zip(expos, places))
+        )
+        parts = [(e, l, f * inverse) for (e, l, _, _, _), f in zip(before, factors)]
+        parts += [(e, l, inverse) for e, (_, l, _) in zip(expos, places)]
         at = 0
-        for e, (_, l, _) in zip(expos, places):
+        for e, l, factor in parts:
             rows = pl.ds(at, e.shape[0])
-            weight = e * inverse
+            weight = e * factor
             weight_ref[rows, here] = weight.astype(BF)
             dscore_ref[rows, here] = (weight * (l - delta)).astype(BF)
             at += e.shape[0]
@@ -336,14 +365,14 @@
         scratch_shapes=[pltpu.VMEM((half, BS), F32), pltpu.VMEM((WIDTH, BS), BF), pltpu.SemaphoreType.DMA((3,))],
     )(*map(in_hbm, (ancestors, parents.reshape(1, BS), freq, latent.T, grad_out.reshape(total, LAT))))
 
-    fetched = by_core(keys, 1, 2)
-    fetched_half = by_core(keys_half, 3, 3)
-
-    q, g, own_score, own_slope = call(
+    fetched = by_core(keys, EVEN, ODD)
+    fetched_half = by_core(keys_half, BOTH, BOTH)
+
+    q, g, own_expo, own_slope, own_stat = call(
         functools.partial(own_kernel, heads),
         "own",
         [outside] * 2 + [whole()] * 4,
-        [((heads * WIDTH, rows), BF), ((total, LAT), BF), ((BS, total), F32), ((BS, total), F32)],
+        [((heads * WIDTH, rows), BF), ((total, LAT), BF), ((BS, total), F32), ((BS, total), F32), ((8, total), F32)],
         flops=2 * total * BS * 1800,
         scratch_shapes=[pltpu.VMEM((total // 2, LAT), BF), pltpu.SemaphoreType.DMA((total // TILE + 1,))],
     )(in_hbm(query.transpose(1, 2, 0).reshape(heads * WIDTH, rows)), in_hbm(grad_out.reshape(total, LAT)),
@@ -351,18 +380,22 @@
 
     mine, q = lax.optimization_barrier((jnp.concatenate([fetched, fetched_half]), q))
     other = other_core(mine)
-    mine_score, mine_slope = call(
-        mine_kernel, "mine", [whole()] * 3, [((SIDE, total), F32), ((SIDE, total), F32)], flops=2 * total * SIDE * 1280
+    mine_expo, mine_slope, mine_stat = call(
+        mine_kernel,
+        "mine",
+        [whole()] * 3,
+        [((SIDE, total), F32), ((SIDE, total), F32), ((8, total), F32)],
+        flops=2 * total * SIDE * 1280,
     )(q, g, mine)
 
     weight, dscore, gother = call(
         main_kernel,
         "main",
-        [whole()] * 8,
+        [whole()] * 10,
         [((KEYS, total), BF), ((KEYS, total), BF), ((SIDE, WIDTH), BF)],
         flops=2 * total * SIDE * 2560,
         scratch_shapes=[pltpu.VMEM((2, SIDE, TILE), F32), pltpu.VMEM((2, SIDE, TILE), F32)],
-    )(bias, q, g, other, own_score, own_slope, mine_score, mine_slope)
+    )(bias, q, g, other, own_expo, own_slope, own_stat, mine_expo, mine_slope, mine_stat)
 
     gother = other_core(gother)
     (gmine,) = call(
@@ -373,8 +406,8 @@
         flops=2 * total * SIDE * 1280,
     )(weight, dscore, q, g)
     gmine = (gmine + gother.astype(F32)).astype(BF)
-    back = by_core(gmine[:BS], -1, -2)
-    back_half = by_core(gmine[BS:], -3, -3)
+    back = by_core(gmine[:BS], -EVEN, -ODD)
+    back_half = by_core(gmine[BS:], -BOTH, -BOTH)
 
     (gown,) = call(
         functools.partial(grads_kernel, slice(0, BS)),

time: 46.4 us -> 44.9 us (0.968)
  starting transfers between devices: 17.4 us -> 14.1 us
  waiting for transfers between devices: 10.6 us -> 13.3 us
  Pallas kernels: 17.4 us -> 16.6 us
    ppermute x4, waiting for transfers between devices: 6.42 us -> 9.27 us  [by_core(): return lax.ppermute(block, ('tp', 'cp'), route)]
    ppermute x4, starting transfers between devices: 10.3 us -> 8 us  [by_core(): return lax.ppermute(block, ('tp', 'cp'), route)]
    ppermute x4, starting transfers between devices: 3.42 us -> 2.41 us  [other_core(): lax.ppermute(block, 'tp', [(t, t ^ 1) for t in range(lax.axis_size('tp'))])]
    pallas_call x1, Pallas kernels: 4.19 us -> 3.31 us  [on_device(): call(main_kernel, 'main', [whole()] * 10, [((KEYS, total), BF), ((KEYS, t...]
  transfers between devices with their start and end apart: 10 -> 10, of which waited for: 6 -> 6; matrix products, arithmetic and copies ran while one was open for 0% -> 0% of each run, Pallas kernels for 22% -> 23%
where the time goes in v4:
time: 44.9 us; the launch traced here: 44.8 us
  Pallas kernels  16.6 us (37%)
  starting transfers between devices  14.1 us (31%)
  waiting for transfers between devices  13.3 us (30%)
  between operations  0.73 us (2%)
    ppermute x4, waiting for transfers between devices, by_core(): return lax.ppermute(block, ('tp', 'cp'), route)  9.27 us
    ppermute x4, starting transfers between devices, by_core(): return lax.ppermute(block, ('tp', 'cp'), route)  8 us
    ppermute x2, starting transfers between devices, along_x(): return lax.ppermute(block, 'tp', route)  3.69 us
    pallas_call x1, Pallas kernels, on_device(): call(functools.partial(own_kernel, heads), 'own', [outside] * 2 + [whole(...  3.33 us
    pallas_call x1, Pallas kernels, on_device(): call(main_kernel, 'main', [whole()] * 10, [((KEYS, total), BF), ((KEYS, t...  3.31 us
    pallas_call x1, Pallas kernels, on_device(): pl.pallas_call(query_kernel, grid=(total // STEP,), in_specs=[whole()] *...  2.84 us
    ppermute x4, starting transfers between devices, other_core(): lax.ppermute(block, 'tp', [(t, t ^ 1) for t in range(lax.axis_size('tp'))])  2.41 us
    ppermute x4, waiting for transfers between devices, other_core(): lax.ppermute(block, 'tp', [(t, t ^ 1) for t in range(lax.axis_size('tp'))])  2.33 us
  transfers between devices with their start and end apart: 10, of which 6 were waited for; matrix products, arithmetic and copies ran while one was open for 0% of the time, Pallas kernels for 23%

profile of v4, /device:TPU:1, one launch (start us, length us, event | category | flops | bytes accessed | tf_op | source)
XLA Modules:
  0.0 44.8 jit_solution(15669799184695658220)
XLA Ops:
  0.6 2.0 %keys.1 = (bf16[128,576]{1,0:T(8,128)(2,1)S(1)}, bf16[64,576]{1,0:T(8,128)(2,1)S(1)}, f32[64,128]{1,0:T(8,128)S(1)}, f32[128,128]{1,0:T(8,128)S(1)}, f32[8,256]{...) custom-call(s32[1,3]{1,0:T(1,128)} %anc_ref.1, s32[1,128]{1,0:T(1,128)} %bitcast.13, f32[32,128]{1,0:T(8,128)} %constant.2.clone.freq_hbm, ...), custom_call_target="tpu_custom_call" | custom-call | bytes 4718592 | tf_op jit(solution)/shard_map/keys/pallas_call | solution.py:360
  2.7 3.6 %collective-permute-start = (bf16[128,576]{1,0:T(8,128)(2,1)S(1)}, bf16[128,576]{1,0:T(8,128)(2,1)S(1)}, u32[]{:S(2)}, u32[]{:S(2)}) collective-permute-start(bf16[128,576]{1,0:T(8,128)(2,1)S(1)} %get-tuple-element.28.keys_ref), channel_id=1, source_target_pairs={{0,2},{1,3},{2,4},{3,5},{4,6},{5,7},{6,8},{7,9},{8,10},{9,11},{10,... | collective-permute-start | bytes 442376 | tf_op jit(solution)/shard_map/ppermute | solution.py:324
  6.3 0.1 collective-permute-start.1
  6.4 3.3 %own.1 = (bf16[9216,128]{1,0:T(8,128)(2,1)S(1)}, bf16[2048,512]{1,0:T(8,128)(2,1)S(1)}, f32[128,2048]{1,0:T(8,128)S(1)}, f32[128,2048]{1,0:T(8,128)S(1)}, f32[8,2048]{1,0:T(8,128)S(1)}) custom-call(bf16[9216,128]{1,0:T(8,128)(2,1)} %bitcast.10, bf16[2048,512]{1,0:T(8,128)(2,1)} %bitcast.9, bf16[1024,512]{1,0:T(8,128)(2,1)S(1)} %get-tuple-element.30.early_ref, ...), custom_call_target="tpu_custom_call" | custom-call | flops 943718400 | bytes 4718592 | tf_op jit(solution)/shard_map/own/pallas_call | solution.py:371
  9.7 7.5 %collective-permute-done.1 = bf16[64,576]{1,0:T(8,128)(2,1)S(1)} collective-permute-done((bf16[64,576]{1,0:T(8,128)(2,1)S(1)}, bf16[64,576]{1,0:T(8,128)(2,1)S(1)}, u32[]{:S(2)}, u32[]{:S(2)}) %collective-permute-start.1) | collective-permute-done | bytes 73760 | tf_op jit(solution)/shard_map/ppermute | solution.py:324
  17.3 0.0 collective-permute-done
  17.3 1.4 %collective-permute-start.2 = (bf16[192,576]{1,0:T(8,128)(2,1)S(1)}, bf16[192,576]{1,0:T(8,128)(2,1)S(1)}, u32[]{:S(2)}, u32[]{:S(2)}) collective-permute-start(bf16[192,576]{1,0:T(8,128)(2,1)S(1)} %pad_maximum_fusion.mine_ref), channel_id=1, source_target_pairs={{0,32},{32,0},{64,96},{96,64},{128,160},{160,128},{192,224},{224,1... | collective-permute-start | bytes 663560 | tf_op jit(solution)/shard_map/ppermute | solution.py:331
  18.7 1.4 %mine.1 = (f32[192,2048]{1,0:T(8,128)S(1)}, f32[192,2048]{1,0:T(8,128)S(1)}, f32[8,2048]{1,0:T(8,128)S(1)}) custom-call(bf16[9216,128]{1,0:T(8,128)(2,1)S(1)} %get-tuple-element.34.query_ref, bf16[2048,512]{1,0:T(8,128)(2,1)S(1)} %get-tuple-element.35.sorted_ref, bf16[192,576]{1,0:T(8,128)(2,1)S(1)} %pad_maximum_fusion.mine_ref), custom_call_target="tpu_custom_call" | custom-call | flops 1006632960 | bytes 4718592 | tf_op jit(solution)/shard_map/mine/pallas_call | solution.py:383
  20.1 0.0 collective-permute-done.2.other_ref
  20.1 3.3 %main.1 = (bf16[512,2048]{1,0:T(8,128)(2,1)S(1)}, bf16[512,2048]{1,0:T(8,128)(2,1)S(1)}, bf16[192,576]{1,0:T(8,128)(2,1)S(1)}) custom-call(f32[8,256]{1,0:T(8,128)S(1)} %get-tuple-element.27.bias_ref, bf16[9216,128]{1,0:T(8,128)(2,1)S(1)} %get-tuple-element.34.query_ref, bf16[2048,512]{1,0:T(8,128)(2,1)S(1)} %get-tuple-element.35.sorted_ref, ...), custom_call_target="tpu_custom_call" | custom-call | flops 2013265920 | bytes 4718592 | tf_op jit(solution)/shard_map/main/pallas_call | solution.py:391
  23.5 0.2 collective-permute-start.3
  23.6 1.4 %grads.1 = f32[192,576]{1,0:T(8,128)S(1)} custom-call(bf16[512,2048]{1,0:T(8,128)(2,1)S(1)} %get-tuple-element.43.weight_ref, bf16[512,2048]{1,0:T(8,128)(2,1)S(1)} %get-tuple-element.48.dscore_ref, bf16[9216,128]{1,0:T(8,128)(2,1)S(1)} %get-tuple-element.34.query_ref, bf16[2048,512]{1,0:T(8,128)(2,1)S(1)} %get-tuple-element.35.sorted_ref), custom_call_target="tpu_custom_call" | custom-call | flops 1006632960 | bytes 4718592 | tf_op jit(solution)/shard_map/grads/pallas_call | solution.py:401
  25.0 0.0 collective-permute-done.3
  25.1 1.0 %collective-permute-start.4 = (bf16[128,576]{1,0:T(8,128)(2,1)S(1)}, bf16[128,576]{1,0:T(8,128)(2,1)S(1)}, u32[]{:S(2)}, u32[]{:S(2)}) collective-permute-start(bf16[128,576]{1,0:T(8,128)(2,1)S(1)} %slice.8), channel_id=1, source_target_pairs={{0,30},{1,31},{2,0},{3,1},{4,2},{5,3},{6,4},{7,5},{8,6},{9,7},{10,... | collective-permute-start | bytes 442376 | tf_op jit(solution)/shard_map/ppermute | solution.py:324
  26.2 3.2 %collective-permute-start.5 = (bf16[64,576]{1,0:T(8,128)(2,1)S(1)}, bf16[64,576]{1,0:T(8,128)(2,1)S(1)}, u32[]{:S(2)}, u32[]{:S(2)}) collective-permute-start(bf16[64,576]{1,0:T(8,128)(2,1)S(1)} %slice.9), channel_id=1, source_target_pairs={{0,31},{1,0},{2,1},{3,2},{4,3},{5,4},{6,5},{7,6},{8,7},{9,8},{10,9... | collective-permute-start | bytes 221192 | tf_op jit(solution)/shard_map/ppermute | solution.py:324
  29.4 1.2 %gown.1.gown_ref = f32[128,576]{1,0:T(8,128)S(1)} custom-call(bf16[512,2048]{1,0:T(8,128)(2,1)S(1)} %get-tuple-element.43.weight_ref, bf16[512,2048]{1,0:T(8,128)(2,1)S(1)} %get-tuple-element.48.dscore_ref, bf16[9216,128]{1,0:T(8,128)(2,1)S(1)} %get-tuple-element.34.query_ref, bf16[2048,512]{1,0:T(8,128)(2,1)S(1)} %get-tuple-element.35.sorted_ref), custom_call_target="tpu_custom_call" | custom-call | flops 671088640 | bytes 4718592 | tf_op jit(solution)/shard_map/gown/pallas_call | solution.py:412
  30.6 1.0 %collective-permute-done.5.half_ref = bf16[64,576]{1,0:T(8,128)(2,1)S(1)} collective-permute-done((bf16[64,576]{1,0:T(8,128)(2,1)S(1)}, bf16[64,576]{1,0:T(8,128)(2,1)S(1)}, u32[]{:S(2)}, u32[]{:S(2)}) %collective-permute-start.5) | collective-permute-done | bytes 73760 | tf_op jit(solution)/shard_map/ppermute | solution.py:324
  31.6 0.8 %collective-permute-done.4.back_ref = bf16[128,576]{1,0:T(8,128)(2,1)S(1)} collective-permute-done((bf16[128,576]{1,0:T(8,128)(2,1)S(1)}, bf16[128,576]{1,0:T(8,128)(2,1)S(1)}, u32[]{:S(2)}, u32[]{:S(2)}) %collective-permute-start.4) | collective-permute-done | bytes 147488 | tf_op jit(solution)/shard_map/ppermute | solution.py:324
  32.4 0.1 device.1.device_ref
  32.4 0.3 collective-permute-start.6
  32.7 1.2 %collective-permute-done.6.other_ref = bf16[128,576]{1,0:T(8,128)(2,1)S(1)} collective-permute-done((bf16[128,576]{1,0:T(8,128)(2,1)S(1)}, bf16[128,576]{1,0:T(8,128)(2,1)S(1)}, u32[]{:S(2)}, u32[]{:S(2)}) %collective-permute-start.6) | collective-permute-done | bytes 147488 | tf_op jit(solution)/shard_map/ppermute | solution.py:331
  33.9 0.1 chip.1
  34.0 2.8 %collective-permute-start.8 = (bf16[64,576]{1,0:T(8,128)(2,1)S(1)}, bf16[64,576]{1,0:T(8,128)(2,1)S(1)}, u32[]{:S(2)}, u32[]{:S(2)}) collective-permute-start(bf16[64,576]{1,0:T(8,128)(2,1)S(1)} %get-tuple-element.51), channel_id=1, source_target_pairs={{0,128},{32,160},{64,192},{96,224},{128,0},{160,32},{192,64},{224,... | collective-permute-start | bytes 221192 | tf_op jit(solution)/shard_map/ppermute | solution.py:336
  36.8 0.9 %collective-permute-start.7 = (bf16[128,576]{1,0:T(8,128)(2,1)S(1)}, bf16[128,576]{1,0:T(8,128)(2,1)S(1)}, u32[]{:S(2)}, u32[]{:S(2)}) collective-permute-start(bf16[128,576]{1,0:T(8,128)(2,1)S(1)} %get-tuple-element.47.chip_ref), channel_id=1, source_target_pairs={{0,64},{32,224},{64,0},{96,160},{128,192},{160,96},{192,128},{224,... | collective-permute-start | bytes 442376 | tf_op jit(solution)/shard_map/ppermute | solution.py:336
  37.7 2.8 %dquery.1 = bf16[16,576,128]{2,1,0:T(8,128)(2,1)} custom-call(bf16[512,2048]{1,0:T(8,128)(2,1)S(1)} %get-tuple-element.48.dscore_ref, bf16[128,576]{1,0:T(8,128)(2,1)S(1)} %get-tuple-element.28.keys_ref, bf16[192,576]{1,0:T(8,128)(2,1)S(1)} %pad_maximum_fusion.mine_ref, bf16[192,576]{1,0:T(8,128)(2,1)S(1)} %collective-permute-done.2.other_ref, ...), custom_call_target="tpu_custom_call" | custom-call | flops 1610612736 | bytes 4718592 | tf_op jit(solution)/shard_map/dquery/pallas_call | solution.py:432
  40.5 1.7 %collective-permute-done.7.near_ref = bf16[128,576]{1,0:T(8,128)(2,1)S(1)} collective-permute-done((bf16[128,576]{1,0:T(8,128)(2,1)S(1)}, bf16[128,576]{1,0:T(8,128)(2,1)S(1)}, u32[]{:S(2)}, u32[]{:S(2)}) %collective-permute-start.7) | collective-permute-done | bytes 147488 | tf_op jit(solution)/shard_map/ppermute | solution.py:336
  42.2 0.0 collective-permute-done.8.far_ref
  42.2 0.5 %collective-permute-start.9 = (bf16[192,576]{1,0:T(8,128)(2,1)S(1)}, bf16[192,576]{1,0:T(8,128)(2,1)S(1)}, u32[]{:S(2)}, u32[]{:S(2)}) collective-permute-start(bf16[192,576]{1,0:T(8,128)(2,1)S(1)} %pad_maximum_fusion.1), channel_id=1, source_target_pairs={{0,32},{32,0},{64,96},{96,64},{128,160},{160,128},{192,224},{224,1... | collective-permute-start | bytes 663560 | tf_op jit(solution)/shard_map/ppermute | solution.py:331
  42.8 1.1 %collective-permute-done.9.rest_ref = bf16[192,576]{1,0:T(8,128)(2,1)S(1)} collective-permute-done((bf16[192,576]{1,0:T(8,128)(2,1)S(1)}, bf16[192,576]{1,0:T(8,128)(2,1)S(1)}, u32[]{:S(2)}, u32[]{:S(2)}) %collective-permute-start.9) | collective-permute-done | bytes 221216 | tf_op jit(solution)/shard_map/ppermute | solution.py:331
  43.9 0.9 %finish.1 = bf16[576,128]{1,0:T(8,128)(2,1)} custom-call(bf16[128,576]{1,0:T(8,128)(2,1)S(1)} %get-tuple-element.47.chip_ref, bf16[128,576]{1,0:T(8,128)(2,1)S(1)} %collective-permute-done.7.near_ref, bf16[64,576]{1,0:T(8,128)(2,1)S(1)} %collective-permute-done.8.far_ref, bf16[192,576]{1,0:T(8,128)(2,1)S(1)} %collective-permute-done.9.rest_ref, ...), custom_call_target="tpu_custom_call" | custom-call | tf_op jit(solution)/shard_map/finish/pallas_call | solution.py:445
  (5 shorter events, 0.1 us)
Async XLA Ops:
  2.7 14.6 %collective-permute-start = (bf16[128,576]{1,0:T(8,128)(2,1)S(1)}, bf16[128,576]{1,0:T(8,128)(2,1)S(1)}, u32[]{:S(2)}, u32[]{:S(2)}) collective-permute-start(bf16[128,576]{1,0:T(8,128)(2,1)S(1)} %get-tuple-element.28.keys_ref), channel_id=1, source_target_pairs={{0,2},{1,3},{2,4},{3,5},{4,6},{5,7},{6,8},{7,9},{8,10},{9,11},{10,... | collective-permute-start | bytes 442376 | tf_op jit(solution)/shard_map/ppermute | solution.py:324
  6.3 11.0 %collective-permute-start.1 = (bf16[64,576]{1,0:T(8,128)(2,1)S(1)}, bf16[64,576]{1,0:T(8,128)(2,1)S(1)}, u32[]{:S(2)}, u32[]{:S(2)}) collective-permute-start(bf16[64,576]{1,0:T(8,128)(2,1)S(1)} %get-tuple-element.29), channel_id=1, source_target_pairs={{0,1},{1,2},{2,3},{3,4},{4,5},{5,6},{6,7},{7,8},{8,9},{9,10},{10,1... | collective-permute-start | bytes 221192 | tf_op jit(solution)/shard_map/ppermute | solution.py:324
  17.3 2.8 %collective-permute-start.2 = (bf16[192,576]{1,0:T(8,128)(2,1)S(1)}, bf16[192,576]{1,0:T(8,128)(2,1)S(1)}, u32[]{:S(2)}, u32[]{:S(2)}) collective-permute-start(bf16[192,576]{1,0:T(8,128)(2,1)S(1)} %pad_maximum_fusion.mine_ref), channel_id=1, source_target_pairs={{0,32},{32,0},{64,96},{96,64},{128,160},{160,128},{192,224},{224,1... | collective-permute-start | bytes 663560 | tf_op jit(solution)/shard_map/ppermute | solution.py:331
  23.5 1.6 %collective-permute-start.3 = (bf16[192,576]{1,0:T(8,128)(2,1)S(1)}, bf16[192,576]{1,0:T(8,128)(2,1)S(1)}, u32[]{:S(2)}, u32[]{:S(2)}) collective-permute-start(bf16[192,576]{1,0:T(8,128)(2,1)S(1)} %get-tuple-element.45), channel_id=1, source_target_pairs={{0,32},{32,0},{64,96},{96,64},{128,160},{160,128},{192,224},{224,1... | collective-permute-start | bytes 663560 | tf_op jit(solution)/shard_map/ppermute | solution.py:331
  25.1 7.2 %collective-permute-start.4 = (bf16[128,576]{1,0:T(8,128)(2,1)S(1)}, bf16[128,576]{1,0:T(8,128)(2,1)S(1)}, u32[]{:S(2)}, u32[]{:S(2)}) collective-permute-start(bf16[128,576]{1,0:T(8,128)(2,1)S(1)} %slice.8), channel_id=1, source_target_pairs={{0,30},{1,31},{2,0},{3,1},{4,2},{5,3},{6,4},{7,5},{8,6},{9,7},{10,... | collective-permute-start | bytes 442376 | tf_op jit(solution)/shard_map/ppermute | solution.py:324
  26.2 5.4 %collective-permute-start.5 = (bf16[64,576]{1,0:T(8,128)(2,1)S(1)}, bf16[64,576]{1,0:T(8,128)(2,1)S(1)}, u32[]{:S(2)}, u32[]{:S(2)}) collective-permute-start(bf16[64,576]{1,0:T(8,128)(2,1)S(1)} %slice.9), channel_id=1, source_target_pairs={{0,31},{1,0},{2,1},{3,2},{4,3},{5,4},{6,5},{7,6},{8,7},{9,8},{10,9... | collective-permute-start | bytes 221192 | tf_op jit(solution)/shard_map/ppermute | solution.py:324
  32.4 1.5 %collective-permute-start.6 = (bf16[128,576]{1,0:T(8,128)(2,1)S(1)}, bf16[128,576]{1,0:T(8,128)(2,1)S(1)}, u32[]{:S(2)}, u32[]{:S(2)}) collective-permute-start(bf16[128,576]{1,0:T(8,128)(2,1)S(1)} %device.1.device_ref), channel_id=1, source_target_pairs={{0,32},{32,0},{64,96},{96,64},{128,160},{160,128},{192,224},{224,1... | collective-permute-start | bytes 442376 | tf_op jit(solution)/shard_map/ppermute | solution.py:331
  34.0 8.2 %collective-permute-start.8 = (bf16[64,576]{1,0:T(8,128)(2,1)S(1)}, bf16[64,576]{1,0:T(8,128)(2,1)S(1)}, u32[]{:S(2)}, u32[]{:S(2)}) collective-permute-start(bf16[64,576]{1,0:T(8,128)(2,1)S(1)} %get-tuple-element.51), channel_id=1, source_target_pairs={{0,128},{32,160},{64,192},{96,224},{128,0},{160,32},{192,64},{224,... | collective-permute-start | bytes 221192 | tf_op jit(solution)/shard_map/ppermute | solution.py:336
  36.8 5.4 %collective-permute-start.7 = (bf16[128,576]{1,0:T(8,128)(2,1)S(1)}, bf16[128,576]{1,0:T(8,128)(2,1)S(1)}, u32[]{:S(2)}, u32[]{:S(2)}) collective-permute-start(bf16[128,576]{1,0:T(8,128)(2,1)S(1)} %get-tuple-element.47.chip_ref), channel_id=1, source_target_pairs={{0,64},{32,224},{64,0},{96,160},{128,192},{160,96},{192,128},{224,... | collective-permute-start | bytes 442376 | tf_op jit(solution)/shard_map/ppermute | solution.py:336
  42.2 1.7 %collective-permute-start.9 = (bf16[192,576]{1,0:T(8,128)(2,1)S(1)}, bf16[192,576]{1,0:T(8,128)(2,1)S(1)}, u32[]{:S(2)}, u32[]{:S(2)}) collective-permute-start(bf16[192,576]{1,0:T(8,128)(2,1)S(1)} %pad_maximum_fusion.1), channel_id=1, source_target_pairs={{0,32},{32,0},{64,96},{96,64},{128,160},{160,128},{192,224},{224,1... | collective-permute-start | bytes 663560 | tf_op jit(solution)/shard_map/ppermute | solution.py:331

commit v5 on v4

--- a/solution.py
+++ b/solution.py
@@ -149,8 +149,8 @@
     per = TILE // BS
     pieces = heads // per
     pair = per * WIDTH
-    late = late_ref.shape[0]
-    grad_copy = pltpu.make_async_copy(grad_hbm.at[pl.ds(late, late)], late_ref, sems.at[pieces])
+    early, late = early_ref.shape[0], late_ref.shape[0]
+    grad_copy = pltpu.make_async_copy(grad_hbm.at[pl.ds(early, late)], late_ref, sems.at[pieces])
     grad_copy.start()
     copies = []
     for t in range(pieces):
@@ -165,9 +165,9 @@
     table = table_ref[...]
     seen = jnp.concatenate([closure_ref[...]] * per, axis=1) > 0.5
     for t in range(pieces):
-        if t == pieces // 2:
+        if t * TILE == early:
             grad_copy.wait()
-        source, at = (early_ref, t * TILE) if t < pieces // 2 else (late_ref, t * TILE - late)
+        source, at = (early_ref, t * TILE) if t * TILE < early else (late_ref, t * TILE - early)
         chunk = dot(order, source[at : at + TILE, :], NN).astype(BF)
         for h in range(heads):
             sorted_ref[pl.ds(h * BS + t * rows, rows), :] = chunk[h * rows : (h + 1) * rows]
@@ -192,15 +192,22 @@
     return turned[:, :LAT] + plain, turned[:, LAT:]
 
 
+def has_earlier():
+    return lax.axis_index("cp") > 0
+
+
 def mine_kernel(query_ref, sorted_ref, mine_ref, expo_ref, slope_ref, stat_ref):
     per = TILE // BS
-    for t in range(sorted_ref.shape[0] // TILE):
-        here = pl.ds(t * TILE, TILE)
-        score = dot(mine_ref[...], heads_of(query_ref, per * t, per), NN) * exponent_scale
-        slope = dot(mine_ref[:, :LAT], sorted_ref[here, :], NT)
-        slope_ref[:, here] = slope
-        expo_ref[:BS, here] = partial_softmax(score[:BS], slope[:BS], stat_ref, 0, here)
-        expo_ref[BS:, here] = partial_softmax(score[BS:], slope[BS:], stat_ref, 3, here)
+
+    @pl.when(has_earlier())
+    def _():
+        for t in range(sorted_ref.shape[0] // TILE):
+            here = pl.ds(t * TILE, TILE)
+            score = dot(mine_ref[...], heads_of(query_ref, per * t, per), NN) * exponent_scale
+            slope = dot(mine_ref[:, :LAT], sorted_ref[here, :], NT)
+            slope_ref[:, here] = slope
+            expo_ref[:BS, here] = partial_softmax(score[:BS], slope[:BS], stat_ref, 0, here)
+            expo_ref[BS:, here] = partial_softmax(score[BS:], slope[BS:], stat_ref, 3, here)
 
 
 def main_kernel(bias_ref, query_ref, sorted_ref, other_ref, own_expo, own_slope, own_stat, mine_expo, mine_slope, mine_stat,
@@ -214,7 +221,7 @@
         score_ref[t % 2] = dot(other_ref[...], heads_of(query_ref, per * t, per), NN) * exponent_scale
         slope_ref[t % 2] = dot(other_ref[:, :LAT], sorted_ref[here, :], NT)
 
-    def softmax(t):
+    def softmax(t, remote):
         here = pl.ds(t * TILE, TILE)
         before = (
             (own_expo[:, here], own_slope[:, here], own_stat, 0, 0.0),
@@ -225,6 +232,8 @@
             (score_ref[t % 2, :BS], slope_ref[t % 2, :BS], whole_other),
             (score_ref[t % 2, BS:], slope_ref[t % 2, BS:], part),
         )
+        if not remote:
+            before, places = before[:1], ()
         tops = [stat[k : k + 1, here] + b for _, _, stat, k, b in before]
         largest = functools.reduce(
             jnp.maximum, tops + [jnp.max(s, axis=0, keepdims=True) + b for s, _, b in places]
@@ -249,14 +258,34 @@
             dscore_ref[rows, here] = (weight * (l - delta)).astype(BF)
             at += e.shape[0]
 
-    products(0)
-    for t in range(tiles):
-        if t + 1 < tiles:
-            products(t + 1)
-        softmax(t)
-    lead, tail = key_grads(pl.ds(BS + SIDE, SIDE), weight_ref, dscore_ref, query_ref, sorted_ref)
-    gother_ref[:, :LAT] = lead.astype(BF)
-    gother_ref[:, LAT:] = tail.astype(BF)
+    @pl.when(has_earlier())
+    def _():
+        products(0)
+        for t in range(tiles):
+            if t + 1 < tiles:
+                products(t + 1)
+            softmax(t, True)
+        lead, tail = key_grads(pl.ds(BS + SIDE, SIDE), weight_ref, dscore_ref, query_ref, sorted_ref)
+        gother_ref[:, :LAT] = lead.astype(BF)
+        gother_ref[:, LAT:] = tail.astype(BF)
+
+    @pl.when(jnp.logical_not(has_earlier()))
+    def _():
+        for t in range(tiles):
+            softmax(t, False)
+        weight_ref[BS:, :] = jnp.zeros((REMOTE, weight_ref.shape[1]), BF)
+        dscore_ref[BS:, :] = jnp.zeros((REMOTE, dscore_ref.shape[1]), BF)
+        gother_ref[...] = jnp.zeros_like(gother_ref)
+
+
+def mine_grads_kernel(weight_ref, dscore_ref, query_ref, sorted_ref, out_ref):
+    @pl.when(has_earlier())
+    def _():
+        grads_kernel(slice(BS, BS + SIDE), weight_ref, dscore_ref, query_ref, sorted_ref, out_ref)
+
+    @pl.when(jnp.logical_not(has_earlier()))
+    def _():
+        out_ref[...] = jnp.zeros_like(out_ref)
 
 
 def grads_kernel(rows, weight_ref, dscore_ref, query_ref, sorted_ref, out_ref):
@@ -361,7 +390,7 @@
         keys_kernel,
         "keys",
         [scalars(), whole(), outside, outside, outside],
-        [((BS, WIDTH), BF), ((HALF, WIDTH), BF), ((ROPE, BS), F32), ((BS, BS), F32), ((8, TILE), F32), ((total // 2, LAT), BF)],
+        [((BS, WIDTH), BF), ((HALF, WIDTH), BF), ((ROPE, BS), F32), ((BS, BS), F32), ((8, TILE), F32), ((total // 4, LAT), BF)],
         scratch_shapes=[pltpu.VMEM((half, BS), F32), pltpu.VMEM((WIDTH, BS), BF), pltpu.SemaphoreType.DMA((3,))],
     )(*map(in_hbm, (ancestors, parents.reshape(1, BS), freq, latent.T, grad_out.reshape(total, LAT))))
 
@@ -374,7 +403,7 @@
         [outside] * 2 + [whole()] * 4,
         [((heads * WIDTH, rows), BF), ((total, LAT), BF), ((BS, total), F32), ((BS, total), F32), ((8, total), F32)],
         flops=2 * total * BS * 1800,
-        scratch_shapes=[pltpu.VMEM((total // 2, LAT), BF), pltpu.SemaphoreType.DMA((total // TILE + 1,))],
+        scratch_shapes=[pltpu.VMEM((total - total // 4, LAT), BF), pltpu.SemaphoreType.DMA((total // TILE + 1,))],
     )(in_hbm(query.transpose(1, 2, 0).reshape(heads * WIDTH, rows)), in_hbm(grad_out.reshape(total, LAT)),
       early, keys, table, closure)
 
@@ -399,7 +428,7 @@
 
     gother = other_core(gother)
     (gmine,) = call(
-        functools.partial(grads_kernel, slice(BS, BS + SIDE)),
+        mine_grads_kernel,
         "grads",
         [whole()] * 4,
         [((SIDE, WIDTH), F32)],

time: 44.9 us -> 44.6 us (level)
  Pallas kernels: 16.6 us -> 10.9 us
  starting transfers between devices: 14.1 us -> 18.3 us
  waiting for transfers between devices: 13.3 us -> 14.5 us
    ppermute x4, starting transfers between devices: 8 us -> 11.2 us  [by_core(): return lax.ppermute(block, ('tp', 'cp'), route)]
    pallas_call x1, Pallas kernels: 3.31 us -> 0.43 us  [on_device(): call(main_kernel, 'main', [whole()] * 10, [((KEYS, total), BF), ((KEYS, t...]
    ppermute x4, waiting for transfers between devices: 2.33 us -> 4.41 us  [other_core(): lax.ppermute(block, 'tp', [(t, t ^ 1) for t in range(lax.axis_size('tp'))])]
    pallas_call x1, Pallas kernels: 1.41 us -> 0.01 us  [on_device(): call(mine_kernel, 'mine', [whole()] * 3, [((SIDE, total), F32), ((SIDE, t...]
    pallas_call x1, Pallas kernels: 1.41 us -> 0.03 us  [on_device(): call(mine_grads_kernel, 'grads', [whole()] * 4, [((SIDE, WIDTH), F32)], f...]
    ppermute x4, starting transfers between devices: 2.41 us -> 3.37 us  [other_core(): lax.ppermute(block, 'tp', [(t, t ^ 1) for t in range(lax.axis_size('tp'))])]
    ppermute x4, waiting for transfers between devices: 9.27 us -> 8.4 us  [by_core(): return lax.ppermute(block, ('tp', 'cp'), route)]
  transfers between devices with their start and end apart: 10 -> 10, of which waited for: 6 -> 7; matrix products, arithmetic and copies ran while one was open for 0% -> 0% of each run, Pallas kernels for 23% -> 17%
where the time goes in v5:
time: 44.6 us; the launch traced here: 44.5 us
  starting transfers between devices  18.3 us (41%)
  waiting for transfers between devices  14.5 us (33%)
  Pallas kernels  10.9 us (24%)
  between operations  0.71 us (2%)
    ppermute x4, starting transfers between devices, by_core(): return lax.ppermute(block, ('tp', 'cp'), route)  11.2 us
    ppermute x4, waiting for transfers between devices, by_core(): return lax.ppermute(block, ('tp', 'cp'), route)  8.4 us
    ppermute x4, waiting for transfers between devices, other_core(): lax.ppermute(block, 'tp', [(t, t ^ 1) for t in range(lax.axis_size('tp'))])  4.41 us
    ppermute x2, starting transfers between devices, along_x(): return lax.ppermute(block, 'tp', route)  3.69 us
    pallas_call x1, Pallas kernels, on_device(): call(functools.partial(own_kernel, heads), 'own', [outside] * 2 + [whole(...  3.45 us
    ppermute x4, starting transfers between devices, other_core(): lax.ppermute(block, 'tp', [(t, t ^ 1) for t in range(lax.axis_size('tp'))])  3.37 us
    pallas_call x1, Pallas kernels, on_device(): pl.pallas_call(query_kernel, grid=(total // STEP,), in_specs=[whole()] *...  2.84 us
    pallas_call x1, Pallas kernels, on_device(): call(keys_kernel, 'keys', [scalars(), whole(), outside, outside, outside]...  1.84 us
  transfers between devices with their start and end apart: 10, of which 7 were waited for; matrix products, arithmetic and copies ran while one was open for 0% of the time, Pallas kernels for 17%

profile of v5, /device:TPU:1, one launch (start us, length us, event | category | flops | bytes accessed | tf_op | source)
XLA Modules:
  0.0 44.5 jit_solution(2929382269606522917)
XLA Ops:
  0.6 1.8 %keys.1 = (bf16[128,576]{1,0:T(8,128)(2,1)S(1)}, bf16[64,576]{1,0:T(8,128)(2,1)S(1)}, f32[64,128]{1,0:T(8,128)S(1)}, f32[128,128]{1,0:T(8,128)S(1)}, f32[8,256]{1,0:T(8,128)S(1)}, /*index=5*/bf16[512,512]{1,0:T(8,128)(2,1)S(1)}) custom-call(s32[1,3]{1,0:T(1,128)} %anc_ref.1, s32[1,128]{1,0:T(1,128)} %bitcast.13, f32[32,128]{1,0:T(8,128)} %constant.2.clone.freq_hbm, ...), custom_call_target="tpu_custom_call" | custom-call | bytes 4718592 | tf_op jit(solution)/shard_map/keys/pallas_call | solution.py:389
  2.5 3.6 %collective-permute-start = (bf16[128,576]{1,0:T(8,128)(2,1)S(1)}, bf16[128,576]{1,0:T(8,128)(2,1)S(1)}, u32[]{:S(2)}, u32[]{:S(2)}) collective-permute-start(bf16[128,576]{1,0:T(8,128)(2,1)S(1)} %get-tuple-element.28.keys_ref), channel_id=1, source_target_pairs={{0,2},{1,3},{2,4},{3,5},{4,6},{5,7},{6,8},{7,9},{8,10},{9,11},{10,... | collective-permute-start | bytes 442376 | tf_op jit(solution)/shard_map/ppermute | solution.py:353
  6.1 0.1 collective-permute-start.1
  6.2 3.5 %own.1 = (bf16[9216,128]{1,0:T(8,128)(2,1)S(1)}, bf16[2048,512]{1,0:T(8,128)(2,1)S(1)}, f32[128,2048]{1,0:T(8,128)S(1)}, f32[128,2048]{1,0:T(8,128)S(1)}, f32[8,2048]{1,0:T(8,128)S(1)}) custom-call(bf16[9216,128]{1,0:T(8,128)(2,1)} %bitcast.10, bf16[2048,512]{1,0:T(8,128)(2,1)} %bitcast.9, bf16[512,512]{1,0:T(8,128)(2,1)S(1)} %get-tuple-element.30.early_ref, ...), custom_call_target="tpu_custom_call" | custom-call | flops 943718400 | bytes 4718592 | tf_op jit(solution)/shard_map/own/pallas_call | solution.py:400
  9.7 7.4 %collective-permute-done.1 = bf16[64,576]{1,0:T(8,128)(2,1)S(1)} collective-permute-done((bf16[64,576]{1,0:T(8,128)(2,1)S(1)}, bf16[64,576]{1,0:T(8,128)(2,1)S(1)}, u32[]{:S(2)}, u32[]{:S(2)}) %collective-permute-start.1) | collective-permute-done | bytes 73760 | tf_op jit(solution)/shard_map/ppermute | solution.py:353
  17.1 0.0 collective-permute-done
  17.1 1.4 %collective-permute-start.2 = (bf16[192,576]{1,0:T(8,128)(2,1)S(1)}, bf16[192,576]{1,0:T(8,128)(2,1)S(1)}, u32[]{:S(2)}, u32[]{:S(2)}) collective-permute-start(bf16[192,576]{1,0:T(8,128)(2,1)S(1)} %pad_maximum_fusion.mine_ref), channel_id=1, source_target_pairs={{0,32},{32,0},{64,96},{96,64},{128,160},{160,128},{192,224},{224,1... | collective-permute-start | bytes 663560 | tf_op jit(solution)/shard_map/ppermute | solution.py:360
  18.5 1.1 %collective-permute-done.2.other_ref = bf16[192,576]{1,0:T(8,128)(2,1)S(1)} collective-permute-done((bf16[192,576]{1,0:T(8,128)(2,1)S(1)}, bf16[192,576]{1,0:T(8,128)(2,1)S(1)}, u32[]{:S(2)}, u32[]{:S(2)}) %collective-permute-start.2) | collective-permute-done | bytes 221216 | tf_op jit(solution)/shard_map/ppermute | solution.py:360
  19.7 0.4 main.1
  20.1 0.5 %collective-permute-start.3 = (bf16[192,576]{1,0:T(8,128)(2,1)S(1)}, bf16[192,576]{1,0:T(8,128)(2,1)S(1)}, u32[]{:S(2)}, u32[]{:S(2)}) collective-permute-start(bf16[192,576]{1,0:T(8,128)(2,1)S(1)} %get-tuple-element.45), channel_id=1, source_target_pairs={{0,32},{32,0},{64,96},{96,64},{128,160},{160,128},{192,224},{224,1... | collective-permute-start | bytes 663560 | tf_op jit(solution)/shard_map/ppermute | solution.py:360
  20.6 1.1 %collective-permute-done.3 = bf16[192,576]{1,0:T(8,128)(2,1)S(1)} collective-permute-done((bf16[192,576]{1,0:T(8,128)(2,1)S(1)}, bf16[192,576]{1,0:T(8,128)(2,1)S(1)}, u32[]{:S(2)}, u32[]{:S(2)}) %collective-permute-start.3) | collective-permute-done | bytes 221216 | tf_op jit(solution)/shard_map/ppermute | solution.py:360
  21.7 0.1 add_convert_fusion
  21.8 4.3 %collective-permute-start.4 = (bf16[128,576]{1,0:T(8,128)(2,1)S(1)}, bf16[128,576]{1,0:T(8,128)(2,1)S(1)}, u32[]{:S(2)}, u32[]{:S(2)}) collective-permute-start(bf16[128,576]{1,0:T(8,128)(2,1)S(1)} %slice.8), channel_id=1, source_target_pairs={{0,30},{1,31},{2,0},{3,1},{4,2},{5,3},{6,4},{7,5},{8,6},{9,7},{10,... | collective-permute-start | bytes 442376 | tf_op jit(solution)/shard_map/ppermute | solution.py:353
  26.1 3.2 %collective-permute-start.5 = (bf16[64,576]{1,0:T(8,128)(2,1)S(1)}, bf16[64,576]{1,0:T(8,128)(2,1)S(1)}, u32[]{:S(2)}, u32[]{:S(2)}) collective-permute-start(bf16[64,576]{1,0:T(8,128)(2,1)S(1)} %slice.9), channel_id=1, source_target_pairs={{0,31},{1,0},{2,1},{3,2},{4,3},{5,4},{6,5},{7,6},{8,7},{9,8},{10,9... | collective-permute-start | bytes 221192 | tf_op jit(solution)/shard_map/ppermute | solution.py:353
  29.3 1.2 %gown.1.gown_ref = f32[128,576]{1,0:T(8,128)S(1)} custom-call(bf16[512,2048]{1,0:T(8,128)(2,1)S(1)} %get-tuple-element.43.weight_ref, bf16[512,2048]{1,0:T(8,128)(2,1)S(1)} %get-tuple-element.48.dscore_ref, bf16[9216,128]{1,0:T(8,128)(2,1)S(1)} %get-tuple-element.34.query_ref, bf16[2048,512]{1,0:T(8,128)(2,1)S(1)} %get-tuple-element.35.sorted_ref), custom_call_target="tpu_custom_call" | custom-call | flops 671088640 | bytes 4718592 | tf_op jit(solution)/shard_map/gown/pallas_call | solution.py:441
  30.5 1.0 %collective-permute-done.5.half_ref = bf16[64,576]{1,0:T(8,128)(2,1)S(1)} collective-permute-done((bf16[64,576]{1,0:T(8,128)(2,1)S(1)}, bf16[64,576]{1,0:T(8,128)(2,1)S(1)}, u32[]{:S(2)}, u32[]{:S(2)}) %collective-permute-start.5) | collective-permute-done | bytes 73760 | tf_op jit(solution)/shard_map/ppermute | solution.py:353
  31.5 0.0 collective-permute-done.4.back_ref
  31.5 0.1 device.1.device_ref
  31.6 0.8 %collective-permute-start.6 = (bf16[128,576]{1,0:T(8,128)(2,1)S(1)}, bf16[128,576]{1,0:T(8,128)(2,1)S(1)}, u32[]{:S(2)}, u32[]{:S(2)}) collective-permute-start(bf16[128,576]{1,0:T(8,128)(2,1)S(1)} %device.1.device_ref), channel_id=1, source_target_pairs={{0,32},{32,0},{64,96},{96,64},{128,160},{160,128},{192,224},{224,1... | collective-permute-start | bytes 442376 | tf_op jit(solution)/shard_map/ppermute | solution.py:360
  32.4 1.0 %collective-permute-done.6.other_ref = bf16[128,576]{1,0:T(8,128)(2,1)S(1)} collective-permute-done((bf16[128,576]{1,0:T(8,128)(2,1)S(1)}, bf16[128,576]{1,0:T(8,128)(2,1)S(1)}, u32[]{:S(2)}, u32[]{:S(2)}) %collective-permute-start.6) | collective-permute-done | bytes 147488 | tf_op jit(solution)/shard_map/ppermute | solution.py:360
  33.4 0.1 chip.1
  33.5 2.8 %collective-permute-start.8 = (bf16[64,576]{1,0:T(8,128)(2,1)S(1)}, bf16[64,576]{1,0:T(8,128)(2,1)S(1)}, u32[]{:S(2)}, u32[]{:S(2)}) collective-permute-start(bf16[64,576]{1,0:T(8,128)(2,1)S(1)} %get-tuple-element.51), channel_id=1, source_target_pairs={{0,128},{32,160},{64,192},{96,224},{128,0},{160,32},{192,64},{224,... | collective-permute-start | bytes 221192 | tf_op jit(solution)/shard_map/ppermute | solution.py:365
  36.3 0.9 %collective-permute-start.7 = (bf16[128,576]{1,0:T(8,128)(2,1)S(1)}, bf16[128,576]{1,0:T(8,128)(2,1)S(1)}, u32[]{:S(2)}, u32[]{:S(2)}) collective-permute-start(bf16[128,576]{1,0:T(8,128)(2,1)S(1)} %get-tuple-element.47.chip_ref), channel_id=1, source_target_pairs={{0,64},{32,224},{64,0},{96,160},{128,192},{160,96},{192,128},{224,... | collective-permute-start | bytes 442376 | tf_op jit(solution)/shard_map/ppermute | solution.py:365
  37.2 2.8 %dquery.1 = bf16[16,576,128]{2,1,0:T(8,128)(2,1)} custom-call(bf16[512,2048]{1,0:T(8,128)(2,1)S(1)} %get-tuple-element.48.dscore_ref, bf16[128,576]{1,0:T(8,128)(2,1)S(1)} %get-tuple-element.28.keys_ref, bf16[192,576]{1,0:T(8,128)(2,1)S(1)} %pad_maximum_fusion.mine_ref, bf16[192,576]{1,0:T(8,128)(2,1)S(1)} %collective-permute-done.2.other_ref, ...), custom_call_target="tpu_custom_call" | custom-call | flops 1610612736 | bytes 4718592 | tf_op jit(solution)/shard_map/dquery/pallas_call | solution.py:461
  40.0 1.7 %collective-permute-done.7.near_ref = bf16[128,576]{1,0:T(8,128)(2,1)S(1)} collective-permute-done((bf16[128,576]{1,0:T(8,128)(2,1)S(1)}, bf16[128,576]{1,0:T(8,128)(2,1)S(1)}, u32[]{:S(2)}, u32[]{:S(2)}) %collective-permute-start.7) | collective-permute-done | bytes 147488 | tf_op jit(solution)/shard_map/ppermute | solution.py:365
  41.7 0.0 collective-permute-done.8.far_ref
  41.7 0.7 %collective-permute-start.9 = (bf16[192,576]{1,0:T(8,128)(2,1)S(1)}, bf16[192,576]{1,0:T(8,128)(2,1)S(1)}, u32[]{:S(2)}, u32[]{:S(2)}) collective-permute-start(bf16[192,576]{1,0:T(8,128)(2,1)S(1)} %pad_maximum_fusion.1), channel_id=1, source_target_pairs={{0,32},{32,0},{64,96},{96,64},{128,160},{160,128},{192,224},{224,1... | collective-permute-start | bytes 663560 | tf_op jit(solution)/shard_map/ppermute | solution.py:360
  42.4 1.1 %collective-permute-done.9.rest_ref = bf16[192,576]{1,0:T(8,128)(2,1)S(1)} collective-permute-done((bf16[192,576]{1,0:T(8,128)(2,1)S(1)}, bf16[192,576]{1,0:T(8,128)(2,1)S(1)}, u32[]{:S(2)}, u32[]{:S(2)}) %collective-permute-start.9) | collective-permute-done | bytes 221216 | tf_op jit(solution)/shard_map/ppermute | solution.py:360
  43.5 0.9 %finish.1 = bf16[576,128]{1,0:T(8,128)(2,1)} custom-call(bf16[128,576]{1,0:T(8,128)(2,1)S(1)} %get-tuple-element.47.chip_ref, bf16[128,576]{1,0:T(8,128)(2,1)S(1)} %collective-permute-done.7.near_ref, bf16[64,576]{1,0:T(8,128)(2,1)S(1)} %collective-permute-done.8.far_ref, bf16[192,576]{1,0:T(8,128)(2,1)S(1)} %collective-permute-done.9.rest_ref, ...), custom_call_target="tpu_custom_call" | custom-call | tf_op jit(solution)/shard_map/finish/pallas_call | solution.py:474
  (6 shorter events, 0.1 us)
Async XLA Ops:
  2.5 14.6 %collective-permute-start = (bf16[128,576]{1,0:T(8,128)(2,1)S(1)}, bf16[128,576]{1,0:T(8,128)(2,1)S(1)}, u32[]{:S(2)}, u32[]{:S(2)}) collective-permute-start(bf16[128,576]{1,0:T(8,128)(2,1)S(1)} %get-tuple-element.28.keys_ref), channel_id=1, source_target_pairs={{0,2},{1,3},{2,4},{3,5},{4,6},{5,7},{6,8},{7,9},{8,10},{9,11},{10,... | collective-permute-start | bytes 442376 | tf_op jit(solution)/shard_map/ppermute | solution.py:353
  6.1 11.0 %collective-permute-start.1 = (bf16[64,576]{1,0:T(8,128)(2,1)S(1)}, bf16[64,576]{1,0:T(8,128)(2,1)S(1)}, u32[]{:S(2)}, u32[]{:S(2)}) collective-permute-start(bf16[64,576]{1,0:T(8,128)(2,1)S(1)} %get-tuple-element.29), channel_id=1, source_target_pairs={{0,1},{1,2},{2,3},{3,4},{4,5},{5,6},{6,7},{7,8},{8,9},{9,10},{10,1... | collective-permute-start | bytes 221192 | tf_op jit(solution)/shard_map/ppermute | solution.py:353
  17.1 2.5 %collective-permute-start.2 = (bf16[192,576]{1,0:T(8,128)(2,1)S(1)}, bf16[192,576]{1,0:T(8,128)(2,1)S(1)}, u32[]{:S(2)}, u32[]{:S(2)}) collective-permute-start(bf16[192,576]{1,0:T(8,128)(2,1)S(1)} %pad_maximum_fusion.mine_ref), channel_id=1, source_target_pairs={{0,32},{32,0},{64,96},{96,64},{128,160},{160,128},{192,224},{224,1... | collective-permute-start | bytes 663560 | tf_op jit(solution)/shard_map/ppermute | solution.py:360
  20.1 1.6 %collective-permute-start.3 = (bf16[192,576]{1,0:T(8,128)(2,1)S(1)}, bf16[192,576]{1,0:T(8,128)(2,1)S(1)}, u32[]{:S(2)}, u32[]{:S(2)}) collective-permute-start(bf16[192,576]{1,0:T(8,128)(2,1)S(1)} %get-tuple-element.45), channel_id=1, source_target_pairs={{0,32},{32,0},{64,96},{96,64},{128,160},{160,128},{192,224},{224,1... | collective-permute-start | bytes 663560 | tf_op jit(solution)/shard_map/ppermute | solution.py:360
  21.8 9.7 %collective-permute-start.4 = (bf16[128,576]{1,0:T(8,128)(2,1)S(1)}, bf16[128,576]{1,0:T(8,128)(2,1)S(1)}, u32[]{:S(2)}, u32[]{:S(2)}) collective-permute-start(bf16[128,576]{1,0:T(8,128)(2,1)S(1)} %slice.8), channel_id=1, source_target_pairs={{0,30},{1,31},{2,0},{3,1},{4,2},{5,3},{6,4},{7,5},{8,6},{9,7},{10,... | collective-permute-start | bytes 442376 | tf_op jit(solution)/shard_map/ppermute | solution.py:353
  26.1 5.4 %collective-permute-start.5 = (bf16[64,576]{1,0:T(8,128)(2,1)S(1)}, bf16[64,576]{1,0:T(8,128)(2,1)S(1)}, u32[]{:S(2)}, u32[]{:S(2)}) collective-permute-start(bf16[64,576]{1,0:T(8,128)(2,1)S(1)} %slice.9), channel_id=1, source_target_pairs={{0,31},{1,0},{2,1},{3,2},{4,3},{5,4},{6,5},{7,6},{8,7},{9,8},{10,9... | collective-permute-start | bytes 221192 | tf_op jit(solution)/shard_map/ppermute | solution.py:353
  31.6 1.9 %collective-permute-start.6 = (bf16[128,576]{1,0:T(8,128)(2,1)S(1)}, bf16[128,576]{1,0:T(8,128)(2,1)S(1)}, u32[]{:S(2)}, u32[]{:S(2)}) collective-permute-start(bf16[128,576]{1,0:T(8,128)(2,1)S(1)} %device.1.device_ref), channel_id=1, source_target_pairs={{0,32},{32,0},{64,96},{96,64},{128,160},{160,128},{192,224},{224,1... | collective-permute-start | bytes 442376 | tf_op jit(solution)/shard_map/ppermute | solution.py:360
  33.5 8.2 %collective-permute-start.8 = (bf16[64,576]{1,0:T(8,128)(2,1)S(1)}, bf16[64,576]{1,0:T(8,128)(2,1)S(1)}, u32[]{:S(2)}, u32[]{:S(2)}) collective-permute-start(bf16[64,576]{1,0:T(8,128)(2,1)S(1)} %get-tuple-element.51), channel_id=1, source_target_pairs={{0,128},{32,160},{64,192},{96,224},{128,0},{160,32},{192,64},{224,... | collective-permute-start | bytes 221192 | tf_op jit(solution)/shard_map/ppermute | solution.py:365
  36.3 5.4 %collective-permute-start.7 = (bf16[128,576]{1,0:T(8,128)(2,1)S(1)}, bf16[128,576]{1,0:T(8,128)(2,1)S(1)}, u32[]{:S(2)}, u32[]{:S(2)}) collective-permute-start(bf16[128,576]{1,0:T(8,128)(2,1)S(1)} %get-tuple-element.47.chip_ref), channel_id=1, source_target_pairs={{0,64},{32,224},{64,0},{96,160},{128,192},{160,96},{192,128},{224,... | collective-permute-start | bytes 442376 | tf_op jit(solution)/shard_map/ppermute | solution.py:365
  41.7 1.8 %collective-permute-start.9 = (bf16[192,576]{1,0:T(8,128)(2,1)S(1)}, bf16[192,576]{1,0:T(8,128)(2,1)S(1)}, u32[]{:S(2)}, u32[]{:S(2)}) collective-permute-start(bf16[192,576]{1,0:T(8,128)(2,1)S(1)} %pad_maximum_fusion.1), channel_id=1, source_target_pairs={{0,32},{32,0},{64,96},{96,64},{128,160},{160,128},{192,224},{224,1... | collective-permute-start | bytes 663560 | tf_op jit(solution)/shard_map/ppermute | solution.py:360

commit v6 on v5

--- a/solution.py
+++ b/solution.py
@@ -338,7 +338,7 @@
     sum_ref[other_half(), :] += rest_ref[BS:, :].astype(F32)
     sum_ref[...] += near_ref[...].astype(F32) + rest_ref[:BS, :].astype(F32)
     for lo in range(0, LAT, BS):
-        out_ref[lo : lo + BS, :] = sum_ref[:, lo : lo + BS].T.astype(BF)
+        out_ref[lo : lo + BS, :] = sum_ref[:, lo : lo + BS].astype(BF).T
     out_ref[LAT:, :] = turn_back(sum_ref[:, LAT:].T, table_ref[...]).astype(BF)
 
 

time: 44.6 us -> 44.6 us (level)
  no operation moved by 1% of the time
where the time goes in v6:
time: 44.6 us; the launch traced here: 44.4 us
  starting transfers between devices  18.3 us (41%)
  waiting for transfers between devices  14.5 us (33%)
  Pallas kernels  10.8 us (24%)
  between operations  0.71 us (2%)
    ppermute x4, starting transfers between devices, by_core(): return lax.ppermute(block, ('tp', 'cp'), route)  11.2 us
    ppermute x4, waiting for transfers between devices, by_core(): return lax.ppermute(block, ('tp', 'cp'), route)  8.4 us
    ppermute x4, waiting for transfers between devices, other_core(): lax.ppermute(block, 'tp', [(t, t ^ 1) for t in range(lax.axis_size('tp'))])  4.41 us
    ppermute x2, starting transfers between devices, along_x(): return lax.ppermute(block, 'tp', route)  3.69 us
    pallas_call x1, Pallas kernels, on_device(): call(functools.partial(own_kernel, heads), 'own', [outside] * 2 + [whole(...  3.45 us
    ppermute x4, starting transfers between devices, other_core(): lax.ppermute(block, 'tp', [(t, t ^ 1) for t in range(lax.axis_size('tp'))])  3.37 us
    pallas_call x1, Pallas kernels, on_device(): pl.pallas_call(query_kernel, grid=(total // STEP,), in_specs=[whole()] *...  2.84 us
    pallas_call x1, Pallas kernels, on_device(): call(keys_kernel, 'keys', [scalars(), whole(), outside, outside, outside]...  1.84 us
  transfers between devices with their start and end apart: 10, of which 7 were waited for; matrix products, arithmetic and copies ran while one was open for 0% of the time, Pallas kernels for 17%

profile of v6, /device:TPU:1, one launch (start us, length us, event | category | flops | bytes accessed | tf_op | source)
XLA Modules:
  0.0 44.4 jit_solution(4914873518414228011)
XLA Ops:
  0.6 1.8 %keys.1 = (bf16[128,576]{1,0:T(8,128)(2,1)S(1)}, bf16[64,576]{1,0:T(8,128)(2,1)S(1)}, f32[64,128]{1,0:T(8,128)S(1)}, f32[128,128]{1,0:T(8,128)S(1)}, f32[8,256]{1,0:T(8,128)S(1)}, /*index=5*/bf16[512,512]{1,0:T(8,128)(2,1)S(1)}) custom-call(s32[1,3]{1,0:T(1,128)} %anc_ref.1, s32[1,128]{1,0:T(1,128)} %bitcast.13, f32[32,128]{1,0:T(8,128)} %constant.2.clone.freq_hbm, ...), custom_call_target="tpu_custom_call" | custom-call | bytes 4718592 | tf_op jit(solution)/shard_map/keys/pallas_call | solution.py:389
  2.5 3.6 %collective-permute-start = (bf16[128,576]{1,0:T(8,128)(2,1)S(1)}, bf16[128,576]{1,0:T(8,128)(2,1)S(1)}, u32[]{:S(2)}, u32[]{:S(2)}) collective-permute-start(bf16[128,576]{1,0:T(8,128)(2,1)S(1)} %get-tuple-element.28.keys_ref), channel_id=1, source_target_pairs={{0,2},{1,3},{2,4},{3,5},{4,6},{5,7},{6,8},{7,9},{8,10},{9,11},{10,... | collective-permute-start | bytes 442376 | tf_op jit(solution)/shard_map/ppermute | solution.py:353
  6.1 0.1 collective-permute-start.1
  6.2 3.5 %own.1 = (bf16[9216,128]{1,0:T(8,128)(2,1)S(1)}, bf16[2048,512]{1,0:T(8,128)(2,1)S(1)}, f32[128,2048]{1,0:T(8,128)S(1)}, f32[128,2048]{1,0:T(8,128)S(1)}, f32[8,2048]{1,0:T(8,128)S(1)}) custom-call(bf16[9216,128]{1,0:T(8,128)(2,1)} %bitcast.10, bf16[2048,512]{1,0:T(8,128)(2,1)} %bitcast.9, bf16[512,512]{1,0:T(8,128)(2,1)S(1)} %get-tuple-element.30.early_ref, ...), custom_call_target="tpu_custom_call" | custom-call | flops 943718400 | bytes 4718592 | tf_op jit(solution)/shard_map/own/pallas_call | solution.py:400
  9.7 7.4 %collective-permute-done.1 = bf16[64,576]{1,0:T(8,128)(2,1)S(1)} collective-permute-done((bf16[64,576]{1,0:T(8,128)(2,1)S(1)}, bf16[64,576]{1,0:T(8,128)(2,1)S(1)}, u32[]{:S(2)}, u32[]{:S(2)}) %collective-permute-start.1) | collective-permute-done | bytes 73760 | tf_op jit(solution)/shard_map/ppermute | solution.py:353
  17.1 0.0 collective-permute-done
  17.1 1.4 %collective-permute-start.2 = (bf16[192,576]{1,0:T(8,128)(2,1)S(1)}, bf16[192,576]{1,0:T(8,128)(2,1)S(1)}, u32[]{:S(2)}, u32[]{:S(2)}) collective-permute-start(bf16[192,576]{1,0:T(8,128)(2,1)S(1)} %pad_maximum_fusion.mine_ref), channel_id=1, source_target_pairs={{0,32},{32,0},{64,96},{96,64},{128,160},{160,128},{192,224},{224,1... | collective-permute-start | bytes 663560 | tf_op jit(solution)/shard_map/ppermute | solution.py:360
  18.5 1.1 %collective-permute-done.2.other_ref = bf16[192,576]{1,0:T(8,128)(2,1)S(1)} collective-permute-done((bf16[192,576]{1,0:T(8,128)(2,1)S(1)}, bf16[192,576]{1,0:T(8,128)(2,1)S(1)}, u32[]{:S(2)}, u32[]{:S(2)}) %collective-permute-start.2) | collective-permute-done | bytes 221216 | tf_op jit(solution)/shard_map/ppermute | solution.py:360
  19.7 0.4 main.1
  20.1 0.5 %collective-permute-start.3 = (bf16[192,576]{1,0:T(8,128)(2,1)S(1)}, bf16[192,576]{1,0:T(8,128)(2,1)S(1)}, u32[]{:S(2)}, u32[]{:S(2)}) collective-permute-start(bf16[192,576]{1,0:T(8,128)(2,1)S(1)} %get-tuple-element.45), channel_id=1, source_target_pairs={{0,32},{32,0},{64,96},{96,64},{128,160},{160,128},{192,224},{224,1... | collective-permute-start | bytes 663560 | tf_op jit(solution)/shard_map/ppermute | solution.py:360
  20.6 1.1 %collective-permute-done.3 = bf16[192,576]{1,0:T(8,128)(2,1)S(1)} collective-permute-done((bf16[192,576]{1,0:T(8,128)(2,1)S(1)}, bf16[192,576]{1,0:T(8,128)(2,1)S(1)}, u32[]{:S(2)}, u32[]{:S(2)}) %collective-permute-start.3) | collective-permute-done | bytes 221216 | tf_op jit(solution)/shard_map/ppermute | solution.py:360
  21.7 0.1 add_convert_fusion
  21.8 4.3 %collective-permute-start.4 = (bf16[128,576]{1,0:T(8,128)(2,1)S(1)}, bf16[128,576]{1,0:T(8,128)(2,1)S(1)}, u32[]{:S(2)}, u32[]{:S(2)}) collective-permute-start(bf16[128,576]{1,0:T(8,128)(2,1)S(1)} %slice.8), channel_id=1, source_target_pairs={{0,30},{1,31},{2,0},{3,1},{4,2},{5,3},{6,4},{7,5},{8,6},{9,7},{10,... | collective-permute-start | bytes 442376 | tf_op jit(solution)/shard_map/ppermute | solution.py:353
  26.1 3.2 %collective-permute-start.5 = (bf16[64,576]{1,0:T(8,128)(2,1)S(1)}, bf16[64,576]{1,0:T(8,128)(2,1)S(1)}, u32[]{:S(2)}, u32[]{:S(2)}) collective-permute-start(bf16[64,576]{1,0:T(8,128)(2,1)S(1)} %slice.9), channel_id=1, source_target_pairs={{0,31},{1,0},{2,1},{3,2},{4,3},{5,4},{6,5},{7,6},{8,7},{9,8},{10,9... | collective-permute-start | bytes 221192 | tf_op jit(solution)/shard_map/ppermute | solution.py:353
  29.3 1.2 %gown.1.gown_ref = f32[128,576]{1,0:T(8,128)S(1)} custom-call(bf16[512,2048]{1,0:T(8,128)(2,1)S(1)} %get-tuple-element.43.weight_ref, bf16[512,2048]{1,0:T(8,128)(2,1)S(1)} %get-tuple-element.48.dscore_ref, bf16[9216,128]{1,0:T(8,128)(2,1)S(1)} %get-tuple-element.34.query_ref, bf16[2048,512]{1,0:T(8,128)(2,1)S(1)} %get-tuple-element.35.sorted_ref), custom_call_target="tpu_custom_call" | custom-call | flops 671088640 | bytes 4718592 | tf_op jit(solution)/shard_map/gown/pallas_call | solution.py:441
  30.5 1.0 %collective-permute-done.5.half_ref = bf16[64,576]{1,0:T(8,128)(2,1)S(1)} collective-permute-done((bf16[64,576]{1,0:T(8,128)(2,1)S(1)}, bf16[64,576]{1,0:T(8,128)(2,1)S(1)}, u32[]{:S(2)}, u32[]{:S(2)}) %collective-permute-start.5) | collective-permute-done | bytes 73760 | tf_op jit(solution)/shard_map/ppermute | solution.py:353
  31.5 0.0 collective-permute-done.4.back_ref
  31.5 0.1 device.1.device_ref
  31.6 0.8 %collective-permute-start.6 = (bf16[128,576]{1,0:T(8,128)(2,1)S(1)}, bf16[128,576]{1,0:T(8,128)(2,1)S(1)}, u32[]{:S(2)}, u32[]{:S(2)}) collective-permute-start(bf16[128,576]{1,0:T(8,128)(2,1)S(1)} %device.1.device_ref), channel_id=1, source_target_pairs={{0,32},{32,0},{64,96},{96,64},{128,160},{160,128},{192,224},{224,1... | collective-permute-start | bytes 442376 | tf_op jit(solution)/shard_map/ppermute | solution.py:360
  32.4 1.0 %collective-permute-done.6.other_ref = bf16[128,576]{1,0:T(8,128)(2,1)S(1)} collective-permute-done((bf16[128,576]{1,0:T(8,128)(2,1)S(1)}, bf16[128,576]{1,0:T(8,128)(2,1)S(1)}, u32[]{:S(2)}, u32[]{:S(2)}) %collective-permute-start.6) | collective-permute-done | bytes 147488 | tf_op jit(solution)/shard_map/ppermute | solution.py:360
  33.4 0.1 chip.1
  33.5 2.8 %collective-permute-start.8 = (bf16[64,576]{1,0:T(8,128)(2,1)S(1)}, bf16[64,576]{1,0:T(8,128)(2,1)S(1)}, u32[]{:S(2)}, u32[]{:S(2)}) collective-permute-start(bf16[64,576]{1,0:T(8,128)(2,1)S(1)} %get-tuple-element.51), channel_id=1, source_target_pairs={{0,128},{32,160},{64,192},{96,224},{128,0},{160,32},{192,64},{224,... | collective-permute-start | bytes 221192 | tf_op jit(solution)/shard_map/ppermute | solution.py:365
  36.3 0.9 %collective-permute-start.7 = (bf16[128,576]{1,0:T(8,128)(2,1)S(1)}, bf16[128,576]{1,0:T(8,128)(2,1)S(1)}, u32[]{:S(2)}, u32[]{:S(2)}) collective-permute-start(bf16[128,576]{1,0:T(8,128)(2,1)S(1)} %get-tuple-element.47.chip_ref), channel_id=1, source_target_pairs={{0,64},{32,224},{64,0},{96,160},{128,192},{160,96},{192,128},{224,... | collective-permute-start | bytes 442376 | tf_op jit(solution)/shard_map/ppermute | solution.py:365
  37.2 2.8 %dquery.1 = bf16[16,576,128]{2,1,0:T(8,128)(2,1)} custom-call(bf16[512,2048]{1,0:T(8,128)(2,1)S(1)} %get-tuple-element.48.dscore_ref, bf16[128,576]{1,0:T(8,128)(2,1)S(1)} %get-tuple-element.28.keys_ref, bf16[192,576]{1,0:T(8,128)(2,1)S(1)} %pad_maximum_fusion.mine_ref, bf16[192,576]{1,0:T(8,128)(2,1)S(1)} %collective-permute-done.2.other_ref, ...), custom_call_target="tpu_custom_call" | custom-call | flops 1610612736 | bytes 4718592 | tf_op jit(solution)/shard_map/dquery/pallas_call | solution.py:461
  40.0 1.7 %collective-permute-done.7.near_ref = bf16[128,576]{1,0:T(8,128)(2,1)S(1)} collective-permute-done((bf16[128,576]{1,0:T(8,128)(2,1)S(1)}, bf16[128,576]{1,0:T(8,128)(2,1)S(1)}, u32[]{:S(2)}, u32[]{:S(2)}) %collective-permute-start.7) | collective-permute-done | bytes 147488 | tf_op jit(solution)/shard_map/ppermute | solution.py:365
  41.7 0.0 collective-permute-done.8.far_ref
  41.7 0.7 %collective-permute-start.9 = (bf16[192,576]{1,0:T(8,128)(2,1)S(1)}, bf16[192,576]{1,0:T(8,128)(2,1)S(1)}, u32[]{:S(2)}, u32[]{:S(2)}) collective-permute-start(bf16[192,576]{1,0:T(8,128)(2,1)S(1)} %pad_maximum_fusion.1), channel_id=1, source_target_pairs={{0,32},{32,0},{64,96},{96,64},{128,160},{160,128},{192,224},{224,1... | collective-permute-start | bytes 663560 | tf_op jit(solution)/shard_map/ppermute | solution.py:360
  42.4 1.1 %collective-permute-done.9.rest_ref = bf16[192,576]{1,0:T(8,128)(2,1)S(1)} collective-permute-done((bf16[192,576]{1,0:T(8,128)(2,1)S(1)}, bf16[192,576]{1,0:T(8,128)(2,1)S(1)}, u32[]{:S(2)}, u32[]{:S(2)}) %collective-permute-start.9) | collective-permute-done | bytes 221216 | tf_op jit(solution)/shard_map/ppermute | solution.py:360
  43.5 0.9 %finish.1 = bf16[576,128]{1,0:T(8,128)(2,1)} custom-call(bf16[128,576]{1,0:T(8,128)(2,1)S(1)} %get-tuple-element.47.chip_ref, bf16[128,576]{1,0:T(8,128)(2,1)S(1)} %collective-permute-done.7.near_ref, bf16[64,576]{1,0:T(8,128)(2,1)S(1)} %collective-permute-done.8.far_ref, bf16[192,576]{1,0:T(8,128)(2,1)S(1)} %collective-permute-done.9.rest_ref, ...), custom_call_target="tpu_custom_call" | custom-call | tf_op jit(solution)/shard_map/finish/pallas_call | solution.py:474
  (6 shorter events, 0.1 us)
Async XLA Ops:
  2.5 14.6 %collective-permute-start = (bf16[128,576]{1,0:T(8,128)(2,1)S(1)}, bf16[128,576]{1,0:T(8,128)(2,1)S(1)}, u32[]{:S(2)}, u32[]{:S(2)}) collective-permute-start(bf16[128,576]{1,0:T(8,128)(2,1)S(1)} %get-tuple-element.28.keys_ref), channel_id=1, source_target_pairs={{0,2},{1,3},{2,4},{3,5},{4,6},{5,7},{6,8},{7,9},{8,10},{9,11},{10,... | collective-permute-start | bytes 442376 | tf_op jit(solution)/shard_map/ppermute | solution.py:353
  6.1 11.0 %collective-permute-start.1 = (bf16[64,576]{1,0:T(8,128)(2,1)S(1)}, bf16[64,576]{1,0:T(8,128)(2,1)S(1)}, u32[]{:S(2)}, u32[]{:S(2)}) collective-permute-start(bf16[64,576]{1,0:T(8,128)(2,1)S(1)} %get-tuple-element.29), channel_id=1, source_target_pairs={{0,1},{1,2},{2,3},{3,4},{4,5},{5,6},{6,7},{7,8},{8,9},{9,10},{10,1... | collective-permute-start | bytes 221192 | tf_op jit(solution)/shard_map/ppermute | solution.py:353
  17.1 2.5 %collective-permute-start.2 = (bf16[192,576]{1,0:T(8,128)(2,1)S(1)}, bf16[192,576]{1,0:T(8,128)(2,1)S(1)}, u32[]{:S(2)}, u32[]{:S(2)}) collective-permute-start(bf16[192,576]{1,0:T(8,128)(2,1)S(1)} %pad_maximum_fusion.mine_ref), channel_id=1, source_target_pairs={{0,32},{32,0},{64,96},{96,64},{128,160},{160,128},{192,224},{224,1... | collective-permute-start | bytes 663560 | tf_op jit(solution)/shard_map/ppermute | solution.py:360
  20.1 1.6 %collective-permute-start.3 = (bf16[192,576]{1,0:T(8,128)(2,1)S(1)}, bf16[192,576]{1,0:T(8,128)(2,1)S(1)}, u32[]{:S(2)}, u32[]{:S(2)}) collective-permute-start(bf16[192,576]{1,0:T(8,128)(2,1)S(1)} %get-tuple-element.45), channel_id=1, source_target_pairs={{0,32},{32,0},{64,96},{96,64},{128,160},{160,128},{192,224},{224,1... | collective-permute-start | bytes 663560 | tf_op jit(solution)/shard_map/ppermute | solution.py:360
  21.8 9.7 %collective-permute-start.4 = (bf16[128,576]{1,0:T(8,128)(2,1)S(1)}, bf16[128,576]{1,0:T(8,128)(2,1)S(1)}, u32[]{:S(2)}, u32[]{:S(2)}) collective-permute-start(bf16[128,576]{1,0:T(8,128)(2,1)S(1)} %slice.8), channel_id=1, source_target_pairs={{0,30},{1,31},{2,0},{3,1},{4,2},{5,3},{6,4},{7,5},{8,6},{9,7},{10,... | collective-permute-start | bytes 442376 | tf_op jit(solution)/shard_map/ppermute | solution.py:353
  26.1 5.4 %collective-permute-start.5 = (bf16[64,576]{1,0:T(8,128)(2,1)S(1)}, bf16[64,576]{1,0:T(8,128)(2,1)S(1)}, u32[]{:S(2)}, u32[]{:S(2)}) collective-permute-start(bf16[64,576]{1,0:T(8,128)(2,1)S(1)} %slice.9), channel_id=1, source_target_pairs={{0,31},{1,0},{2,1},{3,2},{4,3},{5,4},{6,5},{7,6},{8,7},{9,8},{10,9... | collective-permute-start | bytes 221192 | tf_op jit(solution)/shard_map/ppermute | solution.py:353
  31.6 1.9 %collective-permute-start.6 = (bf16[128,576]{1,0:T(8,128)(2,1)S(1)}, bf16[128,576]{1,0:T(8,128)(2,1)S(1)}, u32[]{:S(2)}, u32[]{:S(2)}) collective-permute-start(bf16[128,576]{1,0:T(8,128)(2,1)S(1)} %device.1.device_ref), channel_id=1, source_target_pairs={{0,32},{32,0},{64,96},{96,64},{128,160},{160,128},{192,224},{224,1... | collective-permute-start | bytes 442376 | tf_op jit(solution)/shard_map/ppermute | solution.py:360
  33.5 8.2 %collective-permute-start.8 = (bf16[64,576]{1,0:T(8,128)(2,1)S(1)}, bf16[64,576]{1,0:T(8,128)(2,1)S(1)}, u32[]{:S(2)}, u32[]{:S(2)}) collective-permute-start(bf16[64,576]{1,0:T(8,128)(2,1)S(1)} %get-tuple-element.51), channel_id=1, source_target_pairs={{0,128},{32,160},{64,192},{96,224},{128,0},{160,32},{192,64},{224,... | collective-permute-start | bytes 221192 | tf_op jit(solution)/shard_map/ppermute | solution.py:365
  36.3 5.4 %collective-permute-start.7 = (bf16[128,576]{1,0:T(8,128)(2,1)S(1)}, bf16[128,576]{1,0:T(8,128)(2,1)S(1)}, u32[]{:S(2)}, u32[]{:S(2)}) collective-permute-start(bf16[128,576]{1,0:T(8,128)(2,1)S(1)} %get-tuple-element.47.chip_ref), channel_id=1, source_target_pairs={{0,64},{32,224},{64,0},{96,160},{128,192},{160,96},{192,128},{224,... | collective-permute-start | bytes 442376 | tf_op jit(solution)/shard_map/ppermute | solution.py:365
  41.7 1.8 %collective-permute-start.9 = (bf16[192,576]{1,0:T(8,128)(2,1)S(1)}, bf16[192,576]{1,0:T(8,128)(2,1)S(1)}, u32[]{:S(2)}, u32[]{:S(2)}) collective-permute-start(bf16[192,576]{1,0:T(8,128)(2,1)S(1)} %pad_maximum_fusion.1), channel_id=1, source_target_pairs={{0,32},{32,0},{64,96},{96,64},{128,160},{160,128},{192,224},{224,1... | collective-permute-start | bytes 663560 | tf_op jit(solution)/shard_map/ppermute | solution.py:360
